TPU v7x, 128 devices: a whole 4x4x4 slice. The times are simulated.
128 devices in a mesh: cand: 16 (over y, z_hi, core), tp: 8 (over x, z_lo).
Axes of the slice: x: 4, y: 4, z: 4 (z_hi: 2, z_lo: 2; z = z_hi * 2 + z_lo), core: 2. Of those that a mesh axis runs over, the one named last changes fastest.
Arguments:
- tokens: bfloat16 [512, 24, 8192], P('cand', None, 'tp'), may hold values from -6 to 6
- norm_gain: bfloat16 [8192], replicated, may hold values from 0.5 to 1.5
- w_query: bfloat16 [8192, 4096], P(None, 'tp'), may hold values from -0.0625 to 0.0625
- b_query: bfloat16 [4096], P('tp'), may hold values from -5 to 5
- w_key: bfloat16 [8192, 1024], P(None, 'tp'), may hold values from -0.0625 to 0.0625
- b_key: bfloat16 [1024], P('tp'), may hold values from -5 to 5
- w_value: bfloat16 [8192, 1024], P(None, 'tp'), may hold values from -0.0625 to 0.0625
- b_value: bfloat16 [1024], P('tp'), may hold values from -5 to 5
- w_out: bfloat16 [4096, 8192], P('tp'), may hold values from -0.125 to 0.125
- prefix_keys: bfloat16 [32, 1024, 1024], P('cand', None, 'tp'), may hold values from -52 to 52
- prefix_values: bfloat16 [32, 1024, 1024], P('cand', None, 'tp'), may hold values from -6 to 6
- problem_slot: int32 [32], replicated, may hold values from 0 to 31, each once
- cand_problem: int32 [512, 1], P('cand'), may hold values from 0 to 31; in each aligned block of 32 rows (0 to 31, 32 to 63, ...) at most 2 rows name the same one
- step_len: int32 [512], P('cand'), may hold values from 1 to 24, as said below
Outputs:
- layer_out: bfloat16 [512, 24, 8192], P('cand', None, 'tp')
Inputs may be any that keep to these rules, and one draw needn't show every extreme that they name: Problem p's prefix is stored at row problem_slot[p] of prefix_keys and prefix_values; every row belongs to exactly one problem. `cand_problem`: among the 32 candidates of one index of cand at most 2 belong to one problem; every problem has a candidate. `step_len`: step tokens at and after this length are padding; the lengths of the 32 candidates of one index of cand sum to at most 400, and to exactly 400 on the first index.
All inputs are finite; a program needn't handle non-finite values.
Results may differ from a plain program's by a relative error of at most 0.015.
Values may be sent and summed in bfloat16 or wider, within the bound.
No kernel may reach another device: no remote copies, remote signals or barrier semaphores. Data moves between devices by JAX's collectives and lax.ppermute only.
A program may use at most 192 MiB of HBM per device.

v0:
```python
import jax
import jax.numpy as jnp
from jax import lax
from jax.sharding import PartitionSpec as P

HEAD = 128


rope_base = 1000000.0
norm_eps = 1e-06


def rotary(inputs, offset):
    length = inputs.shape[1]
    half_size = inputs.shape[-1] // 2
    frequency = rope_base ** (-(jnp.arange(half_size, dtype=jnp.float32) * 2.0 / inputs.shape[-1]))
    angles = (offset + jnp.arange(length, dtype=jnp.float32))[:, None] * frequency[None, :]
    cosine = jnp.concatenate([jnp.cos(angles), jnp.cos(angles)], -1)[:, None, :]
    sine_table = jnp.concatenate([jnp.sin(angles), jnp.sin(angles)], -1)[:, None, :]
    turned = jnp.concatenate([-inputs[..., half_size:], inputs[..., :half_size]], -1)
    return inputs * cosine + turned * sine_table


def softmax_block(queries, keys_block, values_block, allowed):
    scores = jnp.einsum(
        "btkge,bske->btkgs", queries, keys_block, preferred_element_type=jnp.float32
    ) * queries.shape[-1] ** (-0.5)
    if allowed is not None:
        scores = jnp.where(allowed[:, :, None, None, :], scores, -1e30)
    row_max = jnp.max(scores, -1)
    weights = jnp.exp(scores - row_max[..., None])
    row_sum = jnp.sum(weights, -1)
    numerator = jnp.einsum(
        "btkgs,bske->btkge",
        weights.astype(jnp.bfloat16),
        values_block,
        preferred_element_type=jnp.float32,
    )
    return (numerator, row_max, row_sum)


def on_device(
    tokens,
    norm_gain,
    w_query,
    b_query,
    w_key,
    b_key,
    w_value,
    b_value,
    w_out,
    prefix_keys,
    prefix_values,
    problem_slot,
    cand_problem,
    step_len,
):
    cand_count, step_count = (tokens.shape[0], tokens.shape[1])
    head_size = HEAD
    heads_dev = w_query.shape[1] // head_size
    kv_dev = w_key.shape[1] // head_size
    group_size = heads_dev // kv_dev
    prefix_len = prefix_keys.shape[1]
    whole = lax.all_gather(tokens, "tp", axis=2, tiled=True)
    flat_rows = whole.reshape(cand_count * step_count, whole.shape[2]).astype(jnp.float32)
    normed = (
        flat_rows
        * lax.rsqrt(jnp.mean(flat_rows * flat_rows, axis=-1, keepdims=True) + norm_eps)
        * norm_gain.astype(jnp.float32)
    ).astype(jnp.bfloat16)
    queries = jnp.dot(normed, w_query, preferred_element_type=jnp.float32) + b_query.astype(
        jnp.float32
    )
    new_keys = jnp.dot(normed, w_key, preferred_element_type=jnp.float32) + b_key.astype(
        jnp.float32
    )
    new_values = jnp.dot(normed, w_value, preferred_element_type=jnp.float32) + b_value.astype(
        jnp.float32
    )
    queries = rotary(
        queries.reshape(cand_count, step_count, heads_dev, head_size), prefix_len
    ).astype(jnp.bfloat16)
    queries = queries.reshape(cand_count, step_count, kv_dev, group_size, head_size)
    new_keys = rotary(
        new_keys.reshape(cand_count, step_count, kv_dev, head_size), prefix_len
    ).astype(jnp.bfloat16)
    new_values = new_values.astype(jnp.bfloat16).reshape(cand_count, step_count, kv_dev, head_size)
    step_pos = jnp.arange(step_count)
    own_allowed = (step_pos[None, None, :] <= step_pos[None, :, None]) & (
        step_pos[None, None, :] < step_len[:, None, None]
    )
    own_num, own_max, own_sum = softmax_block(queries, new_keys, new_values, own_allowed)
    problems = cand_problem[:, 0]
    slot_rows = jnp.sum(
        jnp.where(
            problems[:, None] == jnp.arange(problem_slot.shape[0])[None, :],
            problem_slot[None, :],
            0,
        ),
        axis=1,
    )
    all_keys, all_values = (
        lax.all_gather(prefix_keys, "cand", axis=0, tiled=True),
        lax.all_gather(prefix_values, "cand", axis=0, tiled=True),
    )
    chosen_keys = jnp.take(all_keys, slot_rows, axis=0).reshape(
        cand_count, prefix_len, kv_dev, head_size
    )
    chosen_values = jnp.take(all_values, slot_rows, axis=0).reshape(
        cand_count, prefix_len, kv_dev, head_size
    )
    pre_num, pre_max, pre_sum = softmax_block(queries, chosen_keys, chosen_values, None)
    joint_max = jnp.maximum(pre_max, own_max)
    pre_scale = jnp.exp(pre_max - joint_max)
    own_scale = jnp.exp(own_max - joint_max)
    numerator = pre_num * pre_scale[..., None] + own_num * own_scale[..., None]
    denominator = pre_sum * pre_scale + own_sum * own_scale
    attended = (
        (numerator / denominator[..., None])
        .astype(jnp.bfloat16)
        .reshape(cand_count * step_count, heads_dev * head_size)
    )
    live_rows = step_pos[None, :, None] < step_len[:, None, None]
    projection = jnp.dot(attended, w_out, preferred_element_type=jnp.float32)
    summed = lax.psum_scatter(
        projection.astype(jnp.bfloat16), "tp", scatter_dimension=1, tiled=True
    ).astype(jnp.float32)
    summed = summed.reshape(cand_count, step_count, summed.shape[1])
    summed = jnp.where(live_rows, summed, 0.0)
    return (tokens.astype(jnp.float32) + summed).astype(jnp.bfloat16)


def solution(mesh):
    in_specs = (
        P("cand", None, "tp"),
        P(),
        P(None, "tp"),
        P("tp"),
        P(None, "tp"),
        P("tp"),
        P(None, "tp"),
        P("tp"),
        P("tp", None),
        P("cand", None, "tp"),
        P("cand", None, "tp"),
        P(),
        P("cand", None),
        P("cand"),
    )
    out_specs = P("cand", None, "tp")
    return jax.shard_map(
        on_device, mesh=mesh, in_specs=in_specs, out_specs=out_specs, check_vma=False
    )
```

profile of v0, /device:TPU:30, one launch (start us, length us, event | category | flops | bytes accessed | tf_op | source)
XLA Modules:
  0.0 759.1 jit_solution(2657294958280568623)
XLA Ops:
  6.5 0.7 all-gather.6.cloned.1.call-update
  7.3 0.7 all-gather.4.cloned.1.call-update
  8.1 0.7 all-gather.8.cloned.1.call-update
  8.8 0.7 convert_element_type.70
  9.4 0.7 convert_element_type.72
  10.1 0.7 convert_element_type.67
  10.8 0.7 convert_element_type.65
  11.5 0.9 select_reduce_fusion
  12.6 0.7 iota_compare_fusion.1
  13.5 69.2 %all-gather.6.cloned.1.call-done = bf16[32,1024,128]{2,1,0:T(8,128)(2,1)} async-done(((bf16[2,1024,128]{2,1,0:T(8,128)(2,1)}), bf16[32,1024,128]{2,1,0:T(8,128)(2,1)}) %all-gather.6.cloned.1.call-update) | async-done | bytes 8388624 | tf_op jit(solution)/shard_map/all_gather | solution.py:103
  82.7 8.4 %gather_fusion.1 = bf16[32,1024,128]{2,1,0:T(8,128)(2,1)} fusion(bf16[32,1024,128]{2,1,0:T(8,128)(2,1)} %all-gather.6.cloned.1.call-done, s32[1024]{0:T(1024)S(1)} %pad_clamp_fusion), kind=kCustom, calls=%fused_computation.1.clone | custom fusion | bytes 16777344 | tf_op jit(solution)/shard_map/jit(_take)/gather | solution.py:106
  91.1 64.5 %all-gather.4.cloned.1.call-done = bf16[32,1024,128]{2,1,0:T(8,128)(2,1)} async-done(((bf16[2,1024,128]{2,1,0:T(8,128)(2,1)}), bf16[32,1024,128]{2,1,0:T(8,128)(2,1)}) %all-gather.4.cloned.1.call-update) | async-done | bytes 8388624 | tf_op jit(solution)/shard_map/all_gather | solution.py:104
  155.6 8.4 %gather_fusion = bf16[32,1024,128]{2,1,0:T(8,128)(2,1)} fusion(bf16[32,1024,128]{2,1,0:T(8,128)(2,1)} %all-gather.4.cloned.1.call-done, s32[1024]{0:T(1024)S(1)} %pad_clamp_fusion), kind=kCustom, calls=%fused_computation.clone | custom fusion | bytes 16777344 | tf_op jit(solution)/shard_map/jit(_take)/gather | solution.py:109
  164.0 239.9 %all-gather.8.cloned.1.call-done = bf16[32,24,8192]{2,1,0:T(8,128)(2,1)} async-done(((bf16[32,24,1024]{2,1,0:T(8,128)(2,1)}), bf16[32,24,8192]{2,1,0:T(8,128)(2,1)}) %all-gather.8.cloned.1.call-update) | async-done | bytes 12582928 | tf_op jit(solution)/shard_map/all_gather | solution.py:64
  403.9 7.1 multiply_reduce_fusion
  411.1 8.1 %fusion.1 = bf16[768,8192]{1,0:T(8,128)(2,1)S(1)} fusion(f32[8192]{0:T(1024)S(1)} %convert_element_type.65, f32[768]{0:T(1024)S(1)} %rsqrt.12, bf16[32,24,8192]{2,1,0:T(8,128)(2,1)} %all-gather.8.cloned.1.call-done), kind=kLoop, calls=%fused_computation.4 | loop fusion | flops 25165824 | bytes 25201664 | tf_op jit(solution)/shard_map/convert_element_type | solution.py:70
  419.2 4.5 copy-done.3
  423.7 10.0 %convolution_add_fusion = f32[768,512]{1,0:T(8,128)} fusion(bf16[768,8192]{1,0:T(8,128)(2,1)S(1)} %fusion.1, bf16[8192,512]{1,0:T(8,128)(2,1)} %param.18, f32[512]{0:T(512)S(1)} %convert_element_type.67), kind=kOutput, calls=%fused_computation.39 | convolution fusion | flops 6442844160 | bytes 22546432 | tf_op jit(solution)/shard_map/dot_general | solution.py:71
  433.7 2.7 reshape.244
  436.4 6.7 convolution_add_fusion.2
  443.2 0.9 fusion.35
  444.2 0.6 slice_negate_fusion
  444.7 0.5 fusion.22
  445.2 13.2 %bitcast_reduce_fusion = (f32[32,24,4]{1,2,0:T(4,128)S(1)}, f32[32,1024,24,4]{1,2,3,0:T(8,128)}) fusion(bf16[32,24,4,128]{3,1,2,0:T(8,128)(2,1)S(1)} %fusion.22, bf16[32,1024,128]{2,1,0:T(8,128)(2,1)} %gather_fusion.1, pred[32]{0:T(512)(128)(4,1)S(1)} %compare_and_fusion), kind=kOutput, calls=%fused_computation.8 | convolution fusion | flops 815789056 | bytes 21770272 | tf_op jit(solution)/shard_map/btkge,bske->btkgs/dot_general | solution.py:25
  458.5 6.3 fusion.3
  464.8 12.0 %fusion.7 = f32[32,128,24,4]{1,2,3,0:T(8,128)} fusion(bf16[32,1024,128]{2,1,0:T(8,128)(2,1)} %gather_fusion, pred[32]{0:T(512)(128)(4,1)S(1)} %compare_and_fusion, f32[32,1024,24,4]{1,2,3,0:T(8,128)} %get-tuple-element.16, f32[32,24,4]{1,2,0:T(4,128)S(1)} %get-tuple-element.15), kind=kOutput, calls=%fused_computation.14 | convolution fusion | flops 818937856 | bytes 22556704 | tf_op jit(solution)/shard_map/btkgs,bske->btkge/dot_general | solution.py:33
  476.8 8.8 %fusion.29 = bf16[768,128]{1,0:T(8,128)(2,1)S(1)} fusion(bf16[768,8192]{1,0:T(8,128)(2,1)} %copy-done.3, bf16[8192,128]{1,0:T(8,128)(2,1)} %param.22, f32[128]{0:T(128)S(1)} %convert_element_type.72), kind=kOutput, calls=%fused_computation.44 | convolution fusion | flops 1610809344 | bytes 14877184 | tf_op jit(solution)/shard_map/dot_general | solution.py:77
  485.5 1.5 fusion.50
  487.6 1.9 fusion.28
  489.9 9.9 %convolution_convert_fusion = bf16[768,8192]{1,0:T(8,128)(2,1)} fusion(bf16[512,8192]{1,0:T(8,128)(2,1)S(1)} %bitcast.116, bf16[96,8,4,128]{3,2,1,0:T(4,128)(2,1)S(1)} %bitcast.107), kind=kOutput, calls=%fused_computation.6 | convolution fusion | flops 6448742400 | bytes 21757952 | tf_op jit(solution)/shard_map/dot_general | solution.py:124
  499.8 249.3 %reduce-scatter.2.cloned.1.call-done = bf16[768,1024]{1,0:T(8,128)(2,1)} async-done(((bf16[768,8192]{1,0:T(8,128)(2,1)}), bf16[768,1024]{1,0:T(8,128)(2,1)}) %reduce-scatter.2.cloned.1.call-update) | async-done | bytes 1572880 | tf_op jit(solution)/shard_map/reduce_scatter | solution.py:125
  749.0 3.6 fusion.20
  (36 shorter events, 1.6 us)
Async XLA Ops:
  6.5 429.9 %copy-start = (bf16[8192,128]{1,0:T(8,128)(2,1)S(1)}, bf16[8192,128]{1,0:T(8,128)(2,1)}, u32[]{:S(2)}) copy-start(bf16[8192,128]{1,0:T(8,128)(2,1)} %param.20) | copy-start | bytes 6291460
  6.5 76.2 %all-gather.6.cloned.1.call-start = ((), (), s32[]{:S(2)}) async-start(), calls=%async_computation.2 | async-start | bytes 8912896 | tf_op jit(solution)/shard_map/all_gather | solution.py:103
  7.3 148.3 %all-gather.4.cloned.1.call-start = ((), (), s32[]{:S(2)}) async-start(), calls=%async_computation.1 | async-start | bytes 8912896 | tf_op jit(solution)/shard_map/all_gather | solution.py:104
  8.0 395.9 %all-gather.8.cloned.1.call-start = ((), (), s32[]{:S(2)}) async-start(), calls=%async_computation.3 | async-start | bytes 14155776 | tf_op jit(solution)/shard_map/all_gather | solution.py:64
  8.7 740.3 %reduce-scatter.2.cloned.1.call-start = ((), (), s32[]{:S(2)}) async-start(), calls=%async_computation.4 | async-start | bytes 14155776 | tf_op jit(solution)/shard_map/reduce_scatter | solution.py:125
  419.2 4.5 copy-start.3
  436.4 7.6 %copy-start.2 = (f32[32,24,4,128]{3,2,1,0:T(4,128)S(1)}, f32[32,24,4,128]{3,2,1,0:T(4,128)}, u32[]{:S(2)}) copy-start(f32[32,24,4,128]{3,2,1,0:T(4,128)} %reshape.244) | copy-start | bytes 4718596
  476.8 8.8 %copy-start.4 = (f32[32,24,64]{2,1,0:T(8,128)S(1)}, f32[32,24,64]{2,1,0:T(8,128)}, u32[]{:S(2)}) copy-start(f32[32,24,64]{2,1,0:T(8,128)} %get-tuple-element.12) | copy-start | bytes 589828
  476.8 10.8 %copy-start.5 = (f32[32,128,24,4]{1,2,3,0:T(8,128)S(1)}, f32[32,128,24,4]{1,2,3,0:T(8,128)}, u32[]{:S(2)}) copy-start(f32[32,128,24,4]{1,2,3,0:T(8,128)} %fusion.7) | copy-start | bytes 4718596
  485.5 4.3 slice-start
  487.6 2.3 slice-start.1
  499.8 252.9 %copy-start.1 = (bf16[8192,128]{1,0:T(8,128)(2,1)S(1)}, bf16[8192,128]{1,0:T(8,128)(2,1)}, u32[]{:S(2)}) copy-start(bf16[8192,128]{1,0:T(8,128)(2,1)} %param.20) | copy-start | bytes 6291460
Sparse Core Ops, SparseCore 0:
  9.8 72.9 all-gather.5
  85.1 70.4 all-gather.3
  157.3 246.6 all-gather.7
  499.9 249.0 reduce-scatter.1
where the time goes:
time: 761 us; the launch traced here: 759 us
  waiting for transfers between devices  625 us (82%)
  matrix products  64 us (8%)
  other arithmetic  32.2 us (4%)
  local copies, waits for them, and re-layouts  24.6 us (3%)
  between operations  13.3 us (2%)
    reduce_scatter x1, waiting for transfers between devices, on_device(): lax.psum_scatter(projection.astype(jnp.bfloat16), 'tp', scatter_dimension...  249 us
    all_gather x1, waiting for transfers between devices, on_device(): whole = lax.all_gather(tokens, 'tp', axis=2, tiled=True)  240 us
    all_gather x1, waiting for transfers between devices, on_device(): lax.all_gather(prefix_keys, 'cand', axis=0, tiled=True)  69.2 us
    all_gather x1, waiting for transfers between devices, on_device(): lax.all_gather(prefix_values, 'cand', axis=0, tiled=True)  64.5 us
  transfers between devices with their start and end apart: 4, of which 4 were waited for; matrix products, arithmetic and copies ran while one was open for 3% of the time, Pallas kernels for 0%

commit v1 on v0

v1 whole, which is shorter than its diff:
```python
import functools

import jax
import jax.numpy as jnp
from jax import lax
from jax.experimental import pallas as pl
from jax.experimental.pallas import tpu as pltpu
from jax.sharding import PartitionSpec as P

HEAD = 128
LIVE = 400
CHUNKS = ((0, 400),)
PAD = 432
LOCAL = 16

rope_base = 1000000.0
norm_eps = 1e-06
bf16, f32 = jnp.bfloat16, jnp.float32


def along_x(d):
    return [(i, ((i // 2 + d) % 4) * 2 + i % 2) for i in range(8)]


def along_y(d):
    return [(i, ((i // 4 + d) % 4) * 4 + i % 4) for i in range(16)]


ACROSS_Z_LO = [(i, i ^ 1) for i in range(8)]
ACROSS_Z_HI = [(i, i ^ 2) for i in range(16)]
ACROSS_CORE = [(i, i ^ 1) for i in range(16)]


def dot(a, b):
    return jnp.dot(a, b, preferred_element_type=f32)


def gather_prefixes(prefix_keys, prefix_values):
    own = jnp.stack([prefix_keys, prefix_values], axis=1)
    low = lax.ppermute(own, "cand", along_y(1))
    high = lax.ppermute(own, "cand", along_y(-1))
    far0 = lax.ppermute(low[:1], "cand", along_y(1))
    far1 = lax.ppermute(high[1:], "cand", along_y(-1))
    mine = [own, high, far0, far1, low]
    return mine + [lax.ppermute(part, "cand", ACROSS_CORE) for part in mine]


def attention_kernel(bounds, n_rows, n_kv, meta, *refs):
    row_refs, kv_refs = refs[:n_rows], refs[n_rows : n_rows + n_kv]
    out_ref, kv_buf, rows, outs, sems = refs[n_rows + n_kv :]
    step = 24
    group = 4
    copies = []
    place = 0
    for i, ref in enumerate(kv_refs):
        count = ref.shape[0]
        copies.append(pltpu.make_async_copy(ref, kv_buf.at[pl.ds(place, count)], sems.at[i]))
        place += count
    for copy in copies:
        copy.start()
    at = 0
    for ref in row_refs:
        count = ref.shape[0]
        for i in range(group + 2):
            rows[i, at : at + count, :] = ref[:, i * HEAD : (i + 1) * HEAD].astype(f32)
        at += count
    for i in range(group + 2):
        rows[i, at:, :] = jnp.zeros((PAD - at, HEAD), f32)
    outs[...] = jnp.zeros_like(outs)
    for copy in copies:
        copy.wait()
    scale = HEAD ** (-0.5)
    t_at = lax.broadcasted_iota(jnp.int32, (group, step, step), 1).reshape(group * step, step)
    j_at = lax.broadcasted_iota(jnp.int32, (group * step, step), 1)

    def one(c, _):
        where, offset, length = meta[0, c], meta[1, c], meta[2, c]

        @pl.when(where >= 0)
        def _():
            here = pl.ds(offset, step)
            query = jnp.concatenate([rows[h, here, :] for h in range(group)], 0).astype(bf16)
            new_key = rows[group, here, :].astype(bf16)
            new_value = rows[group + 1, here, :].astype(bf16)
            contract = (((1,), (1,)), ((), ()))
            pre = lax.dot_general(query, kv_buf[where, 0], contract, preferred_element_type=f32) * scale
            own = lax.dot_general(query, new_key, contract, preferred_element_type=f32) * scale
            own = jnp.where((j_at <= t_at) & (j_at < length), own, -1e30)
            top = jnp.maximum(jnp.max(pre, -1, keepdims=True), jnp.max(own, -1, keepdims=True))
            pre = jnp.exp(pre - top)
            own = jnp.exp(own - top)
            total = jnp.sum(pre, -1, keepdims=True) + jnp.sum(own, -1, keepdims=True)
            mixed = dot(pre.astype(bf16), kv_buf[where, 1]) + dot(own.astype(bf16), new_value)
            mixed = mixed / total
            for h in range(group):
                outs[h, here, :] = mixed[h * step : (h + 1) * step]

        return 0

    lax.fori_loop(0, meta.shape[1], one, 0)
    first, last = bounds
    for h in range(group):
        out_ref[:, h * HEAD : (h + 1) * HEAD] = outs[h, first:last, :].astype(bf16)


def attention(bounds, meta, row_parts, kv_parts):
    first, last = bounds
    count = meta.shape[1]
    return pl.pallas_call(
        functools.partial(attention_kernel, bounds, len(row_parts), len(kv_parts)),
        out_shape=jax.ShapeDtypeStruct((last - first, 4 * HEAD), bf16),
        in_specs=[pl.BlockSpec(memory_space=pltpu.SMEM)]
        + [pl.BlockSpec(memory_space=pltpu.VMEM)] * len(row_parts)
        + [pl.BlockSpec(memory_space=pl.ANY)] * len(kv_parts),
        out_specs=pl.BlockSpec(memory_space=pltpu.VMEM),
        scratch_shapes=[
            pltpu.VMEM((LOCAL, 2, 1024, HEAD), bf16),
            pltpu.VMEM((6, PAD, HEAD), f32),
            pltpu.VMEM((4, PAD, HEAD), f32),
            pltpu.SemaphoreType.DMA((len(kv_parts),)),
        ],
        compiler_params=pltpu.CompilerParams(vmem_limit_bytes=40 * 2**20),
        cost_estimate=pl.CostEstimate(
            flops=2 * 2 * count * 96 * 1024 * HEAD,
            bytes_accessed=LOCAL * 2 * 1024 * HEAD * 2,
            transcendentals=count * 96 * 1024,
        ),
    )(meta, *row_parts, *kv_parts)


def on_device(
    tokens,
    norm_gain,
    w_query,
    b_query,
    w_key,
    b_key,
    w_value,
    b_value,
    w_out,
    prefix_keys,
    prefix_values,
    problem_slot,
    cand_problem,
    step_len,
):
    cand_count, step, width = tokens.shape
    tp_at, cand_at = lax.axis_index("tp"), lax.axis_index("cand")
    x_at, z_at = tp_at // 2, tp_at % 2
    y_at, half_at, core_at = cand_at // 4, (cand_at // 2) % 2, cand_at % 2

    problems = cand_problem[:, 0]
    slots = jnp.sum(
        jnp.where(
            problems[:, None] == jnp.arange(problem_slot.shape[0])[None, :],
            problem_slot[None, :],
            0,
        ),
        axis=1,
    )
    order = jnp.arange(cand_count)
    offsets = jnp.sum(jnp.where(order[None, :] < order[:, None], step_len[None, :], 0), axis=1)
    table = jnp.stack([slots, offsets, step_len])
    other_table = lax.ppermute(table, "cand", ACROSS_Z_HI)

    def local_place(slot):
        near = ((slot // 8 - y_at) % 4) * 2 + slot % 2 + 8 * (((slot // 2) % 2) ^ core_at)
        return jnp.where((slot // 4) % 2 == half_at, near, -1)

    def meta_of(table, bounds):
        slot, offset, length = table[0], table[1], table[2]
        inside = (offset < bounds[1]) & (offset + length > bounds[0])
        return jnp.stack([jnp.where(inside, local_place(slot), -1), offset, length])

    row_at = jnp.arange(LIVE)
    slot_row = (offsets[:, None] + jnp.arange(step)[None, :]).reshape(-1)
    alive = (jnp.arange(step)[None, :] < step_len[:, None]).reshape(-1)
    slot_row = jnp.where(alive, slot_row, -1)
    pick = (slot_row[None, :] == row_at[:, None]).astype(bf16)
    held = (row_at[:, None] >= offsets[None, :]) & (row_at[:, None] < (offsets + step_len)[None, :])
    position = jnp.sum(jnp.where(held, row_at[:, None] - offsets[None, :], 0), axis=1)
    is_near = jnp.any(held & (local_place(slots) >= 0)[None, :], axis=1)

    frequency = rope_base ** (-(jnp.arange(HEAD // 2, dtype=f32) * 2.0 / HEAD))
    angles = (prefix_keys.shape[1] + position.astype(f32))[:, None] * frequency[None, :]
    cosine = jnp.concatenate([jnp.cos(angles), jnp.cos(angles)], -1)
    sine = jnp.concatenate([-jnp.sin(angles), jnp.sin(angles)], -1)

    weights = jnp.concatenate([w_query, w_key, w_value], axis=1)
    bias = jnp.concatenate([b_query, b_key, b_value]).astype(f32)
    flat = tokens.reshape(cand_count * step, width)
    gain = norm_gain.astype(f32)

    kv_parts = gather_prefixes(prefix_keys, prefix_values)

    def project(bounds):
        first, last = bounds
        block = dot(pick[first:last], flat).astype(bf16)
        cut = width // 2
        across = lax.ppermute(block, "tp", ACROSS_Z_LO)
        blocks = []
        for part, z in ((block, z_at), (across, 1 - z_at)):
            low = lax.ppermute(part, "tp", along_x(1))
            high = lax.ppermute(part, "tp", along_x(-1))
            far0 = lax.ppermute(low[:, :cut], "tp", along_x(1))
            far1 = lax.ppermute(high[:, cut:], "tp", along_x(-1))
            far = ((x_at + 2) % 4) * 2 + z
            blocks += [
                (part, (x_at * 2 + z) * width),
                (low, (((x_at + 3) % 4) * 2 + z) * width),
                (high, (((x_at + 1) % 4) * 2 + z) * width),
                (far0, far * width),
                (far1, far * width + cut),
            ]
        total, squares = 0.0, 0.0
        for part, start in blocks:
            features = part.shape[1]
            wide = part.astype(f32)
            scaled = (wide * lax.dynamic_slice(gain, (start,), (features,))[None, :]).astype(bf16)
            total = total + dot(
                scaled, lax.dynamic_slice(weights, (start, 0), (features, weights.shape[1]))
            )
            squares = squares + jnp.sum(wide * wide, axis=1, keepdims=True)
        mean = squares / (8 * width)
        raw = total * lax.rsqrt(mean + norm_eps) + bias[None, :]
        cos_part, sin_part = cosine[first:last], sine[first:last]
        heads = []
        for h in range(5):
            head = raw[:, h * HEAD : (h + 1) * HEAD]
            heads.append(head * cos_part + jnp.roll(head, HEAD // 2, axis=1) * sin_part)
        heads.append(raw[:, 5 * HEAD :])
        return jnp.concatenate(heads, 1).astype(bf16)

    def scatter(attended):
        cut = width // 2

        def term(d, z):
            start = (((x_at + d) % 4) * 2 + z) * width
            return dot(attended, lax.dynamic_slice(w_out, (0, start), (w_out.shape[0], width)))

        sides = (1 - z_at, z_at)
        far = []
        for z in sides:
            block = term(2, z).astype(bf16)
            far.append(
                (
                    lax.ppermute(block[:, :cut], "tp", along_x(1)),
                    lax.ppermute(block[:, cut:], "tp", along_x(-1)),
                )
            )
        sums = []
        for z, (left, right) in zip(sides, far):
            up, down = term(1, z), term(3, z)
            up = jnp.concatenate([up[:, :cut] + left.astype(f32), up[:, cut:]], 1).astype(bf16)
            down = jnp.concatenate([down[:, :cut], down[:, cut:] + right.astype(f32)], 1).astype(bf16)
            up = lax.ppermute(up, "tp", along_x(1))
            down = lax.ppermute(down, "tp", along_x(-1))
            sums.append(term(0, z) + up.astype(f32) + down.astype(f32))
        return sums[1] + lax.ppermute(sums[0].astype(bf16), "tp", ACROSS_Z_LO).astype(f32)

    mine, theirs, updates = [], [], []
    for bounds in CHUNKS:
        part = project(bounds)
        mine.append(part)
        theirs.append(lax.ppermute(part, "cand", ACROSS_Z_HI))
        near = attention(bounds, meta_of(table, bounds), mine, kv_parts)
        for_other = attention(bounds, meta_of(other_table, bounds), theirs, kv_parts)
        back = lax.ppermute(for_other, "cand", ACROSS_Z_HI)
        attended = jnp.where(is_near[bounds[0] : bounds[1], None], near, back)
        updates.append(scatter(attended))
    update = jnp.concatenate(updates, 0)

    coarse = lax.reduce_precision(update, 8, 7)
    spread = (slot_row[:, None] == row_at[None, :]).astype(bf16)
    placed = dot(spread, coarse.astype(bf16)) + dot(spread, (update - coarse).astype(bf16))
    return (tokens.astype(f32) + placed.reshape(tokens.shape)).astype(bf16)


def solution(mesh):
    in_specs = (
        P("cand", None, "tp"),
        P(),
        P(None, "tp"),
        P("tp"),
        P(None, "tp"),
        P("tp"),
        P(None, "tp"),
        P("tp"),
        P("tp", None),
        P("cand", None, "tp"),
        P("cand", None, "tp"),
        P(),
        P("cand", None),
        P("cand"),
    )
    out_specs = P("cand", None, "tp")
    return jax.shard_map(
        on_device, mesh=mesh, in_specs=in_specs, out_specs=out_specs, check_vma=False
    )
```

time: 761 us -> 210 us (0.28)
  waiting for transfers between devices: 625 us -> 76.2 us
  starting transfers between devices: 0.12 us -> 33.6 us
  matrix products: 64 us -> 30.7 us
  Pallas kernels: 0 us -> 21.7 us
  other arithmetic: 32.2 us -> 16.9 us
  between operations: 13.3 us -> 0.84 us
    all_gather x3 -> x0, waiting for transfers between devices: 374 us -> none  [the longest x1 240 us: on_device(): whole = lax.all_gather(tokens, 'tp', axis=2, tiled=True)]
    reduce_scatter x1 -> x0, waiting for transfers between devices: 249 us -> none  [on_device(): lax.psum_scatter(projection.astype(jnp.bfloat16), 'tp', scatter_dimension...]
    ppermute x0 -> x30, waiting for transfers between devices: none -> 76.2 us  [the longest x2 22.1 us: scatter(): up = lax.ppermute(up, 'tp', along_x(1))]
    ppermute x0 -> x30, starting transfers between devices: none -> 33.6 us  [the longest x2 5.7 us: project(): low = lax.ppermute(part, 'tp', along_x(1))]
    dot_general x8 -> x21, matrix products: 64 us -> 30.7 us  [dot(): return jnp.dot(a, b, preferred_element_type=f32)]
    pallas_call x0 -> x2, Pallas kernels: none -> 21.7 us  [attention(): pl.pallas_call(functools.partial(attention_kernel, bounds, len(row_parts)...]
    gather x2 -> x0, local copies, waits for them, and re-layouts: 16.8 us -> none  [the longest x1 8.4 us: on_device(): jnp.take(all_keys, slot_rows, axis=0)]
    unnamed x16 -> x72, local copies, waits for them, and re-layouts: 4.55 us -> 21.1 us
  transfers between devices with their start and end apart: 4 -> 30, of which waited for: 4 -> 13; matrix products, arithmetic and copies ran while one was open for 3% -> 22% of each run, Pallas kernels for 0% -> 5%
where the time goes in v1:
time: 210 us; the launch traced here: 207 us
  waiting for transfers between devices  76.2 us (36%)
  starting transfers between devices  33.6 us (16%)
  matrix products  30.7 us (15%)
  local copies, waits for them, and re-layouts  26.5 us (13%)
  Pallas kernels  21.7 us (10%)
  other arithmetic  16.9 us (8%)
    dot_general x21, matrix products, dot(): return jnp.dot(a, b, preferred_element_type=f32)  30.7 us
    ppermute x2, waiting for transfers between devices, scatter(): up = lax.ppermute(up, 'tp', along_x(1))  22.1 us
    pallas_call x2, Pallas kernels, attention(): pl.pallas_call(functools.partial(attention_kernel, bounds, len(row_parts)...  21.7 us
    unnamed x72, local copies, waits for them, and re-layouts  21.1 us
    ppermute x2, waiting for transfers between devices, scatter(): lax.ppermute(block[:, :cut], 'tp', along_x(1))  12.2 us
    ppermute x2, waiting for transfers between devices, project(): low = lax.ppermute(part, 'tp', along_x(1))  11.6 us
    ppermute x1, waiting for transfers between devices, on_device(): theirs.append(lax.ppermute(part, 'cand', ACROSS_Z_HI))  11.4 us
    ppermute x2, starting transfers between devices, project(): low = lax.ppermute(part, 'tp', along_x(1))  5.7 us
  transfers between devices with their start and end apart: 30, of which 13 were waited for; matrix products, arithmetic and copies ran while one was open for 22% of the time, Pallas kernels for 5%

profile of v1, /device:TPU:30, one launch (start us, length us, event | category | flops | bytes accessed | tf_op | source)
XLA Modules:
  0.0 206.5 jit_solution(15865013659678469677)
XLA Ops:
  1.6 3.2 %fusion.1 = (f32[400]{0:T(512)S(1)}, bf16[400,1024]{1,0:T(8,128)(2,1)}) fusion(bf16[768,1024]{1,0:T(8,128)(2,1)} %bitcast.22, s32[768]{0:T(1024)S(1)} %select_n.265), kind=kOutput, calls=%fused_computation.17 | convolution fusion | flops 631090816 | bytes 2396736 | tf_op jit(solution)/shard_map/dot_general | solution.py:35
  5.7 2.4 %collective-permute-start = (bf16[400,1024]{1,0:T(8,128)(2,1)}, bf16[400,1024]{1,0:T(8,128)(2,1)}, u32[]{:S(2)}, u32[]{:S(2)}) collective-permute-start(bf16[400,1024]{1,0:T(8,128)(2,1)} %get-tuple-element.41), channel_id=1, source_target_pairs={{0,2},{1,3},{2,4},{3,5},{4,6},{5,7},{6,0},{7,1},{8,10},{9,11},{10,... | collective-permute-start | bytes 2457608 | tf_op jit(solution)/shard_map/ppermute | solution.py:203
  8.1 1.9 collective-permute-start.4
  12.2 7.4 %constant_dynamic-update-slice_fusion.2 = bf16[8192,768]{1,0:T(8,128)(2,1)} fusion(bf16[8192,512]{1,0:T(8,128)(2,1)} %param.16), kind=kLoop, calls=%fused_computation.167 | loop fusion | bytes 16777216
  21.1 3.5 %constant_dynamic-update-slice_fusion.1 = bf16[8192,768]{1,0:T(8,128)(2,1)} fusion(bf16[8192,768]{1,0:T(8,128)(2,1)} %constant_dynamic-update-slice_fusion.2, bf16[8192,128]{1,0:T(8,128)(2,1)} %param.18), kind=kLoop, calls=%fused_computation.166 | loop fusion | bytes 4194304
  27.1 2.6 %fusion.23 = f32[400,768]{1,0:T(8,128)S(1)} fusion(bf16[8192,768]{1,0:T(8,128)(2,1)} %constant_dynamic-update-slice_fusion, s32[]{:T(128)S(6)} %select_n.282, bf16[400,1024]{1,0:T(8,128)(2,1)} %get-tuple-element.41, f32[1024]{0:T(1024)S(1)} %get-tuple-element.27), kind=kOutput, calls=%fused_computation.41 | convolution fusion | flops 630374400 | bytes 3624964 | tf_op jit(solution)/shard_map/dot_general | solution.py:35
  34.7 2.1 %collective-permute-start.3 = (bf16[400,512]{1,0:T(8,128)(2,1)S(1)}, bf16[400,512]{1,0:T(8,128)(2,1)S(1)}, u32[]{:S(2)}, u32[]{:S(2)}) collective-permute-start(bf16[400,512]{1,0:T(8,128)(2,1)S(1)} %slice.170), channel_id=1, source_target_pairs={{0,6},{1,7},{2,0},{3,1},{4,2},{5,3},{6,4},{7,5},{8,14},{9,15},{10,... | collective-permute-start | bytes 1228808 | tf_op jit(solution)/shard_map/ppermute | solution.py:206
  38.1 2.5 %fusion.19 = f32[400,768]{1,0:T(8,128)S(1)} fusion(bf16[8192,768]{1,0:T(8,128)(2,1)} %constant_dynamic-update-slice_fusion, s32[]{:T(128)S(6)} %select_n.286, bf16[400,1024]{1,0:T(8,128)(2,1)} %collective-permute-done.1, f32[1024]{0:T(1024)S(1)} %get-tuple-element.28), kind=kOutput, calls=%fused_computation.37 | convolution fusion | flops 630374400 | bytes 3624964 | tf_op jit(solution)/shard_map/dot_general | solution.py:35
  40.6 1.9 fusion.17
  43.9 3.7 %collective-permute-start.18 = (s32[3,32]{1,0:T(4,128)S(1)}, s32[3,32]{1,0:T(4,128)S(1)}, u32[]{:S(2)}, u32[]{:S(2)}) collective-permute-start(s32[3,32]{1,0:T(4,128)S(1)} %get-tuple-element.38), channel_id=1, source_target_pairs={{0,16},{8,24},{16,0},{24,8},{32,48},{40,56},{48,32},{56,40},{64,80... | collective-permute-start | bytes 1160 | tf_op jit(solution)/shard_map/ppermute | solution.py:164
  47.8 3.3 %collective-permute-start.5 = (bf16[400,1024]{1,0:T(8,128)(2,1)}, bf16[400,1024]{1,0:T(8,128)(2,1)S(1)}, u32[]{:S(2)}, u32[]{:S(2)}) collective-permute-start(bf16[400,1024]{1,0:T(8,128)(2,1)} %collective-permute-done.4), channel_id=1, source_target_pairs={{0,2},{1,3},{2,4},{3,5},{4,6},{5,7},{6,0},{7,1},{8,10},{9,11},{10,... | collective-permute-start | bytes 2457608 | tf_op jit(solution)/shard_map/ppermute | solution.py:203
  54.1 2.0 fusion.56
  56.1 11.6 %collective-permute-done.5 = bf16[400,1024]{1,0:T(8,128)(2,1)S(1)} collective-permute-done((bf16[400,1024]{1,0:T(8,128)(2,1)}, bf16[400,1024]{1,0:T(8,128)(2,1)S(1)}, u32[]{:S(2)}, u32[]{:S(2)}) %collective-permute-start.5) | collective-permute-done | bytes 819232 | tf_op jit(solution)/shard_map/ppermute | solution.py:203
  67.7 3.7 %collective-permute-start.7 = (bf16[400,512]{1,0:T(8,128)(2,1)S(1)}, bf16[400,512]{1,0:T(8,128)(2,1)S(1)}, u32[]{:S(2)}, u32[]{:S(2)}) collective-permute-start(bf16[400,512]{1,0:T(8,128)(2,1)S(1)} %slice.171), channel_id=1, source_target_pairs={{0,2},{1,3},{2,4},{3,5},{4,6},{5,7},{6,0},{7,1},{8,10},{9,11},{10,... | collective-permute-start | bytes 1228808 | tf_op jit(solution)/shard_map/ppermute | solution.py:205
  72.8 5.2 %collective-permute-done.7 = bf16[400,512]{1,0:T(8,128)(2,1)S(1)} collective-permute-done((bf16[400,512]{1,0:T(8,128)(2,1)S(1)}, bf16[400,512]{1,0:T(8,128)(2,1)S(1)}, u32[]{:S(2)}, u32[]{:S(2)}) %collective-permute-start.7) | collective-permute-done | bytes 409632 | tf_op jit(solution)/shard_map/ppermute | solution.py:205
  78.9 2.6 %collective-permute-done.8 = bf16[400,512]{1,0:T(8,128)(2,1)S(1)} collective-permute-done((bf16[400,512]{1,0:T(8,128)(2,1)S(1)}, bf16[400,512]{1,0:T(8,128)(2,1)S(1)}, u32[]{:S(2)}, u32[]{:S(2)}) %collective-permute-start.8) | collective-permute-done | bytes 409632 | tf_op jit(solution)/shard_map/ppermute | solution.py:206
  86.4 3.4 %collective-permute-done.12.refs_4_ = bf16[1,2,1024,128]{3,2,1,0:T(8,128)(2,1)S(1)} collective-permute-done((bf16[1,2,1024,128]{3,2,1,0:T(8,128)(2,1)S(1)}, bf16[1,2,1024,128]{3,2,1,0:T(8,128)(2,1)S(1)}, u32[]{:S(2)}, u32[]{:S(2)}) %collective-permute-start.12) | collective-permute-done | bytes 524320 | tf_op jit(solution)/shard_map/ppermute | solution.py:43
  91.8 11.4 %collective-permute-done.19.refs_0_ = bf16[400,768]{1,0:T(8,128)(2,1)S(1)} collective-permute-done((bf16[400,768]{1,0:T(8,128)(2,1)S(1)}, bf16[400,768]{1,0:T(8,128)(2,1)S(1)}, u32[]{:S(2)}, u32[]{:S(2)}) %collective-permute-start.19) | collective-permute-done | bytes 614432 | tf_op jit(solution)/shard_map/ppermute | solution.py:265
  103.1 10.9 %shard_map.137 = bf16[400,512]{1,0:T(8,128)(2,1)S(1)} custom-call(s32[3,32]{1,0:T(4,128)S(1)} %pad_add_fusion.4.meta, bf16[400,768]{1,0:T(8,128)(2,1)S(1)} %collective-permute-done.19.refs_0_, bf16[2,2,1024,128]{3,2,1,0:T(8,128)(2,1)S(1)} %pad_maximum_fusion.refs_1_, bf16[2,2,1024,128]{3,2,1,0:T(8,128)(2,1)S(1)} %collective-permute-done.9.refs_2_, ...), custom_call_target="tpu_custom_call" | custom-call | flops 1610612736 | bytes 8388608 | tf_op jit(solution)/shard_map/pallas_call | solution.py:109
  124.6 10.9 %shard_map.136 = bf16[400,512]{1,0:T(8,128)(2,1)S(1)} custom-call(s32[3,32]{1,0:T(4,128)S(1)} %copy-done.16, bf16[400,768]{1,0:T(8,128)(2,1)S(1)} %copy-done.15, bf16[2,2,1024,128]{3,2,1,0:T(8,128)(2,1)S(1)} %pad_maximum_fusion.refs_1_, bf16[2,2,1024,128]{3,2,1,0:T(8,128)(2,1)S(1)} %collective-permute-done.9.refs_2_, ...), custom_call_target="tpu_custom_call" | custom-call | flops 1610612736 | bytes 8388608 | tf_op jit(solution)/shard_map/pallas_call | solution.py:109
  136.8 1.9 fusion.68
  144.8 2.5 %collective-permute-start.21 = (bf16[400,512]{1,0:T(8,128)(2,1)S(1)}, bf16[400,512]{1,0:T(8,128)(2,1)S(1)}, u32[]{:S(2)}, u32[]{:S(2)}) collective-permute-start(bf16[400,512]{1,0:T(8,128)(2,1)S(1)} %get-tuple-element.21), channel_id=1, source_target_pairs={{0,2},{1,3},{2,4},{3,5},{4,6},{5,7},{6,0},{7,1},{8,10},{9,11},{10,... | collective-permute-start | bytes 1228808 | tf_op jit(solution)/shard_map/ppermute | solution.py:247
  147.3 7.1 %collective-permute-done.25 = bf16[400,512]{1,0:T(8,128)(2,1)S(1)} collective-permute-done((bf16[400,512]{1,0:T(8,128)(2,1)S(1)}, bf16[400,512]{1,0:T(8,128)(2,1)S(1)}, u32[]{:S(2)}, u32[]{:S(2)}) %collective-permute-start.25) | collective-permute-done | bytes 409632 | tf_op jit(solution)/shard_map/ppermute | solution.py:247
  154.7 2.5 %collective-permute-start.26 = (bf16[400,1024]{1,0:T(8,128)(2,1)S(1)}, bf16[400,1024]{1,0:T(8,128)(2,1)S(1)}, u32[]{:S(2)}, u32[]{:S(2)}) collective-permute-start(bf16[400,1024]{1,0:T(8,128)(2,1)S(1)} %pad_maximum_fusion.3), channel_id=1, source_target_pairs={{0,2},{1,3},{2,4},{3,5},{4,6},{5,7},{6,0},{7,1},{8,10},{9,11},{10,... | collective-permute-start | bytes 2457608 | tf_op jit(solution)/shard_map/ppermute | solution.py:256
  158.2 5.0 %collective-permute-done.21 = bf16[400,512]{1,0:T(8,128)(2,1)S(1)} collective-permute-done((bf16[400,512]{1,0:T(8,128)(2,1)S(1)}, bf16[400,512]{1,0:T(8,128)(2,1)S(1)}, u32[]{:S(2)}, u32[]{:S(2)}) %collective-permute-start.21) | collective-permute-done | bytes 409632 | tf_op jit(solution)/shard_map/ppermute | solution.py:247
  164.4 2.4 %collective-permute-start.22 = (bf16[400,1024]{1,0:T(8,128)(2,1)}, bf16[400,1024]{1,0:T(8,128)(2,1)}, u32[]{:S(2)}, u32[]{:S(2)}) collective-permute-start(bf16[400,1024]{1,0:T(8,128)(2,1)} %pad_maximum_fusion.1), channel_id=1, source_target_pairs={{0,2},{1,3},{2,4},{3,5},{4,6},{5,7},{6,0},{7,1},{8,10},{9,11},{10,... | collective-permute-start | bytes 2457608 | tf_op jit(solution)/shard_map/ppermute | solution.py:256
  168.0 12.9 %collective-permute-done.26 = bf16[400,1024]{1,0:T(8,128)(2,1)S(1)} collective-permute-done((bf16[400,1024]{1,0:T(8,128)(2,1)S(1)}, bf16[400,1024]{1,0:T(8,128)(2,1)S(1)}, u32[]{:S(2)}, u32[]{:S(2)}) %collective-permute-start.26) | collective-permute-done | bytes 819232 | tf_op jit(solution)/shard_map/ppermute | solution.py:256
  180.8 2.4 %collective-permute-done.28 = bf16[400,1024]{1,0:T(8,128)(2,1)S(1)} collective-permute-done((bf16[400,1024]{1,0:T(8,128)(2,1)S(1)}, bf16[400,1024]{1,0:T(8,128)(2,1)S(1)}, u32[]{:S(2)}, u32[]{:S(2)}) %collective-permute-start.28) | collective-permute-done | bytes 819232 | tf_op jit(solution)/shard_map/ppermute | solution.py:257
  186.6 9.2 %collective-permute-done.22 = bf16[400,1024]{1,0:T(8,128)(2,1)} collective-permute-done((bf16[400,1024]{1,0:T(8,128)(2,1)}, bf16[400,1024]{1,0:T(8,128)(2,1)}, u32[]{:S(2)}, u32[]{:S(2)}) %collective-permute-start.22) | collective-permute-done | bytes 819232 | tf_op jit(solution)/shard_map/ppermute | solution.py:256
  195.8 2.0 collective-permute-done.24
  199.4 2.6 %fusion.25 = f32[768,1024]{1,0:T(8,128)S(1)} fusion(s32[768]{0:T(1024)S(1)} %copy-done.24, bf16[400,1024]{1,0:T(8,128)(2,1)} %collective-permute-done.29, bf16[400,1024]{1,0:T(8,128)(2,1)S(1)} %collective-permute-done.24, f32[400,1024]{1,0:T(8,128)S(1)} %fusion.70, bf16[400,1024]{1,0:T(8,128)(2,1)} %collective-permute-done.22), kind=kOutput, calls=%fused_computation.44 | convolution fusion | flops 633139200 | bytes 7244800 | tf_op jit(solution)/shard_map/dot_general | solution.py:35
  202.0 2.7 %convolution_add_fusion = f32[768,1024]{1,0:T(8,128)S(1)} fusion(f32[768,1024]{1,0:T(8,128)S(1)} %fusion.25, s32[768]{0:T(1024)S(1)} %copy-done.24, bf16[400,1024]{1,0:T(8,128)(2,1)} %collective-permute-done.29, bf16[400,1024]{1,0:T(8,128)(2,1)S(1)} %collective-permute-done.24, f32[400,1024]{1,0:T(8,128)S(1)} %fusion.70, ...), kind=kOutput, calls=%fused_computation.15 | convolution fusion | flops 633516032 | bytes 10390528 | tf_op jit(solution)/shard_map/dot_general | solution.py:35
  (183 shorter events, 56.6 us)
Async XLA Ops:
  0.8 29.0 %copy-start.25 = (s32[32]{0:T(128)}, s32[32]{0:T(128)S(1)}, u32[]{:S(2)}) copy-start(s32[32]{0:T(128)S(1)} %select_reduce_fusion.2) | copy-start | bytes 388
  4.8 27.3 %collective-permute-start.1 = (bf16[400,1024]{1,0:T(8,128)(2,1)}, bf16[400,1024]{1,0:T(8,128)(2,1)}, u32[]{:S(2)}, u32[]{:S(2)}) collective-permute-start(bf16[400,1024]{1,0:T(8,128)(2,1)} %get-tuple-element.41), channel_id=1, source_target_pairs={{0,6},{1,7},{2,0},{3,1},{4,2},{5,3},{6,4},{7,5},{8,14},{9,15},{10,... | collective-permute-start | bytes 2457608 | tf_op jit(solution)/shard_map/ppermute | solution.py:204
  5.7 24.7 %collective-permute-start = (bf16[400,1024]{1,0:T(8,128)(2,1)}, bf16[400,1024]{1,0:T(8,128)(2,1)}, u32[]{:S(2)}, u32[]{:S(2)}) collective-permute-start(bf16[400,1024]{1,0:T(8,128)(2,1)} %get-tuple-element.41), channel_id=1, source_target_pairs={{0,2},{1,3},{2,4},{3,5},{4,6},{5,7},{6,0},{7,1},{8,10},{9,11},{10,... | collective-permute-start | bytes 2457608 | tf_op jit(solution)/shard_map/ppermute | solution.py:203
  8.1 26.6 %collective-permute-start.4 = (bf16[400,1024]{1,0:T(8,128)(2,1)}, bf16[400,1024]{1,0:T(8,128)(2,1)}, u32[]{:S(2)}, u32[]{:S(2)}) collective-permute-start(bf16[400,1024]{1,0:T(8,128)(2,1)} %get-tuple-element.41), channel_id=1, source_target_pairs={{0,1},{1,0},{2,3},{3,2},{4,5},{5,4},{6,7},{7,6},{8,9},{9,8},{10,11... | collective-permute-start | bytes 2457608 | tf_op jit(solution)/shard_map/ppermute | solution.py:200
  10.1 33.9 %collective-permute-start.10 = (bf16[2,2,1024,128]{3,2,1,0:T(8,128)(2,1)S(1)}, bf16[2,2,1024,128]{3,2,1,0:T(8,128)(2,1)S(1)}, u32[]{:S(2)}, u32[]{:S(2)}) collective-permute-start(bf16[2,2,1024,128]{3,2,1,0:T(8,128)(2,1)S(1)} %pad_maximum_fusion.refs_1_), channel_id=1, source_target_pairs={{0,32},{8,40},{16,48},{24,56},{32,64},{40,72},{48,80},{56,88},{64,... | collective-permute-start | bytes 3145736 | tf_op jit(solution)/shard_map/ppermute | solution.py:40
  10.4 37.3 %collective-permute-start.9 = (bf16[2,2,1024,128]{3,2,1,0:T(8,128)(2,1)S(1)}, bf16[2,2,1024,128]{3,2,1,0:T(8,128)(2,1)S(1)}, u32[]{:S(2)}, u32[]{:S(2)}) collective-permute-start(bf16[2,2,1024,128]{3,2,1,0:T(8,128)(2,1)S(1)} %pad_maximum_fusion.refs_1_), channel_id=1, source_target_pairs={{0,96},{8,104},{16,112},{24,120},{32,0},{40,8},{48,16},{56,24},{64... | collective-permute-start | bytes 3145736 | tf_op jit(solution)/shard_map/ppermute | solution.py:41
  30.4 55.4 %collective-permute-start.13 = (bf16[2,2,1024,128]{3,2,1,0:T(8,128)(2,1)S(1)}, bf16[2,2,1024,128]{3,2,1,0:T(8,128)(2,1)S(1)}, u32[]{:S(2)}, u32[]{:S(2)}) collective-permute-start(bf16[2,2,1024,128]{3,2,1,0:T(8,128)(2,1)S(1)} %pad_maximum_fusion.refs_1_), channel_id=1, source_target_pairs={{0,8},{8,0},{16,24},{24,16},{32,40},{40,32},{48,56},{56,48},{64,72... | collective-permute-start | bytes 3145736 | tf_op jit(solution)/shard_map/ppermute | solution.py:45
  32.2 15.6 %collective-permute-start.2 = (bf16[400,512]{1,0:T(8,128)(2,1)S(1)}, bf16[400,512]{1,0:T(8,128)(2,1)S(1)}, u32[]{:S(2)}, u32[]{:S(2)}) collective-permute-start(bf16[400,512]{1,0:T(8,128)(2,1)S(1)} %slice.169), channel_id=1, source_target_pairs={{0,2},{1,3},{2,4},{3,5},{4,6},{5,7},{6,0},{7,1},{8,10},{9,11},{10,... | collective-permute-start | bytes 1228808 | tf_op jit(solution)/shard_map/ppermute | solution.py:205
  34.7 17.1 %collective-permute-start.3 = (bf16[400,512]{1,0:T(8,128)(2,1)S(1)}, bf16[400,512]{1,0:T(8,128)(2,1)S(1)}, u32[]{:S(2)}, u32[]{:S(2)}) collective-permute-start(bf16[400,512]{1,0:T(8,128)(2,1)S(1)} %slice.170), channel_id=1, source_target_pairs={{0,6},{1,7},{2,0},{3,1},{4,2},{5,3},{6,4},{7,5},{8,14},{9,15},{10,... | collective-permute-start | bytes 1228808 | tf_op jit(solution)/shard_map/ppermute | solution.py:206
  43.9 40.9 %collective-permute-start.18 = (s32[3,32]{1,0:T(4,128)S(1)}, s32[3,32]{1,0:T(4,128)S(1)}, u32[]{:S(2)}, u32[]{:S(2)}) collective-permute-start(s32[3,32]{1,0:T(4,128)S(1)} %get-tuple-element.38), channel_id=1, source_target_pairs={{0,16},{8,24},{16,0},{24,8},{32,48},{40,56},{48,32},{56,40},{64,80... | collective-permute-start | bytes 1160 | tf_op jit(solution)/shard_map/ppermute | solution.py:164
  47.7 23.7 %collective-permute-start.6 = (bf16[400,1024]{1,0:T(8,128)(2,1)}, bf16[400,1024]{1,0:T(8,128)(2,1)S(1)}, u32[]{:S(2)}, u32[]{:S(2)}) collective-permute-start(bf16[400,1024]{1,0:T(8,128)(2,1)} %collective-permute-done.4), channel_id=1, source_target_pairs={{0,6},{1,7},{2,0},{3,1},{4,2},{5,3},{6,4},{7,5},{8,14},{9,15},{10,... | collective-permute-start | bytes 2457608 | tf_op jit(solution)/shard_map/ppermute | solution.py:204
  47.8 19.9 %collective-permute-start.5 = (bf16[400,1024]{1,0:T(8,128)(2,1)}, bf16[400,1024]{1,0:T(8,128)(2,1)S(1)}, u32[]{:S(2)}, u32[]{:S(2)}) collective-permute-start(bf16[400,1024]{1,0:T(8,128)(2,1)} %collective-permute-done.4), channel_id=1, source_target_pairs={{0,2},{1,3},{2,4},{3,5},{4,6},{5,7},{6,0},{7,1},{8,10},{9,11},{10,... | collective-permute-start | bytes 2457608 | tf_op jit(solution)/shard_map/ppermute | solution.py:203
  51.8 34.7 %collective-permute-start.11 = (bf16[1,2,1024,128]{3,2,1,0:T(8,128)(2,1)S(1)}, bf16[1,2,1024,128]{3,2,1,0:T(8,128)(2,1)S(1)}, u32[]{:S(2)}, u32[]{:S(2)}) collective-permute-start(bf16[1,2,1024,128]{3,2,1,0:T(8,128)(2,1)S(1)} %slice.189), channel_id=1, source_target_pairs={{0,32},{8,40},{16,48},{24,56},{32,64},{40,72},{48,80},{56,88},{64,... | collective-permute-start | bytes 1572872 | tf_op jit(solution)/shard_map/ppermute | solution.py:42
  67.7 10.3 %collective-permute-start.7 = (bf16[400,512]{1,0:T(8,128)(2,1)S(1)}, bf16[400,512]{1,0:T(8,128)(2,1)S(1)}, u32[]{:S(2)}, u32[]{:S(2)}) collective-permute-start(bf16[400,512]{1,0:T(8,128)(2,1)S(1)} %slice.171), channel_id=1, source_target_pairs={{0,2},{1,3},{2,4},{3,5},{4,6},{5,7},{6,0},{7,1},{8,10},{9,11},{10,... | collective-permute-start | bytes 1228808 | tf_op jit(solution)/shard_map/ppermute | solution.py:205
  71.4 10.1 %collective-permute-start.8 = (bf16[400,512]{1,0:T(8,128)(2,1)S(1)}, bf16[400,512]{1,0:T(8,128)(2,1)S(1)}, u32[]{:S(2)}, u32[]{:S(2)}) collective-permute-start(bf16[400,512]{1,0:T(8,128)(2,1)S(1)} %slice.172), channel_id=1, source_target_pairs={{0,6},{1,7},{2,0},{3,1},{4,2},{5,3},{6,4},{7,5},{8,14},{9,15},{10,... | collective-permute-start | bytes 1228808 | tf_op jit(solution)/shard_map/ppermute | solution.py:206
  78.0 11.8 %collective-permute-start.12 = (bf16[1,2,1024,128]{3,2,1,0:T(8,128)(2,1)S(1)}, bf16[1,2,1024,128]{3,2,1,0:T(8,128)(2,1)S(1)}, u32[]{:S(2)}, u32[]{:S(2)}) collective-permute-start(bf16[1,2,1024,128]{3,2,1,0:T(8,128)(2,1)S(1)} %slice.190), channel_id=1, source_target_pairs={{0,96},{8,104},{16,112},{24,120},{32,0},{40,8},{48,16},{56,24},{64... | collective-permute-start | bytes 1572872 | tf_op jit(solution)/shard_map/ppermute | solution.py:43
  81.5 10.2 %collective-permute-start.14 = (bf16[2,2,1024,128]{3,2,1,0:T(8,128)(2,1)S(1)}, bf16[2,2,1024,128]{3,2,1,0:T(8,128)(2,1)S(1)}, u32[]{:S(2)}, u32[]{:S(2)}) collective-permute-start(bf16[2,2,1024,128]{3,2,1,0:T(8,128)(2,1)S(1)} %collective-permute-done.9.refs_2_), channel_id=1, source_target_pairs={{0,8},{8,0},{16,24},{24,16},{32,40},{40,32},{48,56},{56,48},{64,72... | collective-permute-start | bytes 3145736 | tf_op jit(solution)/shard_map/ppermute | solution.py:45
  84.9 6.9 %collective-permute-start.17 = (bf16[2,2,1024,128]{3,2,1,0:T(8,128)(2,1)S(1)}, bf16[2,2,1024,128]{3,2,1,0:T(8,128)(2,1)S(1)}, u32[]{:S(2)}, u32[]{:S(2)}) collective-permute-start(bf16[2,2,1024,128]{3,2,1,0:T(8,128)(2,1)S(1)} %collective-permute-done.10.refs_5_), channel_id=1, source_target_pairs={{0,8},{8,0},{16,24},{24,16},{32,40},{40,32},{48,56},{56,48},{64,72... | collective-permute-start | bytes 3145736 | tf_op jit(solution)/shard_map/ppermute | solution.py:45
  85.7 28.3 %copy-start.14 = (bf16[400,768]{1,0:T(8,128)(2,1)}, bf16[400,768]{1,0:T(8,128)(2,1)S(1)}, u32[]{:S(2)}) copy-start(bf16[400,768]{1,0:T(8,128)(2,1)S(1)} %fusion.131.refs_0_) | copy-start | bytes 1843204
  85.8 17.4 %collective-permute-start.19 = (bf16[400,768]{1,0:T(8,128)(2,1)S(1)}, bf16[400,768]{1,0:T(8,128)(2,1)S(1)}, u32[]{:S(2)}, u32[]{:S(2)}) collective-permute-start(bf16[400,768]{1,0:T(8,128)(2,1)S(1)} %fusion.131.refs_0_), channel_id=1, source_target_pairs={{0,16},{8,24},{16,0},{24,8},{32,48},{40,56},{48,32},{56,40},{64,80... | collective-permute-start | bytes 1843208 | tf_op jit(solution)/shard_map/ppermute | solution.py:265
  86.4 3.4 %collective-permute-start.15 = (bf16[1,2,1024,128]{3,2,1,0:T(8,128)(2,1)S(1)}, bf16[1,2,1024,128]{3,2,1,0:T(8,128)(2,1)S(1)}, u32[]{:S(2)}, u32[]{:S(2)}) collective-permute-start(bf16[1,2,1024,128]{3,2,1,0:T(8,128)(2,1)S(1)} %collective-permute-done.11.refs_3_), channel_id=1, source_target_pairs={{0,8},{8,0},{16,24},{24,16},{32,40},{40,32},{48,56},{56,48},{64,72... | collective-permute-start | bytes 1572872 | tf_op jit(solution)/shard_map/ppermute | solution.py:45
  89.8 1.9 collective-permute-start.16
  114.1 21.4 %collective-permute-start.20 = (bf16[400,512]{1,0:T(8,128)(2,1)S(1)}, bf16[400,512]{1,0:T(8,128)(2,1)}, u32[]{:S(2)}, u32[]{:S(2)}) collective-permute-start(bf16[400,512]{1,0:T(8,128)(2,1)S(1)} %shard_map.137), channel_id=1, source_target_pairs={{0,16},{8,24},{16,0},{24,8},{32,48},{40,56},{48,32},{56,40},{64,80... | collective-permute-start | bytes 1228808 | tf_op jit(solution)/shard_map/ppermute | solution.py:268
  141.8 12.7 %collective-permute-start.25 = (bf16[400,512]{1,0:T(8,128)(2,1)S(1)}, bf16[400,512]{1,0:T(8,128)(2,1)S(1)}, u32[]{:S(2)}, u32[]{:S(2)}) collective-permute-start(bf16[400,512]{1,0:T(8,128)(2,1)S(1)} %get-tuple-element.23), channel_id=1, source_target_pairs={{0,2},{1,3},{2,4},{3,5},{4,6},{5,7},{6,0},{7,1},{8,10},{9,11},{10,... | collective-permute-start | bytes 1228808 | tf_op jit(solution)/shard_map/ppermute | solution.py:247
  143.2 13.9 %collective-permute-start.27 = (bf16[400,512]{1,0:T(8,128)(2,1)S(1)}, bf16[400,512]{1,0:T(8,128)(2,1)S(1)}, u32[]{:S(2)}, u32[]{:S(2)}) collective-permute-start(bf16[400,512]{1,0:T(8,128)(2,1)S(1)} %get-tuple-element.24), channel_id=1, source_target_pairs={{0,6},{1,7},{2,0},{3,1},{4,2},{5,3},{6,4},{7,5},{8,14},{9,15},{10,... | collective-permute-start | bytes 1228808 | tf_op jit(solution)/shard_map/ppermute | solution.py:248
  144.8 18.5 %collective-permute-start.21 = (bf16[400,512]{1,0:T(8,128)(2,1)S(1)}, bf16[400,512]{1,0:T(8,128)(2,1)S(1)}, u32[]{:S(2)}, u32[]{:S(2)}) collective-permute-start(bf16[400,512]{1,0:T(8,128)(2,1)S(1)} %get-tuple-element.21), channel_id=1, source_target_pairs={{0,2},{1,3},{2,4},{3,5},{4,6},{5,7},{6,0},{7,1},{8,10},{9,11},{10,... | collective-permute-start | bytes 1228808 | tf_op jit(solution)/shard_map/ppermute | solution.py:247
  147.2 19.6 %collective-permute-start.23 = (bf16[400,512]{1,0:T(8,128)(2,1)S(1)}, bf16[400,512]{1,0:T(8,128)(2,1)S(1)}, u32[]{:S(2)}, u32[]{:S(2)}) collective-permute-start(bf16[400,512]{1,0:T(8,128)(2,1)S(1)} %get-tuple-element.22), channel_id=1, source_target_pairs={{0,6},{1,7},{2,0},{3,1},{4,2},{5,3},{6,4},{7,5},{8,14},{9,15},{10,... | collective-permute-start | bytes 1228808 | tf_op jit(solution)/shard_map/ppermute | solution.py:248
  154.7 26.1 %collective-permute-start.26 = (bf16[400,1024]{1,0:T(8,128)(2,1)S(1)}, bf16[400,1024]{1,0:T(8,128)(2,1)S(1)}, u32[]{:S(2)}, u32[]{:S(2)}) collective-permute-start(bf16[400,1024]{1,0:T(8,128)(2,1)S(1)} %pad_maximum_fusion.3), channel_id=1, source_target_pairs={{0,2},{1,3},{2,4},{3,5},{4,6},{5,7},{6,0},{7,1},{8,10},{9,11},{10,... | collective-permute-start | bytes 2457608 | tf_op jit(solution)/shard_map/ppermute | solution.py:256
  157.4 25.8 %collective-permute-start.28 = (bf16[400,1024]{1,0:T(8,128)(2,1)S(1)}, bf16[400,1024]{1,0:T(8,128)(2,1)S(1)}, u32[]{:S(2)}, u32[]{:S(2)}) collective-permute-start(bf16[400,1024]{1,0:T(8,128)(2,1)S(1)} %pad_maximum_fusion.4), channel_id=1, source_target_pairs={{0,6},{1,7},{2,0},{3,1},{4,2},{5,3},{6,4},{7,5},{8,14},{9,15},{10,... | collective-permute-start | bytes 2457608 | tf_op jit(solution)/shard_map/ppermute | solution.py:257
  164.4 31.4 %collective-permute-start.22 = (bf16[400,1024]{1,0:T(8,128)(2,1)}, bf16[400,1024]{1,0:T(8,128)(2,1)}, u32[]{:S(2)}, u32[]{:S(2)}) collective-permute-start(bf16[400,1024]{1,0:T(8,128)(2,1)} %pad_maximum_fusion.1), channel_id=1, source_target_pairs={{0,2},{1,3},{2,4},{3,5},{4,6},{5,7},{6,0},{7,1},{8,10},{9,11},{10,... | collective-permute-start | bytes 2457608 | tf_op jit(solution)/shard_map/ppermute | solution.py:256
  167.9 29.8 %collective-permute-start.24 = (bf16[400,1024]{1,0:T(8,128)(2,1)}, bf16[400,1024]{1,0:T(8,128)(2,1)S(1)}, u32[]{:S(2)}, u32[]{:S(2)}) collective-permute-start(bf16[400,1024]{1,0:T(8,128)(2,1)} %pad_maximum_fusion.2), channel_id=1, source_target_pairs={{0,6},{1,7},{2,0},{3,1},{4,2},{5,3},{6,4},{7,5},{8,14},{9,15},{10,... | collective-permute-start | bytes 2457608 | tf_op jit(solution)/shard_map/ppermute | solution.py:257
  184.7 14.7 %collective-permute-start.29 = (bf16[400,1024]{1,0:T(8,128)(2,1)}, bf16[400,1024]{1,0:T(8,128)(2,1)}, u32[]{:S(2)}, u32[]{:S(2)}) collective-permute-start(bf16[400,1024]{1,0:T(8,128)(2,1)} %add_convert_fusion.1), channel_id=1, source_target_pairs={{0,1},{1,0},{2,3},{3,2},{4,5},{5,4},{6,7},{7,6},{8,9},{9,8},{10,11... | collective-permute-start | bytes 2457608 | tf_op jit(solution)/shard_map/ppermute | solution.py:259
  (33 other events, 286.4 us)

commit v2 on v1

v2 whole, which is shorter than its diff:
```python
import functools

import jax
import jax.numpy as jnp
from jax import lax
from jax.experimental import pallas as pl
from jax.experimental.pallas import tpu as pltpu
from jax.sharding import PartitionSpec as P

HEAD = 128
LIVE = 400
ALL = (0, LIVE)
SIDE = 40
VMEM = 60 * 2**20
PAD = 432
LOCAL = 16

rope_base = 1000000.0
norm_eps = 1e-06
bf16, f32 = jnp.bfloat16, jnp.float32


def along_x(d):
    return [(i, ((i // 2 + d) % 4) * 2 + i % 2) for i in range(8)]


def along_y(d):
    return [(i, ((i // 4 + d) % 4) * 4 + i % 4) for i in range(16)]


ACROSS_Z_LO = [(i, i ^ 1) for i in range(8)]
ACROSS_Z_HI = [(i, i ^ 2) for i in range(16)]


def dot(a, b):
    return jnp.dot(a, b, preferred_element_type=f32)


SAME_HALF = [[i for i in range(16) if (i // 2) % 2 == half] for half in range(2)]


def gather_prefix(rows):
    every = lax.all_gather(rows, "cand", axis=0, axis_index_groups=SAME_HALF)
    return every.reshape((-1,) + rows.shape[1:])


def tie(values, *after):
    return lax.optimization_barrier((values, after))[0]


def finish_kernel(slot_row, tokens, term, up, down, crossed, out):
    update = term[...] + up[...].astype(f32) + down[...].astype(f32) + crossed[...].astype(f32)
    coarse = update.astype(bf16)
    fine = (update - coarse.astype(f32)).astype(bf16)
    at = lax.broadcasted_iota(jnp.int32, (tokens.shape[0], term.shape[0]), 1)
    spread = jnp.where(slot_row[...] == at, 1.0, 0.0).astype(bf16)
    placed = dot(spread, coarse) + dot(spread, fine)
    out[...] = (tokens[...].astype(f32) + placed).astype(bf16)


def finish(slot_row, tokens, *parts):
    tile = 256
    columns = lambda array: pl.BlockSpec((array.shape[0], tile), lambda i: (0, i))
    return pl.pallas_call(
        finish_kernel,
        out_shape=jax.ShapeDtypeStruct(tokens.shape, bf16),
        grid=(tokens.shape[1] // tile,),
        in_specs=[pl.BlockSpec((tokens.shape[0], 1), lambda i: (0, 0)), columns(tokens)]
        + [columns(part) for part in parts],
        out_specs=columns(tokens),
        compiler_params=pltpu.CompilerParams(vmem_limit_bytes=VMEM),
        cost_estimate=pl.CostEstimate(
            flops=4 * LIVE * tokens.size, bytes_accessed=8 * tokens.size, transcendentals=0
        ),
    )(slot_row[:, None], tokens, *parts)


def list_kernel(at, mine, other, problem_slot, out):
    half_at = at[0]
    for t, table in enumerate((mine, other)):

        def one(c, carry):
            offset, count0, count1 = carry
            slot, length = problem_slot[table[0, c]], table[1, c]
            place = (slot >> 3) * 4 + (slot & 3)
            side = place >> 3
            near = jnp.where(((slot >> 2) & 1) == half_at, 1, 0)
            to = jnp.where(side == 1, SIDE + count1, count0)
            out[t, 0, to] = place
            out[t, 1, to] = offset
            out[t, 2, to] = length
            return offset + length, count0 + near * (1 - side), count1 + near * side

        zero = jnp.int32(0)
        _, count0, count1 = lax.fori_loop(0, table.shape[1], one, (zero, zero, zero))
        for side, count in enumerate((count0, count1)):
            for r in range(3):
                out[t, r, side * SIDE + count] = out[t, r, side * SIDE]
            out[t, 3, side] = (count + 1) // 2


def candidate_lists(at, mine, other, problem_slot):
    return pl.pallas_call(
        list_kernel,
        out_shape=jax.ShapeDtypeStruct((2, 4, 2 * SIDE), jnp.int32),
        in_specs=[pl.BlockSpec(memory_space=pltpu.SMEM)] * 4,
        out_specs=pl.BlockSpec(memory_space=pltpu.SMEM),
    )(at, mine, other, problem_slot)


def attention_kernel(which, bounds, n_rows, n_kv, meta, *refs):
    row_refs, kv_refs = refs[:n_rows], refs[n_rows : n_rows + n_kv]
    out_ref, keys, values, rows, outs, sems = refs[n_rows + n_kv :]
    step = 24
    group = 4
    copies = []
    for side in range(2):
        held = pl.ds(side * LOCAL // 2, LOCAL // 2)
        for i, (ref, buffer) in enumerate(zip(kv_refs, (keys, values))):
            copies.append(pltpu.make_async_copy(ref.at[held], buffer.at[held], sems.at[2 * side + i]))
    for copy in copies:
        copy.start()
    at = 0
    for ref in row_refs:
        count = ref.shape[0]
        for i in range(group + 2):
            rows[i, at : at + count, :] = ref[:, i * HEAD : (i + 1) * HEAD].astype(f32)
        at += count
    for i in range(group + 2):
        rows[i, at:, :] = jnp.zeros((PAD - at, HEAD), f32)
    outs[...] = jnp.zeros_like(outs)
    scale = HEAD ** (-0.5)
    t_at = lax.broadcasted_iota(jnp.int32, (group, step, step), 1).reshape(group * step, step)
    j_at = lax.broadcasted_iota(jnp.int32, (group * step, step), 1)
    row_t = lax.broadcasted_iota(jnp.int32, (step, HEAD), 0)
    contract = (((1,), (1,)), ((), ()))

    def attend(where, offset, length):
        here = pl.ds(offset, step)
        query = jnp.concatenate([rows[h, here, :] for h in range(group)], 0).astype(bf16)
        new_key = rows[group, here, :].astype(bf16)
        new_value = rows[group + 1, here, :].astype(bf16)
        pre = lax.dot_general(query, keys[where], contract, preferred_element_type=f32)
        own = lax.dot_general(query, new_key, contract, preferred_element_type=f32)
        own = jnp.where((j_at <= t_at) & (j_at < length), own, -1e30)
        top = jnp.maximum(jnp.max(pre, -1, keepdims=True), jnp.max(own, -1, keepdims=True))
        pre = jnp.exp((pre - top) * scale)
        own = jnp.exp((own - top) * scale)
        total = jnp.sum(pre, -1, keepdims=True) + jnp.sum(own, -1, keepdims=True)
        mixed = dot(pre.astype(bf16), values[where]) + dot(own.astype(bf16), new_value)
        return mixed / total

    def two(first_at, i, _):
        entries = [[meta[which, r, first_at + 2 * i + j] for r in range(3)] for j in range(2)]
        results = [attend(*entry) for entry in entries]
        for (_, offset, length), mixed in zip(entries, results):
            here = pl.ds(offset, step)
            for h in range(group):
                new = mixed[h * step : (h + 1) * step]
                outs[h, here, :] = jnp.where(row_t < length, new, outs[h, here, :])
        return 0

    for side in range(2):
        for copy in copies[2 * side : 2 * side + 2]:
            copy.wait()
        lax.fori_loop(0, meta[which, 3, side], functools.partial(two, side * SIDE), 0)
    first, last = bounds
    for h in range(group):
        out_ref[:, h * HEAD : (h + 1) * HEAD] = outs[h, first:last, :].astype(bf16)


def attention(which, bounds, meta, row_parts, kv_parts):
    first, last = bounds
    count = 32
    return pl.pallas_call(
        functools.partial(attention_kernel, which, bounds, len(row_parts), len(kv_parts)),
        out_shape=jax.ShapeDtypeStruct((last - first, 4 * HEAD), bf16),
        in_specs=[pl.BlockSpec(memory_space=pltpu.SMEM)]
        + [pl.BlockSpec(memory_space=pltpu.VMEM)] * len(row_parts)
        + [pl.BlockSpec(memory_space=pl.ANY)] * len(kv_parts),
        out_specs=pl.BlockSpec(memory_space=pltpu.VMEM),
        scratch_shapes=[
            pltpu.VMEM((LOCAL, 1024, HEAD), bf16),
            pltpu.VMEM((LOCAL, 1024, HEAD), bf16),
            pltpu.VMEM((6, PAD, HEAD), f32),
            pltpu.VMEM((4, PAD, HEAD), f32),
            pltpu.SemaphoreType.DMA((4,)),
        ],
        compiler_params=pltpu.CompilerParams(vmem_limit_bytes=VMEM),
        cost_estimate=pl.CostEstimate(
            flops=2 * 2 * count * 96 * 1024 * HEAD,
            bytes_accessed=LOCAL * 2 * 1024 * HEAD * 2,
            transcendentals=count * 96 * 1024,
        ),
    )(meta, *row_parts, *kv_parts)


def on_device(
    tokens,
    norm_gain,
    w_query,
    b_query,
    w_key,
    b_key,
    w_value,
    b_value,
    w_out,
    prefix_keys,
    prefix_values,
    problem_slot,
    cand_problem,
    step_len,
):
    cand_count, step, width = tokens.shape
    tp_at, cand_at = lax.axis_index("tp"), lax.axis_index("cand")
    x_at, z_at = tp_at // 2, tp_at % 2
    half_at = (cand_at // 2) % 2

    z, o = z_at, 1 - z_at
    cut = width // 2

    def feature(d, z):
        return (((x_at + d) % 4) * 2 + z) * width

    def pass_up(part):
        return lax.ppermute(part, "tp", along_x(1))

    def pass_down(part):
        return lax.ppermute(part, "tp", along_x(-1))

    def pass_over(part):
        return lax.ppermute(part, "tp", ACROSS_Z_LO)

    problems = cand_problem[:, 0]
    order = jnp.arange(cand_count)
    offsets = jnp.sum(jnp.where(order[None, :] < order[:, None], step_len[None, :], 0), axis=1)
    row_at, step_at = jnp.arange(LIVE), jnp.arange(step)
    slot_row = jnp.where(
        step_at[None, :] < step_len[:, None], offsets[:, None] + step_at[None, :], -1
    ).reshape(-1)
    pick = (slot_row[None, :] == row_at[:, None]).astype(bf16)
    flat = tokens.reshape(cand_count * step, width)
    block = dot(pick, flat).astype(bf16)

    kv_parts = [gather_prefix(prefix_keys), gather_prefix(prefix_values)]

    low, high, across = pass_up(block), pass_down(block), pass_over(block)
    table = jnp.stack([problems, step_len])
    other_table = lax.ppermute(table, "cand", ACROSS_Z_HI)
    lists = candidate_lists(half_at[None], table, other_table, problem_slot)
    low, high, across = tie((low, high, across), lists)
    o_low, o_high = pass_up(across), pass_down(across)
    far0, far1 = pass_up(low[:, :cut]), pass_down(high[:, cut:])
    o_far0, o_far1 = pass_up(o_low[:, :cut]), pass_down(o_high[:, cut:])

    slots = jnp.sum(
        jnp.where(
            problems[:, None] == jnp.arange(problem_slot.shape[0])[None, :],
            problem_slot[None, :],
            0,
        ),
        axis=1,
    )
    is_near = ((slots // 4) % 2 == half_at).astype(bf16)
    traits = jnp.stack(
        [
            jnp.broadcast_to(step_at.astype(bf16)[None, :], (cand_count, step)),
            jnp.broadcast_to(is_near[:, None], (cand_count, step)),
        ],
        axis=-1,
    ).reshape(cand_count * step, 2)
    traits = dot(pick, traits)
    frequency = rope_base ** (-(jnp.arange(HEAD // 2, dtype=f32) * 2.0 / HEAD))
    angles = (prefix_keys.shape[1] + traits[:, :1]) * frequency[None, :]
    cosine = jnp.concatenate([jnp.cos(angles), jnp.cos(angles)], -1)
    sine = jnp.concatenate([-jnp.sin(angles), jnp.sin(angles)], -1)
    bias = jnp.concatenate([b_query, b_key, b_value]).astype(f32)[None, :]
    w_pair = jnp.concatenate([w_key, w_value], axis=1)
    gain = norm_gain.astype(f32)
    first = tie(block, low)
    blocks = [
        (first, feature(0, z)),
        (low, feature(3, z)),
        (high, feature(1, z)),
        (across, feature(0, o)),
        (far0, feature(2, z)),
        (far1, feature(2, z) + cut),
        (o_low, feature(3, o)),
        (o_high, feature(1, o)),
        (o_far0, feature(2, o)),
        (o_far1, feature(2, o) + cut),
    ]
    total, pair, squares = 0.0, 0.0, 0.0
    for part, start in blocks:
        features = part.shape[1]
        wide = part.astype(f32)
        scaled = (wide * lax.dynamic_slice(gain, (start,), (features,))[None, :]).astype(bf16)
        total = total + dot(
            scaled, lax.dynamic_slice(w_query, (start, 0), (features, w_query.shape[1]))
        )
        pair = pair + dot(
            scaled, lax.dynamic_slice(w_pair, (start, 0), (features, w_pair.shape[1]))
        )
        squares = squares + jnp.sum(wide * wide, axis=1, keepdims=True)
    scale = lax.rsqrt(squares / (8 * width) + norm_eps)
    raw = jnp.concatenate([total, pair], 1) * scale + bias
    heads = []
    for h in range(5):
        head = raw[:, h * HEAD : (h + 1) * HEAD]
        heads.append(head * cosine + jnp.roll(head, HEAD // 2, axis=1) * sine)
    heads.append(raw[:, 5 * HEAD :])
    rows = jnp.concatenate(heads, 1).astype(bf16)

    others = lax.ppermute(rows, "cand", ACROSS_Z_HI)
    near = attention(0, ALL, lists, [rows], kv_parts)
    others = tie(others, near)
    for_other = attention(1, ALL, lists, [others], kv_parts)
    back = lax.ppermute(for_other, "cand", ACROSS_Z_HI)
    attended = jnp.where(traits[:, 1:] > 0.5, near, back)

    def term(d, z, attended, first=0, last=width):
        start = feature(d, z) + first
        return dot(attended, lax.dynamic_slice(w_out, (0, start), (w_out.shape[0], last - first)))

    later, far = attended, []
    for side in (o, z):
        left = term(2, side, later, 0, cut).astype(bf16)
        right = term(2, side, tie(attended, left), cut, width).astype(bf16)
        far.append((pass_up(left), pass_down(right)))
        later = tie(attended, right)
    near_sums = []
    for side, (left, right) in zip((o, z), far):
        up, down = term(1, side, later), term(3, side, later)
        up = jnp.concatenate([up[:, :cut] + left.astype(f32), up[:, cut:]], 1).astype(bf16)
        down = jnp.concatenate([down[:, :cut], down[:, cut:] + right.astype(f32)], 1).astype(bf16)
        last = tie(attended, up, down)
        near_sums.append((term(0, side, last), pass_up(up), pass_down(down)))
    (own, up, down), rest = near_sums[0], near_sums[1]
    crossed = pass_over((own + up.astype(f32) + down.astype(f32)).astype(bf16))
    return finish(slot_row, flat, *rest, crossed).reshape(tokens.shape)


def solution(mesh):
    in_specs = (
        P("cand", None, "tp"),
        P(),
        P(None, "tp"),
        P("tp"),
        P(None, "tp"),
        P("tp"),
        P(None, "tp"),
        P("tp"),
        P("tp", None),
        P("cand", None, "tp"),
        P("cand", None, "tp"),
        P(),
        P("cand", None),
        P("cand"),
    )
    out_specs = P("cand", None, "tp")
    return jax.shard_map(
        on_device, mesh=mesh, in_specs=in_specs, out_specs=out_specs, check_vma=False
    )
```

time: 210 us -> 201 us (0.957)
  local copies, waits for them, and re-layouts: 26.5 us -> 11.4 us
  between operations: 0.84 us -> 14.4 us
  Pallas kernels: 21.7 us -> 34.3 us
  waiting for transfers between devices: 76.2 us -> 63.8 us
  other arithmetic: 16.9 us -> 8.18 us
  matrix products: 30.7 us -> 34.1 us
  starting transfers between devices: 33.6 us -> 31.3 us
    ppermute x28 -> x19, waiting for transfers between devices: 76.2 us -> 46.4 us  [the longest x8 39.3 us: pass_down(): return lax.ppermute(part, 'tp', along_x(-1))]
    unnamed x72 -> x35, local copies, waits for them, and re-layouts: 21.1 us -> 6.12 us
    pallas_call x2 -> x4, Pallas kernels: 21.7 us -> 34.3 us  [the longest x2 25.6 us: attention(): pl.pallas_call(functools.partial(attention_kernel, which, bounds, len(row...]
    ppermute x1, waiting for transfers between devices: 0.01 us -> 9.62 us  [on_device(): back = lax.ppermute(for_other, 'cand', ACROSS_Z_HI)]
    ppermute x1, waiting for transfers between devices: 0.01 us -> 7.11 us  [on_device(): other_table = lax.ppermute(table, 'cand', ACROSS_Z_HI)]
    reduce_sum x10 -> x8, other arithmetic: 5.37 us -> 1.93 us  [on_device(): squares = squares + jnp.sum(wide * wide, axis=1, keepdims=True)]
    dot_general x21 -> x32, matrix products: 30.7 us -> 34.1 us  [dot(): return jnp.dot(a, b, preferred_element_type=f32)]
    slice x14 -> x9, local copies, waits for them, and re-layouts: 3.6 us -> 0.66 us  [the longest x1 0.34 us: on_device(): heads.append(head * cosine + jnp.roll(head, HEAD // 2, axis=1) * sine)]
  transfers between devices with their start and end apart: 30 -> 23, of which waited for: 13 -> 10; matrix products, arithmetic and copies ran while one was open for 22% -> 24% of each run, Pallas kernels for 5% -> 8%
where the time goes in v2:
time: 201 us; the launch traced here: 197 us
  waiting for transfers between devices  63.8 us (32%)
  Pallas kernels  34.3 us (17%)
  matrix products  34.1 us (17%)
  starting transfers between devices  31.3 us (16%)
  between operations  14.4 us (7%)
  local copies, waits for them, and re-layouts  11.4 us (6%)
  other arithmetic  8.18 us (4%)
    ppermute x8, waiting for transfers between devices, pass_down(): return lax.ppermute(part, 'tp', along_x(-1))  39.3 us
    dot_general x32, matrix products, dot(): return jnp.dot(a, b, preferred_element_type=f32)  34.1 us
    pallas_call x2, Pallas kernels, attention(): pl.pallas_call(functools.partial(attention_kernel, which, bounds, len(row...  25.6 us
    ppermute x8, starting transfers between devices, pass_up(): return lax.ppermute(part, 'tp', along_x(1))  19.4 us
    ppermute x1, waiting for transfers between devices, on_device(): back = lax.ppermute(for_other, 'cand', ACROSS_Z_HI)  9.62 us
    ppermute x1, waiting for transfers between devices, on_device(): other_table = lax.ppermute(table, 'cand', ACROSS_Z_HI)  7.11 us
    pallas_call x1, Pallas kernels, finish(): pl.pallas_call(finish_kernel, out_shape=jax.ShapeDtypeStruct(tokens.shape...  6.14 us
    unnamed x35, local copies, waits for them, and re-layouts  6.12 us
  transfers between devices with their start and end apart: 23, of which 10 were waited for; matrix products, arithmetic and copies ran while one was open for 24% of the time, Pallas kernels for 8%

profile of v2, /device:TPU:30, one launch (start us, length us, event | category | flops | bytes accessed | tf_op | source)
XLA Modules:
  0.0 197.4 jit_solution(6276203240538772283)
XLA Ops:
  8.9 2.2 %convolution_convert_fusion = bf16[400,1024]{1,0:T(8,128)(2,1)S(1)} fusion(bf16[768,1024]{1,0:T(8,128)(2,1)} %bitcast.21, s32[768]{0:T(1024)S(1)} %select_n.172), kind=kOutput, calls=%fused_computation.25 | convolution fusion | flops 629862400 | bytes 2395136 | tf_op jit(solution)/shard_map/dot_general | solution.py:36
  13.2 1.9 collective-permute-start.3
  15.7 3.6 %collective-permute-start = (s32[2,32]{1,0:T(2,128)}, s32[2,32]{1,0:T(2,128)}, u32[]{:S(2)}, u32[]{:S(2)}) collective-permute-start(s32[2,32]{1,0:T(2,128)} %pad_add_fusion.mine), channel_id=1, source_target_pairs={{0,16},{8,24},{16,0},{24,8},{32,48},{40,56},{48,32},{56,40},{64,80... | collective-permute-start | bytes 776 | tf_op jit(solution)/shard_map/ppermute | solution.py:249
  19.5 3.3 %constant_dynamic-update-slice_fusion.1 = bf16[8192,256]{1,0:T(8,128)(2,1)} fusion(bf16[8192,128]{1,0:T(8,128)(2,1)} %param.18), kind=kLoop, calls=%fused_computation.168 | loop fusion | bytes 4194304
  25.9 3.2 %constant_dynamic-update-slice_fusion = bf16[8192,256]{1,0:T(8,128)(2,1)} fusion(bf16[8192,256]{1,0:T(8,128)(2,1)} %constant_dynamic-update-slice_fusion.1, bf16[8192,128]{1,0:T(8,128)(2,1)} %param.20), kind=kLoop, calls=%fused_computation.167 | loop fusion | bytes 4194304 | tf_op jit(solution)/shard_map/concatenate | solution.py:278
  29.2 7.1 %collective-permute-done.other = s32[2,32]{1,0:T(2,128)} collective-permute-done((s32[2,32]{1,0:T(2,128)}, s32[2,32]{1,0:T(2,128)}, u32[]{:S(2)}, u32[]{:S(2)}) %collective-permute-start) | collective-permute-done | bytes 288 | tf_op jit(solution)/shard_map/ppermute | solution.py:249
  36.3 2.5 %shard_map.136.meta = s32[2,4,80]{2,1,0:T(4,128)} custom-call(s32[1]{0:T(128)} %bitcast.2.at, s32[2,32]{1,0:T(2,128)} %pad_add_fusion.mine, s32[2,32]{1,0:T(2,128)} %collective-permute-done.other, s32[32]{0:T(128)} %problem_slot.1), custom_call_target="tpu_custom_call" | custom-call | tf_op jit(solution)/shard_map/pallas_call | solution.py:103
  39.7 2.4 %collective-permute-start.6 = (bf16[400,1024]{1,0:T(8,128)(2,1)S(1)}, bf16[400,1024]{1,0:T(8,128)(2,1)S(1)}, u32[]{:S(2)}, u32[]{:S(2)}) collective-permute-start(bf16[400,1024]{1,0:T(8,128)(2,1)S(1)} %collective-permute-done.3), channel_id=1, source_target_pairs={{0,2},{1,3},{2,4},{3,5},{4,6},{5,7},{6,0},{7,1},{8,10},{9,11},{10,... | collective-permute-start | bytes 2457608 | tf_op jit(solution)/shard_map/ppermute | solution.py:226
  42.3 3.2 %collective-permute-start.4 = (bf16[400,512]{1,0:T(8,128)(2,1)S(1)}, bf16[400,512]{1,0:T(8,128)(2,1)S(1)}, u32[]{:S(2)}, u32[]{:S(2)}) collective-permute-start(bf16[400,512]{1,0:T(8,128)(2,1)S(1)} %slice.108), channel_id=1, source_target_pairs={{0,2},{1,3},{2,4},{3,5},{4,6},{5,7},{6,0},{7,1},{8,10},{9,11},{10,... | collective-permute-start | bytes 1228808 | tf_op jit(solution)/shard_map/ppermute | solution.py:226
  47.4 2.0 %fusion.43 = f32[400,512]{1,0:T(8,128)S(1)} fusion(bf16[8192,512]{1,0:T(8,128)(2,1)} %param.16, s32[]{:T(128)S(6)} %select_n.181, bf16[400,1024]{1,0:T(8,128)(2,1)S(1)} %convolution_convert_fusion, f32[1024]{0:T(1024)S(1)} %get-tuple-element.42), kind=kOutput, calls=%fused_computation.70 | convolution fusion | flops 420659200 | bytes 2691076 | tf_op jit(solution)/shard_map/dot_general | solution.py:36
  50.2 2.0 %convolution_add_fusion.3 = f32[400,512]{1,0:T(8,128)S(1)} fusion(f32[400,512]{1,0:T(8,128)S(1)} %fusion.43, bf16[8192,512]{1,0:T(8,128)(2,1)} %param.16, s32[]{:T(128)S(6)} %select_n.183, bf16[400,1024]{1,0:T(8,128)(2,1)S(1)} %collective-permute-done.1, f32[1024]{0:T(1024)S(1)} %get-tuple-element.41), kind=kOutput, calls=%fused_computation.29 | convolution fusion | flops 420864000 | bytes 3510276 | tf_op jit(solution)/shard_map/dot_general | solution.py:36
  52.2 1.8 convolution_add_fusion.2
  55.5 11.6 %collective-permute-done.5 = bf16[400,512]{1,0:T(8,128)(2,1)S(1)} collective-permute-done((bf16[400,512]{1,0:T(8,128)(2,1)S(1)}, bf16[400,512]{1,0:T(8,128)(2,1)S(1)}, u32[]{:S(2)}, u32[]{:S(2)}) %collective-permute-start.5) | collective-permute-done | bytes 409632 | tf_op jit(solution)/shard_map/ppermute | solution.py:229
  68.6 3.5 %collective-permute-start.8 = (bf16[400,512]{1,0:T(8,128)(2,1)S(1)}, bf16[400,512]{1,0:T(8,128)(2,1)S(1)}, u32[]{:S(2)}, u32[]{:S(2)}) collective-permute-start(bf16[400,512]{1,0:T(8,128)(2,1)S(1)} %slice.138), channel_id=1, source_target_pairs={{0,2},{1,3},{2,4},{3,5},{4,6},{5,7},{6,0},{7,1},{8,10},{9,11},{10,... | collective-permute-start | bytes 1228808 | tf_op jit(solution)/shard_map/ppermute | solution.py:226
  74.5 3.8 %collective-permute-done.9 = bf16[400,512]{1,0:T(8,128)(2,1)S(1)} collective-permute-done((bf16[400,512]{1,0:T(8,128)(2,1)S(1)}, bf16[400,512]{1,0:T(8,128)(2,1)S(1)}, u32[]{:S(2)}, u32[]{:S(2)}) %collective-permute-start.9) | collective-permute-done | bytes 409632 | tf_op jit(solution)/shard_map/ppermute | solution.py:229
  84.3 12.3 %shard_map.137 = bf16[400,512]{1,0:T(8,128)(2,1)} custom-call(s32[2,4,80]{2,1,0:T(4,128)} %shard_map.136.meta, bf16[400,768]{1,0:T(8,128)(2,1)} %copy-done.2, bf16[16,1024,128]{2,1,0:T(8,128)(2,1)} %all-gather.5.cloned.1.call-done.refs_1_, bf16[16,1024,128]{2,1,0:T(8,128)(2,1)} %all-gather.7.cloned.1.call-done.refs_2_), custom_call_target="tpu_custom_call" | custom-call | flops 1610612736 | bytes 8388608 | tf_op jit(solution)/shard_map/pallas_call | solution.py:175
  98.0 13.3 %shard_map.138 = bf16[400,512]{1,0:T(8,128)(2,1)} custom-call(s32[2,4,80]{2,1,0:T(4,128)} %shard_map.136.meta, bf16[400,768]{1,0:T(8,128)(2,1)} %copy-done.5, bf16[16,1024,128]{2,1,0:T(8,128)(2,1)} %all-gather.5.cloned.1.call-done.refs_1_, bf16[16,1024,128]{2,1,0:T(8,128)(2,1)} %all-gather.7.cloned.1.call-done.refs_2_), custom_call_target="tpu_custom_call" | custom-call | flops 1610612736 | bytes 8388608 | tf_op jit(solution)/shard_map/pallas_call | solution.py:175
  111.4 9.6 %collective-permute-done.11 = bf16[400,512]{1,0:T(8,128)(2,1)S(1)} collective-permute-done((bf16[400,512]{1,0:T(8,128)(2,1)}, bf16[400,512]{1,0:T(8,128)(2,1)S(1)}, u32[]{:S(2)}, u32[]{:S(2)}) %collective-permute-start.11) | collective-permute-done | bytes 409632 | tf_op jit(solution)/shard_map/ppermute | solution.py:318
  125.4 2.8 %collective-permute-start.12 = (bf16[400,512]{1,0:T(8,128)(2,1)S(1)}, bf16[400,512]{1,0:T(8,128)(2,1)S(1)}, u32[]{:S(2)}, u32[]{:S(2)}) collective-permute-start(bf16[400,512]{1,0:T(8,128)(2,1)S(1)} %convolution_convert_fusion.2), channel_id=1, source_target_pairs={{0,2},{1,3},{2,4},{3,5},{4,6},{5,7},{6,0},{7,1},{8,10},{9,11},{10,... | collective-permute-start | bytes 1228808 | tf_op jit(solution)/shard_map/ppermute | solution.py:226
  129.8 1.8 fusion.34
  131.7 1.8 fusion.26
  133.5 3.5 %collective-permute-start.16 = (bf16[400,512]{1,0:T(8,128)(2,1)S(1)}, bf16[400,512]{1,0:T(8,128)(2,1)S(1)}, u32[]{:S(2)}, u32[]{:S(2)}) collective-permute-start(bf16[400,512]{1,0:T(8,128)(2,1)S(1)} %convolution_convert_fusion.4), channel_id=1, source_target_pairs={{0,2},{1,3},{2,4},{3,5},{4,6},{5,7},{6,0},{7,1},{8,10},{9,11},{10,... | collective-permute-start | bytes 1228808 | tf_op jit(solution)/shard_map/ppermute | solution.py:226
  137.0 1.8 fusion.28
  138.9 8.9 %collective-permute-done.17 = bf16[400,512]{1,0:T(8,128)(2,1)S(1)} collective-permute-done((bf16[400,512]{1,0:T(8,128)(2,1)S(1)}, bf16[400,512]{1,0:T(8,128)(2,1)S(1)}, u32[]{:S(2)}, u32[]{:S(2)}) %collective-permute-start.17) | collective-permute-done | bytes 409632 | tf_op jit(solution)/shard_map/ppermute | solution.py:229
  148.4 3.3 %collective-permute-start.18 = (bf16[400,1024]{1,0:T(8,128)(2,1)S(1)}, bf16[400,1024]{1,0:T(8,128)(2,1)S(1)}, u32[]{:S(2)}, u32[]{:S(2)}) collective-permute-start(bf16[400,1024]{1,0:T(8,128)(2,1)S(1)} %pad_maximum_fusion.2), channel_id=1, source_target_pairs={{0,2},{1,3},{2,4},{3,5},{4,6},{5,7},{6,0},{7,1},{8,10},{9,11},{10,... | collective-permute-start | bytes 2457608 | tf_op jit(solution)/shard_map/ppermute | solution.py:226
  151.7 1.8 fusion.32
  154.2 2.1 %collective-permute-start.15 = (bf16[400,1024]{1,0:T(8,128)(2,1)S(1)}, bf16[400,1024]{1,0:T(8,128)(2,1)}, u32[]{:S(2)}, u32[]{:S(2)}) collective-permute-start(bf16[400,1024]{1,0:T(8,128)(2,1)S(1)} %pad_maximum_fusion.1), channel_id=1, source_target_pairs={{0,6},{1,7},{2,0},{3,1},{4,2},{5,3},{6,4},{7,5},{8,14},{9,15},{10,... | collective-permute-start | bytes 2457608 | tf_op jit(solution)/shard_map/ppermute | solution.py:229
  156.3 13.7 %collective-permute-done.19 = bf16[400,1024]{1,0:T(8,128)(2,1)S(1)} collective-permute-done((bf16[400,1024]{1,0:T(8,128)(2,1)S(1)}, bf16[400,1024]{1,0:T(8,128)(2,1)S(1)}, u32[]{:S(2)}, u32[]{:S(2)}) %collective-permute-start.19) | collective-permute-done | bytes 819232 | tf_op jit(solution)/shard_map/ppermute | solution.py:229
  170.0 1.9 add_convert_fusion
  173.6 3.0 %fusion.30.term = f32[400,1024]{1,0:T(8,128)} fusion(bf16[400,512]{1,0:T(8,128)(2,1)S(1)} %broadcast_select_fusion, bf16[512,8192]{1,0:T(8,128)(2,1)} %param.22, s32[]{:T(128)S(6)} %select_n.181), kind=kOutput, calls=%fused_computation.57 | convolution fusion | flops 419430400 | bytes 3096580 | tf_op jit(solution)/shard_map/dot_general | solution.py:36
  178.9 5.5 %collective-permute-done.20.crossed = bf16[400,1024]{1,0:T(8,128)(2,1)} collective-permute-done((bf16[400,1024]{1,0:T(8,128)(2,1)S(1)}, bf16[400,1024]{1,0:T(8,128)(2,1)}, u32[]{:S(2)}, u32[]{:S(2)}) %collective-permute-start.20) | collective-permute-done | bytes 819232 | tf_op jit(solution)/shard_map/ppermute | solution.py:232
  184.4 6.1 %shard_map.139 = bf16[768,1024]{1,0:T(8,128)(2,1)} custom-call(s32[768,1]{1,0:T(8,128)} %select_n.195.slot_row, bf16[768,1024]{1,0:T(8,128)(2,1)} %bitcast.22, f32[400,1024]{1,0:T(8,128)} %fusion.30.term, bf16[400,1024]{1,0:T(8,128)(2,1)} %collective-permute-done.14.up, bf16[400,1024]{1,0:T(8,128)(2,1)} %collective-permute-done.15.down, ...), custom_call_target="tpu_custom_call" | custom-call | flops 1258291200 | bytes 6291456 | tf_op jit(solution)/shard_map/pallas_call | solution.py:64
  (143 shorter events, 35.6 us)
Async XLA Ops:
  6.5 77.6 %all-gather.5.cloned.1.call-start = ((), (), s32[]{:S(2)}) async-start(), calls=%async_computation | async-start | bytes 4718592 | tf_op jit(solution)/shard_map/all_gather | solution.py:43
  7.3 76.9 %all-gather.7.cloned.1.call-start = ((), (), s32[]{:S(2)}) async-start(), calls=%async_computation.1 | async-start | bytes 4718592 | tf_op jit(solution)/shard_map/all_gather | solution.py:43
  8.9 6.3 %copy-start.9 = (s32[32]{0:T(128)S(1)}, s32[32]{0:T(128)}, u32[]{:S(2)}) copy-start(s32[32]{0:T(128)} %param.27) | copy-start | bytes 388
  8.9 6.3 %copy-start.14 = (s32[32,1]{0,1:T(1,128)S(1)}, s32[32,1]{0,1:T(1,128)}, u32[]{:S(2)}) copy-start(s32[32,1]{0,1:T(1,128)} %param.26) | copy-start | bytes 388
  11.1 27.6 %collective-permute-start.1 = (bf16[400,1024]{1,0:T(8,128)(2,1)S(1)}, bf16[400,1024]{1,0:T(8,128)(2,1)S(1)}, u32[]{:S(2)}, u32[]{:S(2)}) collective-permute-start(bf16[400,1024]{1,0:T(8,128)(2,1)S(1)} %convolution_convert_fusion), channel_id=1, source_target_pairs={{0,2},{1,3},{2,4},{3,5},{4,6},{5,7},{6,0},{7,1},{8,10},{9,11},{10,... | collective-permute-start | bytes 2457608 | tf_op jit(solution)/shard_map/ppermute | solution.py:226
  11.7 27.1 %collective-permute-start.2 = (bf16[400,1024]{1,0:T(8,128)(2,1)S(1)}, bf16[400,1024]{1,0:T(8,128)(2,1)S(1)}, u32[]{:S(2)}, u32[]{:S(2)}) collective-permute-start(bf16[400,1024]{1,0:T(8,128)(2,1)S(1)} %convolution_convert_fusion), channel_id=1, source_target_pairs={{0,6},{1,7},{2,0},{3,1},{4,2},{5,3},{6,4},{7,5},{8,14},{9,15},{10,... | collective-permute-start | bytes 2457608 | tf_op jit(solution)/shard_map/ppermute | solution.py:229
  13.2 25.6 %collective-permute-start.3 = (bf16[400,1024]{1,0:T(8,128)(2,1)S(1)}, bf16[400,1024]{1,0:T(8,128)(2,1)S(1)}, u32[]{:S(2)}, u32[]{:S(2)}) collective-permute-start(bf16[400,1024]{1,0:T(8,128)(2,1)S(1)} %convolution_convert_fusion), channel_id=1, source_target_pairs={{0,1},{1,0},{2,3},{3,2},{4,5},{5,4},{6,7},{7,6},{8,9},{9,8},{10,11... | collective-permute-start | bytes 2457608 | tf_op jit(solution)/shard_map/ppermute | solution.py:232
  15.7 20.5 %collective-permute-start = (s32[2,32]{1,0:T(2,128)}, s32[2,32]{1,0:T(2,128)}, u32[]{:S(2)}, u32[]{:S(2)}) collective-permute-start(s32[2,32]{1,0:T(2,128)} %pad_add_fusion.mine), channel_id=1, source_target_pairs={{0,16},{8,24},{16,0},{24,8},{32,48},{40,56},{48,32},{56,40},{64,80... | collective-permute-start | bytes 776 | tf_op jit(solution)/shard_map/ppermute | solution.py:249
  19.5 3.4 %copy-start.11 = (s32[32]{0:T(128)S(1)}, s32[32]{0:T(128)}, u32[]{:S(2)}) copy-start(s32[32]{0:T(128)} %problem_slot.1) | copy-start | bytes 388
  19.5 6.3 %copy-start.6 = (bf16[8192]{0:T(1024)(128)(2,1)S(1)}, bf16[8192]{0:T(1024)(128)(2,1)}, u32[]{:S(2)}) copy-start(bf16[8192]{0:T(1024)(128)(2,1)} %param.15) | copy-start | bytes 49156
  25.9 3.2 %copy-start.10 = (bf16[512]{0:T(512)(128)(2,1)S(1)}, bf16[512]{0:T(512)(128)(2,1)}, u32[]{:S(2)}) copy-start(bf16[512]{0:T(512)(128)(2,1)} %param.17) | copy-start | bytes 3076
  38.8 29.6 %collective-permute-start.7 = (bf16[400,1024]{1,0:T(8,128)(2,1)S(1)}, bf16[400,1024]{1,0:T(8,128)(2,1)S(1)}, u32[]{:S(2)}, u32[]{:S(2)}) collective-permute-start(bf16[400,1024]{1,0:T(8,128)(2,1)S(1)} %collective-permute-done.3), channel_id=1, source_target_pairs={{0,6},{1,7},{2,0},{3,1},{4,2},{5,3},{6,4},{7,5},{8,14},{9,15},{10,... | collective-permute-start | bytes 2457608 | tf_op jit(solution)/shard_map/ppermute | solution.py:229
  39.7 28.8 %collective-permute-start.6 = (bf16[400,1024]{1,0:T(8,128)(2,1)S(1)}, bf16[400,1024]{1,0:T(8,128)(2,1)S(1)}, u32[]{:S(2)}, u32[]{:S(2)}) collective-permute-start(bf16[400,1024]{1,0:T(8,128)(2,1)S(1)} %collective-permute-done.3), channel_id=1, source_target_pairs={{0,2},{1,3},{2,4},{3,5},{4,6},{5,7},{6,0},{7,1},{8,10},{9,11},{10,... | collective-permute-start | bytes 2457608 | tf_op jit(solution)/shard_map/ppermute | solution.py:226
  42.2 24.9 %collective-permute-start.5 = (bf16[400,512]{1,0:T(8,128)(2,1)S(1)}, bf16[400,512]{1,0:T(8,128)(2,1)S(1)}, u32[]{:S(2)}, u32[]{:S(2)}) collective-permute-start(bf16[400,512]{1,0:T(8,128)(2,1)S(1)} %slice.109), channel_id=1, source_target_pairs={{0,6},{1,7},{2,0},{3,1},{4,2},{5,3},{6,4},{7,5},{8,14},{9,15},{10,... | collective-permute-start | bytes 1228808 | tf_op jit(solution)/shard_map/ppermute | solution.py:229
  42.3 25.0 %collective-permute-start.4 = (bf16[400,512]{1,0:T(8,128)(2,1)S(1)}, bf16[400,512]{1,0:T(8,128)(2,1)S(1)}, u32[]{:S(2)}, u32[]{:S(2)}) collective-permute-start(bf16[400,512]{1,0:T(8,128)(2,1)S(1)} %slice.108), channel_id=1, source_target_pairs={{0,2},{1,3},{2,4},{3,5},{4,6},{5,7},{6,0},{7,1},{8,10},{9,11},{10,... | collective-permute-start | bytes 1228808 | tf_op jit(solution)/shard_map/ppermute | solution.py:226
  47.3 6.7 %slice-start = ((s8[8388608]{0:T(1024)(128)(4,1)}), s8[4194304]{0:T(1024)(128)(4,1)S(1)}, s32[]{:S(2)}) async-start(s8[8388608]{0:T(1024)(128)(4,1)} %bitcast.23), calls=%async_computation.2 | async-start | bytes 8388608
  50.2 3.9 %slice-start.1 = ((s8[8388608]{0:T(1024)(128)(4,1)}), s8[4194304]{0:T(1024)(128)(4,1)S(1)}, s32[]{:S(2)}) async-start(s8[8388608]{0:T(1024)(128)(4,1)} %bitcast.23), calls=%async_computation.3 | async-start | bytes 8388608
  68.4 9.9 %collective-permute-start.9 = (bf16[400,512]{1,0:T(8,128)(2,1)S(1)}, bf16[400,512]{1,0:T(8,128)(2,1)S(1)}, u32[]{:S(2)}, u32[]{:S(2)}) collective-permute-start(bf16[400,512]{1,0:T(8,128)(2,1)S(1)} %slice.139), channel_id=1, source_target_pairs={{0,6},{1,7},{2,0},{3,1},{4,2},{5,3},{6,4},{7,5},{8,14},{9,15},{10,... | collective-permute-start | bytes 1228808 | tf_op jit(solution)/shard_map/ppermute | solution.py:229
  68.6 9.9 %collective-permute-start.8 = (bf16[400,512]{1,0:T(8,128)(2,1)S(1)}, bf16[400,512]{1,0:T(8,128)(2,1)S(1)}, u32[]{:S(2)}, u32[]{:S(2)}) collective-permute-start(bf16[400,512]{1,0:T(8,128)(2,1)S(1)} %slice.138), channel_id=1, source_target_pairs={{0,2},{1,3},{2,4},{3,5},{4,6},{5,7},{6,0},{7,1},{8,10},{9,11},{10,... | collective-permute-start | bytes 1228808 | tf_op jit(solution)/shard_map/ppermute | solution.py:226
  83.5 13.7 %collective-permute-start.10 = (bf16[400,768]{1,0:T(8,128)(2,1)S(1)}, bf16[400,768]{1,0:T(8,128)(2,1)S(1)}, u32[]{:S(2)}, u32[]{:S(2)}) collective-permute-start(bf16[400,768]{1,0:T(8,128)(2,1)S(1)} %fusion.122.refs_0_), channel_id=1, source_target_pairs={{0,16},{8,24},{16,0},{24,8},{32,48},{40,56},{48,32},{56,40},{64,80... | collective-permute-start | bytes 1843208 | tf_op jit(solution)/shard_map/ppermute | solution.py:314
  96.6 14.7 %copy-start.8 = (f32[400,2]{0,1:T(2,128)S(1)}, f32[400,2]{0,1:T(2,128)}, u32[]{:S(2)}) copy-start(f32[400,2]{0,1:T(2,128)} %copy-done.7) | copy-start | bytes 9604
  96.7 24.3 %copy-start.1 = (bf16[400,512]{1,0:T(8,128)(2,1)S(1)}, bf16[400,512]{1,0:T(8,128)(2,1)}, u32[]{:S(2)}) copy-start(bf16[400,512]{1,0:T(8,128)(2,1)} %shard_map.137) | copy-start | bytes 1228804
  111.2 9.7 %collective-permute-start.11 = (bf16[400,512]{1,0:T(8,128)(2,1)}, bf16[400,512]{1,0:T(8,128)(2,1)S(1)}, u32[]{:S(2)}, u32[]{:S(2)}) collective-permute-start(bf16[400,512]{1,0:T(8,128)(2,1)} %shard_map.138), channel_id=1, source_target_pairs={{0,16},{8,24},{16,0},{24,8},{32,48},{40,56},{48,32},{56,40},{64,80... | collective-permute-start | bytes 1228808 | tf_op jit(solution)/shard_map/ppermute | solution.py:318
  125.4 28.2 %collective-permute-start.12 = (bf16[400,512]{1,0:T(8,128)(2,1)S(1)}, bf16[400,512]{1,0:T(8,128)(2,1)S(1)}, u32[]{:S(2)}, u32[]{:S(2)}) collective-permute-start(bf16[400,512]{1,0:T(8,128)(2,1)S(1)} %convolution_convert_fusion.2), channel_id=1, source_target_pairs={{0,2},{1,3},{2,4},{3,5},{4,6},{5,7},{6,0},{7,1},{8,10},{9,11},{10,... | collective-permute-start | bytes 1228808 | tf_op jit(solution)/shard_map/ppermute | solution.py:226
  129.7 24.3 %collective-permute-start.13 = (bf16[400,512]{1,0:T(8,128)(2,1)S(1)}, bf16[400,512]{1,0:T(8,128)(2,1)S(1)}, u32[]{:S(2)}, u32[]{:S(2)}) collective-permute-start(bf16[400,512]{1,0:T(8,128)(2,1)S(1)} %convolution_convert_fusion.1), channel_id=1, source_target_pairs={{0,6},{1,7},{2,0},{3,1},{4,2},{5,3},{6,4},{7,5},{8,14},{9,15},{10,... | collective-permute-start | bytes 1228808 | tf_op jit(solution)/shard_map/ppermute | solution.py:229
  129.8 18.1 %collective-permute-start.17 = (bf16[400,512]{1,0:T(8,128)(2,1)S(1)}, bf16[400,512]{1,0:T(8,128)(2,1)S(1)}, u32[]{:S(2)}, u32[]{:S(2)}) collective-permute-start(bf16[400,512]{1,0:T(8,128)(2,1)S(1)} %convolution_convert_fusion.3), channel_id=1, source_target_pairs={{0,6},{1,7},{2,0},{3,1},{4,2},{5,3},{6,4},{7,5},{8,14},{9,15},{10,... | collective-permute-start | bytes 1228808 | tf_op jit(solution)/shard_map/ppermute | solution.py:229
  133.5 14.7 %collective-permute-start.16 = (bf16[400,512]{1,0:T(8,128)(2,1)S(1)}, bf16[400,512]{1,0:T(8,128)(2,1)S(1)}, u32[]{:S(2)}, u32[]{:S(2)}) collective-permute-start(bf16[400,512]{1,0:T(8,128)(2,1)S(1)} %convolution_convert_fusion.4), channel_id=1, source_target_pairs={{0,2},{1,3},{2,4},{3,5},{4,6},{5,7},{6,0},{7,1},{8,10},{9,11},{10,... | collective-permute-start | bytes 1228808 | tf_op jit(solution)/shard_map/ppermute | solution.py:226
  148.1 21.9 %collective-permute-start.19 = (bf16[400,1024]{1,0:T(8,128)(2,1)S(1)}, bf16[400,1024]{1,0:T(8,128)(2,1)S(1)}, u32[]{:S(2)}, u32[]{:S(2)}) collective-permute-start(bf16[400,1024]{1,0:T(8,128)(2,1)S(1)} %pad_maximum_fusion.3), channel_id=1, source_target_pairs={{0,6},{1,7},{2,0},{3,1},{4,2},{5,3},{6,4},{7,5},{8,14},{9,15},{10,... | collective-permute-start | bytes 2457608 | tf_op jit(solution)/shard_map/ppermute | solution.py:229
  148.4 21.6 %collective-permute-start.18 = (bf16[400,1024]{1,0:T(8,128)(2,1)S(1)}, bf16[400,1024]{1,0:T(8,128)(2,1)S(1)}, u32[]{:S(2)}, u32[]{:S(2)}) collective-permute-start(bf16[400,1024]{1,0:T(8,128)(2,1)S(1)} %pad_maximum_fusion.2), channel_id=1, source_target_pairs={{0,2},{1,3},{2,4},{3,5},{4,6},{5,7},{6,0},{7,1},{8,10},{9,11},{10,... | collective-permute-start | bytes 2457608 | tf_op jit(solution)/shard_map/ppermute | solution.py:226
  153.9 23.7 %collective-permute-start.14 = (bf16[400,1024]{1,0:T(8,128)(2,1)S(1)}, bf16[400,1024]{1,0:T(8,128)(2,1)}, u32[]{:S(2)}, u32[]{:S(2)}) collective-permute-start(bf16[400,1024]{1,0:T(8,128)(2,1)S(1)} %pad_maximum_fusion), channel_id=1, source_target_pairs={{0,2},{1,3},{2,4},{3,5},{4,6},{5,7},{6,0},{7,1},{8,10},{9,11},{10,... | collective-permute-start | bytes 2457608 | tf_op jit(solution)/shard_map/ppermute | solution.py:226
  154.2 24.7 %collective-permute-start.15 = (bf16[400,1024]{1,0:T(8,128)(2,1)S(1)}, bf16[400,1024]{1,0:T(8,128)(2,1)}, u32[]{:S(2)}, u32[]{:S(2)}) collective-permute-start(bf16[400,1024]{1,0:T(8,128)(2,1)S(1)} %pad_maximum_fusion.1), channel_id=1, source_target_pairs={{0,6},{1,7},{2,0},{3,1},{4,2},{5,3},{6,4},{7,5},{8,14},{9,15},{10,... | collective-permute-start | bytes 2457608 | tf_op jit(solution)/shard_map/ppermute | solution.py:229
  171.9 12.5 %collective-permute-start.20 = (bf16[400,1024]{1,0:T(8,128)(2,1)S(1)}, bf16[400,1024]{1,0:T(8,128)(2,1)}, u32[]{:S(2)}, u32[]{:S(2)}) collective-permute-start(bf16[400,1024]{1,0:T(8,128)(2,1)S(1)} %add_convert_fusion), channel_id=1, source_target_pairs={{0,1},{1,0},{2,3},{3,2},{4,5},{5,4},{6,7},{7,6},{8,9},{9,8},{10,11... | collective-permute-start | bytes 2457608 | tf_op jit(solution)/shard_map/ppermute | solution.py:232
  (8 other events, 13.1 us)
Sparse Core Ops, SparseCore 0:
  9.1 32.2 all-gather.4
  43.1 32.0 all-gather.6

commit v3 on v2

--- a/solution.py
+++ b/solution.py
@@ -11,7 +11,6 @@
 LIVE = 400
 ALL = (0, LIVE)
 SIDE = 40
-VMEM = 60 * 2**20
 PAD = 432
 LOCAL = 16
 
@@ -36,54 +35,147 @@
     return jnp.dot(a, b, preferred_element_type=f32)
 
 
-SAME_HALF = [[i for i in range(16) if (i // 2) % 2 == half] for half in range(2)]
-
-
-def gather_prefix(rows):
-    every = lax.all_gather(rows, "cand", axis=0, axis_index_groups=SAME_HALF)
-    return every.reshape((-1,) + rows.shape[1:])
+ACROSS_CORE = [(i, i ^ 1) for i in range(16)]
 
 
 def tie(values, *after):
     return lax.optimization_barrier((values, after))[0]
 
 
-def finish_kernel(slot_row, tokens, term, up, down, crossed, out):
+def project_kernel(n_parts, plan, has_sum, is_last, starts, *refs):
+    parts, refs = refs[:n_parts], refs[n_parts:]
+    gain, w_query, w_key, w_value = refs[:4]
+    refs = refs[4:]
+    if has_sum:
+        sum_in, square_in = refs[:2]
+        refs = refs[2:]
+    if is_last:
+        bias, cosine, sine, out, total, squares = refs
+    else:
+        sum_out, square_out, total, squares = refs
+    at = pl.program_id(0)
+
+    @pl.when(at == 0)
+    def _():
+        if has_sum:
+            total[...] = sum_in[...]
+            squares[...] = square_in[...]
+        else:
+            total[...] = jnp.zeros_like(total)
+            squares[...] = jnp.zeros_like(squares)
+
+    for place, pieces in enumerate(plan):
+
+        @pl.when(at == place)
+        def _(pieces=pieces):
+            wide = [parts[i][first : first + count, :] for i, first, count in pieces]
+            wide = jnp.concatenate(wide, 0).astype(f32)
+            scaled = (wide * gain[...].astype(f32)).astype(bf16)
+            total[:, :512] += dot(scaled, w_query[...])
+            keys = jnp.concatenate([w_key[...], w_value[...]], 1)
+            total[:, 512:] += dot(scaled, keys)
+            square = wide * wide
+            squares[...] += sum(square[:, i : i + HEAD] for i in range(0, square.shape[1], HEAD))
+
+    @pl.when(at == len(plan) - 1)
+    def _():
+        if not is_last:
+            sum_out[...] = total[...]
+            square_out[...] = squares[...]
+            return
+        mean = jnp.sum(squares[...], axis=1, keepdims=True) / 8192.0
+        raw = total[...] * lax.rsqrt(mean + norm_eps) + bias[...]
+        for h in range(6):
+            head = raw[:, h * HEAD : (h + 1) * HEAD]
+            if h < 5:
+                turned = jnp.concatenate([head[:, HEAD // 2 :], head[:, : HEAD // 2]], 1)
+                head = head * cosine[...] + turned * sine[...]
+            out[:, h * HEAD : (h + 1) * HEAD] = head.astype(bf16)
+
+
+def project_parts(parts, plan, firsts, sums, last_args, gain, w_query, w_key, w_value):
+    rows, deep = LIVE, parts[0].shape[1]
+    starts = jnp.stack([first // deep for first in firsts])
+    steps = starts.shape[0]
+    whole = lambda array: pl.BlockSpec(array.shape, lambda i, s: (0,) * array.ndim)
+    arrays = list(parts)
+    operands = arrays + [gain, w_query, w_key, w_value]
+    specs = [whole(array) for array in arrays] + [
+        pl.BlockSpec((1, deep), lambda i, s: (0, s[i])),
+        pl.BlockSpec((deep, w_query.shape[1]), lambda i, s: (s[i], 0)),
+        pl.BlockSpec((deep, HEAD), lambda i, s: (s[i], 0)),
+        pl.BlockSpec((deep, HEAD), lambda i, s: (s[i], 0)),
+    ]
+    if sums is not None:
+        operands += list(sums)
+        specs += [whole(array) for array in sums]
+    if last_args is not None:
+        operands += list(last_args)
+        specs += [whole(array) for array in last_args]
+        out_shape = jax.ShapeDtypeStruct((rows, 768), bf16)
+        out_specs = pl.BlockSpec((rows, 768), lambda i, s: (0, 0))
+    else:
+        out_shape = (
+            jax.ShapeDtypeStruct((rows, 768), f32),
+            jax.ShapeDtypeStruct((rows, 128), f32),
+        )
+        out_specs = (
+            pl.BlockSpec((rows, 768), lambda i, s: (0, 0)),
+            pl.BlockSpec((rows, 128), lambda i, s: (0, 0)),
+        )
+    return pl.pallas_call(
+        functools.partial(project_kernel, len(parts), plan, sums is not None, last_args is not None),
+        out_shape=out_shape,
+        grid_spec=pltpu.PrefetchScalarGridSpec(
+            num_scalar_prefetch=1,
+            grid=(steps,),
+            in_specs=specs,
+            out_specs=out_specs,
+            scratch_shapes=[pltpu.VMEM((rows, 768), f32), pltpu.VMEM((rows, 128), f32)],
+        ),
+        compiler_params=pltpu.CompilerParams(vmem_limit_bytes=46 * 2**20),
+        cost_estimate=pl.CostEstimate(
+            flops=2 * rows * deep * steps * 768,
+            bytes_accessed=steps * deep * 768 * 2,
+            transcendentals=0,
+        ),
+    )(starts, *operands)
+
+
+def finish_kernel(spread, tokens, term, up, down, crossed, out):
     update = term[...] + up[...].astype(f32) + down[...].astype(f32) + crossed[...].astype(f32)
     coarse = update.astype(bf16)
     fine = (update - coarse.astype(f32)).astype(bf16)
-    at = lax.broadcasted_iota(jnp.int32, (tokens.shape[0], term.shape[0]), 1)
-    spread = jnp.where(slot_row[...] == at, 1.0, 0.0).astype(bf16)
-    placed = dot(spread, coarse) + dot(spread, fine)
+    placed = dot(spread[...], coarse) + dot(spread[...], fine)
     out[...] = (tokens[...].astype(f32) + placed).astype(bf16)
 
 
-def finish(slot_row, tokens, *parts):
+def finish(spread, tokens, *parts):
     tile = 256
     columns = lambda array: pl.BlockSpec((array.shape[0], tile), lambda i: (0, i))
     return pl.pallas_call(
         finish_kernel,
         out_shape=jax.ShapeDtypeStruct(tokens.shape, bf16),
         grid=(tokens.shape[1] // tile,),
-        in_specs=[pl.BlockSpec((tokens.shape[0], 1), lambda i: (0, 0)), columns(tokens)]
+        in_specs=[pl.BlockSpec(spread.shape, lambda i: (0, 0)), columns(tokens)]
         + [columns(part) for part in parts],
         out_specs=columns(tokens),
-        compiler_params=pltpu.CompilerParams(vmem_limit_bytes=VMEM),
+        compiler_params=pltpu.CompilerParams(vmem_limit_bytes=16 * 2**20),
         cost_estimate=pl.CostEstimate(
             flops=4 * LIVE * tokens.size, bytes_accessed=8 * tokens.size, transcendentals=0
         ),
-    )(slot_row[:, None], tokens, *parts)
+    )(spread, tokens, *parts)
 
 
 def list_kernel(at, mine, other, problem_slot, out):
-    half_at = at[0]
+    y_at, half_at, core_at = at[0], at[1], at[2]
     for t, table in enumerate((mine, other)):
 
         def one(c, carry):
             offset, count0, count1 = carry
             slot, length = problem_slot[table[0, c]], table[1, c]
-            place = (slot >> 3) * 4 + (slot & 3)
-            side = place >> 3
+            side = ((slot >> 1) & 1) ^ core_at
+            place = ((y_at - (slot >> 3)) & 3) * 2 + (slot & 1) + 8 * side
             near = jnp.where(((slot >> 2) & 1) == half_at, 1, 0)
             to = jnp.where(side == 1, SIDE + count1, count0)
             out[t, 0, to] = place
@@ -115,9 +207,12 @@
     group = 4
     copies = []
     for side in range(2):
-        held = pl.ds(side * LOCAL // 2, LOCAL // 2)
-        for i, (ref, buffer) in enumerate(zip(kv_refs, (keys, values))):
-            copies.append(pltpu.make_async_copy(ref.at[held], buffer.at[held], sems.at[2 * side + i]))
+        for which_buffer, buffer in enumerate((keys, values)):
+            for i in range(4):
+                part = (which_buffer * 2 + side) * 4 + i
+                behind = (4 - i) % 4 if which_buffer else i
+                held = pl.ds(side * 8 + behind * 2, 2)
+                copies.append(pltpu.make_async_copy(kv_refs[part], buffer.at[held], sems.at[part]))
     for copy in copies:
         copy.start()
     at = 0
@@ -161,7 +256,7 @@
         return 0
 
     for side in range(2):
-        for copy in copies[2 * side : 2 * side + 2]:
+        for copy in copies[8 * side : 8 * side + 8]:
             copy.wait()
         lax.fori_loop(0, meta[which, 3, side], functools.partial(two, side * SIDE), 0)
     first, last = bounds
@@ -177,16 +272,16 @@
         out_shape=jax.ShapeDtypeStruct((last - first, 4 * HEAD), bf16),
         in_specs=[pl.BlockSpec(memory_space=pltpu.SMEM)]
         + [pl.BlockSpec(memory_space=pltpu.VMEM)] * len(row_parts)
-        + [pl.BlockSpec(memory_space=pl.ANY)] * len(kv_parts),
+        + [pl.BlockSpec(memory_space=pltpu.HBM)] * len(kv_parts),
         out_specs=pl.BlockSpec(memory_space=pltpu.VMEM),
         scratch_shapes=[
             pltpu.VMEM((LOCAL, 1024, HEAD), bf16),
             pltpu.VMEM((LOCAL, 1024, HEAD), bf16),
             pltpu.VMEM((6, PAD, HEAD), f32),
             pltpu.VMEM((4, PAD, HEAD), f32),
-            pltpu.SemaphoreType.DMA((4,)),
+            pltpu.SemaphoreType.DMA((16,)),
         ],
-        compiler_params=pltpu.CompilerParams(vmem_limit_bytes=VMEM),
+        compiler_params=pltpu.CompilerParams(vmem_limit_bytes=28 * 2**20),
         cost_estimate=pl.CostEstimate(
             flops=2 * 2 * count * 96 * 1024 * HEAD,
             bytes_accessed=LOCAL * 2 * 1024 * HEAD * 2,
@@ -214,10 +309,9 @@
     cand_count, step, width = tokens.shape
     tp_at, cand_at = lax.axis_index("tp"), lax.axis_index("cand")
     x_at, z_at = tp_at // 2, tp_at % 2
-    half_at = (cand_at // 2) % 2
+    y_at, half_at, core_at = cand_at // 4, (cand_at // 2) % 2, cand_at % 2
 
     z, o = z_at, 1 - z_at
-    cut = width // 2
 
     def feature(d, z):
         return (((x_at + d) % 4) * 2 + z) * width
@@ -239,19 +333,51 @@
         step_at[None, :] < step_len[:, None], offsets[:, None] + step_at[None, :], -1
     ).reshape(-1)
     pick = (slot_row[None, :] == row_at[:, None]).astype(bf16)
+    spread = (slot_row[:, None] == row_at[None, :]).astype(bf16)
     flat = tokens.reshape(cand_count * step, width)
     block = dot(pick, flat).astype(bf16)
 
-    kv_parts = [gather_prefix(prefix_keys), gather_prefix(prefix_values)]
-
     low, high, across = pass_up(block), pass_down(block), pass_over(block)
+    key_parts, value_parts = [prefix_keys], [prefix_values]
+
+    def pass_prefixes():
+        key_parts.append(lax.ppermute(key_parts[-1], "cand", along_y(1)))
+        value_parts.append(lax.ppermute(value_parts[-1], "cand", along_y(-1)))
+
+    pass_prefixes()
     table = jnp.stack([problems, step_len])
-    other_table = lax.ppermute(table, "cand", ACROSS_Z_HI)
-    lists = candidate_lists(half_at[None], table, other_table, problem_slot)
-    low, high, across = tie((low, high, across), lists)
+    low, high, across, key_parts[1], value_parts[1], late_table = tie(
+        (low, high, across, key_parts[1], value_parts[1], table), block
+    )
     o_low, o_high = pass_up(across), pass_down(across)
-    far0, far1 = pass_up(low[:, :cut]), pass_down(high[:, cut:])
-    o_far0, o_far1 = pass_up(o_low[:, :cut]), pass_down(o_high[:, cut:])
+    other_table = lax.ppermute(late_table, "cand", ACROSS_Z_HI)
+    pass_prefixes()
+    lists = candidate_lists(
+        jnp.stack([y_at, half_at, core_at]), table, other_table, problem_slot
+    )
+    add_up = functools.partial(
+        project_parts, gain=norm_gain[None, :], w_query=w_query, w_key=w_key, w_value=w_value
+    )
+    all_rows = [((i, 0, LIVE),) for i in range(4)]
+    sums = add_up(
+        (block, low, high, across),
+        all_rows,
+        (feature(0, z), feature(3, z), feature(1, z), feature(0, o)),
+        None,
+        None,
+    )
+    o_low, o_high, low2, key_parts[2], value_parts[2], sums = tie(
+        (o_low, o_high, low, key_parts[2], value_parts[2], sums), block
+    )
+    fars = pass_up(low2), pass_down(o_high)
+    pass_prefixes()
+    sums = add_up((o_low, o_high), all_rows[:2], (feature(3, o), feature(1, o)), sums, None)
+    key_parts, value_parts, sums, lists = tie((key_parts, value_parts, sums, lists), block)
+    kv_parts = [
+        part
+        for parts in (key_parts, value_parts)
+        for part in parts + [lax.ppermute(part, "cand", ACROSS_CORE) for part in parts]
+    ]
 
     slots = jnp.sum(
         jnp.where(
@@ -275,41 +401,8 @@
     cosine = jnp.concatenate([jnp.cos(angles), jnp.cos(angles)], -1)
     sine = jnp.concatenate([-jnp.sin(angles), jnp.sin(angles)], -1)
     bias = jnp.concatenate([b_query, b_key, b_value]).astype(f32)[None, :]
-    w_pair = jnp.concatenate([w_key, w_value], axis=1)
-    gain = norm_gain.astype(f32)
-    first = tie(block, low)
-    blocks = [
-        (first, feature(0, z)),
-        (low, feature(3, z)),
-        (high, feature(1, z)),
-        (across, feature(0, o)),
-        (far0, feature(2, z)),
-        (far1, feature(2, z) + cut),
-        (o_low, feature(3, o)),
-        (o_high, feature(1, o)),
-        (o_far0, feature(2, o)),
-        (o_far1, feature(2, o) + cut),
-    ]
-    total, pair, squares = 0.0, 0.0, 0.0
-    for part, start in blocks:
-        features = part.shape[1]
-        wide = part.astype(f32)
-        scaled = (wide * lax.dynamic_slice(gain, (start,), (features,))[None, :]).astype(bf16)
-        total = total + dot(
-            scaled, lax.dynamic_slice(w_query, (start, 0), (features, w_query.shape[1]))
-        )
-        pair = pair + dot(
-            scaled, lax.dynamic_slice(w_pair, (start, 0), (features, w_pair.shape[1]))
-        )
-        squares = squares + jnp.sum(wide * wide, axis=1, keepdims=True)
-    scale = lax.rsqrt(squares / (8 * width) + norm_eps)
-    raw = jnp.concatenate([total, pair], 1) * scale + bias
-    heads = []
-    for h in range(5):
-        head = raw[:, h * HEAD : (h + 1) * HEAD]
-        heads.append(head * cosine + jnp.roll(head, HEAD // 2, axis=1) * sine)
-    heads.append(raw[:, 5 * HEAD :])
-    rows = jnp.concatenate(heads, 1).astype(bf16)
+    last_args = bias, cosine, sine
+    rows = add_up(fars, all_rows[:2], (feature(2, z), feature(2, o)), sums, last_args)
 
     others = lax.ppermute(rows, "cand", ACROSS_Z_HI)
     near = attention(0, ALL, lists, [rows], kv_parts)
@@ -317,6 +410,8 @@
     for_other = attention(1, ALL, lists, [others], kv_parts)
     back = lax.ppermute(for_other, "cand", ACROSS_Z_HI)
     attended = jnp.where(traits[:, 1:] > 0.5, near, back)
+
+    cut = width // 2
 
     def term(d, z, attended, first=0, last=width):
         start = feature(d, z) + first
@@ -330,6 +425,7 @@
         later = tie(attended, right)
     near_sums = []
     for side, (left, right) in zip((o, z), far):
+        later = tie(attended, left, right)
         up, down = term(1, side, later), term(3, side, later)
         up = jnp.concatenate([up[:, :cut] + left.astype(f32), up[:, cut:]], 1).astype(bf16)
         down = jnp.concatenate([down[:, :cut], down[:, cut:] + right.astype(f32)], 1).astype(bf16)
@@ -337,7 +433,7 @@
         near_sums.append((term(0, side, last), pass_up(up), pass_down(down)))
     (own, up, down), rest = near_sums[0], near_sums[1]
     crossed = pass_over((own + up.astype(f32) + down.astype(f32)).astype(bf16))
-    return finish(slot_row, flat, *rest, crossed).reshape(tokens.shape)
+    return finish(spread, flat, *rest, crossed).reshape(tokens.shape)
 
 
 def solution(mesh):

time: 201 us -> 189 us (0.940)
  the two profiles are of different devices: /device:TPU:30 before, /device:TPU:14 now
where the time goes in v3:
time: 189 us; the launch traced here: 187 us
  waiting for transfers between devices  71.1 us (38%)
  Pallas kernels  42.3 us (22%)
  starting transfers between devices  34.6 us (18%)
  matrix products  20.3 us (11%)
  local copies, waits for them, and re-layouts  11.5 us (6%)
  other arithmetic  6.57 us (3%)
    ppermute x7, waiting for transfers between devices, pass_down(): return lax.ppermute(part, 'tp', along_x(-1))  26.3 us
    dot_general x12, matrix products, dot(): return jnp.dot(a, b, preferred_element_type=f32)  20.3 us
    pallas_call x2, Pallas kernels, attention(): pl.pallas_call(functools.partial(attention_kernel, which, bounds, len(row...  19.6 us
    pallas_call x3, Pallas kernels, project_parts(): pl.pallas_call(functools.partial(project_kernel, len(parts), plan, sums i...  14.8 us
    ppermute x3, waiting for transfers between devices, pass_prefixes(): key_parts.append(lax.ppermute(key_parts[-1], 'cand', along_y(1)))  11 us
    unnamed x52, local copies, waits for them, and re-layouts  10.8 us
    ppermute x7, waiting for transfers between devices, pass_up(): return lax.ppermute(part, 'tp', along_x(1))  10.8 us
    ppermute x1, waiting for transfers between devices, on_device(): back = lax.ppermute(for_other, 'cand', ACROSS_Z_HI)  10.7 us
  transfers between devices with their start and end apart: 33, of which 17 were waited for; matrix products, arithmetic and copies ran while one was open for 12% of the time, Pallas kernels for 15%

profile of v3, /device:TPU:14, one launch (start us, length us, event | category | flops | bytes accessed | tf_op | source)
XLA Modules:
  0.0 187.1 jit_solution(6114617678590648304)
XLA Ops:
  1.7 2.4 %convolution_convert_fusion.refs_0_ = bf16[400,1024]{1,0:T(8,128)(2,1)S(1)} fusion(bf16[768,1024]{1,0:T(8,128)(2,1)} %bitcast.33, s32[768]{0:T(1024)S(1)} %select_n.162), kind=kOutput, calls=%fused_computation.3 | convolution fusion | flops 629862400 | bytes 2395136 | tf_op jit(solution)/shard_map/dot_general | solution.py:35
  6.1 1.9 %collective-permute-start.2 = (bf16[400,1024]{1,0:T(8,128)(2,1)S(1)}, bf16[400,1024]{1,0:T(8,128)(2,1)}, u32[]{:S(2)}, u32[]{:S(2)}) collective-permute-start(bf16[400,1024]{1,0:T(8,128)(2,1)S(1)} %convolution_convert_fusion.refs_0_), channel_id=1, source_target_pairs={{0,1},{1,0},{2,3},{3,2},{4,5},{5,4},{6,7},{7,6},{8,9},{9,8},{10,11... | collective-permute-start | bytes 2457608 | tf_op jit(solution)/shard_map/ppermute | solution.py:326
  11.0 10.9 %collective-permute-done.3.refs_2_ = bf16[2,1024,128]{2,1,0:T(8,128)(2,1)} collective-permute-done((bf16[2,1024,128]{2,1,0:T(8,128)(2,1)S(1)}, bf16[2,1024,128]{2,1,0:T(8,128)(2,1)}, u32[]{:S(2)}, u32[]{:S(2)}) %collective-permute-start.3) | collective-permute-done | bytes 524320 | tf_op jit(solution)/shard_map/ppermute | solution.py:344
  33.7 6.3 %shard_map.136 = (f32[400,768]{1,0:T(8,128)S(1)}, f32[400,128]{1,0:T(8,128)S(1)}) custom-call(s32[4]{0:T(128)S(1)} %pad_add_fusion.1.starts, bf16[400,1024]{1,0:T(8,128)(2,1)S(1)} %copy-done.11, bf16[400,1024]{1,0:T(8,128)(2,1)} %collective-permute-done.refs_1_, bf16[400,1024]{1,0:T(8,128)(2,1)S(1)} %copy-done.13, ...), custom_call_target="tpu_custom_call" | custom-call | flops 2516582400 | bytes 6291456 | tf_op jit(solution)/shard_map/pallas_call | solution.py:126
  42.5 3.1 %collective-permute-done.5.refs_0_ = bf16[400,1024]{1,0:T(8,128)(2,1)} collective-permute-done((bf16[400,1024]{1,0:T(8,128)(2,1)}, bf16[400,1024]{1,0:T(8,128)(2,1)}, u32[]{:S(2)}, u32[]{:S(2)}) %collective-permute-start.5) | collective-permute-done | bytes 819232 | tf_op jit(solution)/shard_map/ppermute | solution.py:320
  45.5 1.9 %collective-permute-done.6.refs_1_ = bf16[400,1024]{1,0:T(8,128)(2,1)} collective-permute-done((bf16[400,1024]{1,0:T(8,128)(2,1)}, bf16[400,1024]{1,0:T(8,128)(2,1)}, u32[]{:S(2)}, u32[]{:S(2)}) %collective-permute-start.6) | collective-permute-done | bytes 819232 | tf_op jit(solution)/shard_map/ppermute | solution.py:323
  50.3 3.6 %collective-permute-start.11 = (s32[2,32]{1,0:T(2,128)S(1)}, s32[2,32]{1,0:T(2,128)S(1)}, u32[]{:S(2)}, u32[]{:S(2)}) collective-permute-start(s32[2,32]{1,0:T(2,128)S(1)} %pad_add_fusion.mine), channel_id=1, source_target_pairs={{0,16},{8,24},{16,0},{24,8},{32,48},{40,56},{48,32},{56,40},{64,80... | collective-permute-start | bytes 776 | tf_op jit(solution)/shard_map/ppermute | solution.py:353
  53.9 1.7 collective-permute-start.13
  56.8 2.6 %shard_map.138.meta = s32[2,4,80]{2,1,0:T(4,128)} custom-call(s32[3]{0:T(128)} %pad_add_fusion.3.at, s32[2,32]{1,0:T(2,128)} %copy-done.18, s32[2,32]{1,0:T(2,128)} %copy-done.21, s32[32]{0:T(128)} %problem_slot.1), custom_call_target="tpu_custom_call" | custom-call | tf_op jit(solution)/shard_map/pallas_call | solution.py:195
  60.7 4.1 %shard_map.137 = (f32[400,768]{1,0:T(8,128)S(1)}, f32[400,128]{1,0:T(8,128)S(1)}) custom-call(s32[2]{0:T(128)S(1)} %pad_add_fusion.2.starts, bf16[400,1024]{1,0:T(8,128)(2,1)} %collective-permute-done.5.refs_0_, bf16[400,1024]{1,0:T(8,128)(2,1)} %collective-permute-done.6.refs_1_, bf16[1,8192]{1,0:T(2,128)(2,1)S(1)} %broadcast_in_dim.59.refs_4_.refs_2_, ...), custom_call_target="tpu_custom_call" | custom-call | flops 1258291200 | bytes 3145728 | tf_op jit(solution)/shard_map/pallas_call | solution.py:126
  68.9 3.1 %collective-permute-done.13.refs_1_ = bf16[400,1024]{1,0:T(8,128)(2,1)} collective-permute-done((bf16[400,1024]{1,0:T(8,128)(2,1)}, bf16[400,1024]{1,0:T(8,128)(2,1)}, u32[]{:S(2)}, u32[]{:S(2)}) %collective-permute-start.13) | collective-permute-done | bytes 819232 | tf_op jit(solution)/shard_map/ppermute | solution.py:323
  74.3 4.3 %shard_map.139.refs_0_ = bf16[400,768]{1,0:T(8,128)(2,1)S(1)} custom-call(s32[2]{0:T(128)S(1)} %pad_add_fusion.4.starts, bf16[400,1024]{1,0:T(8,128)(2,1)} %collective-permute-done.12.refs_0_, bf16[400,1024]{1,0:T(8,128)(2,1)} %collective-permute-done.13.refs_1_, bf16[1,8192]{1,0:T(2,128)(2,1)S(1)} %broadcast_in_dim.59.refs_4_.refs_2_, ...), custom_call_target="tpu_custom_call" | custom-call | flops 1258291200 | bytes 3145728 | tf_op jit(solution)/shard_map/pallas_call | solution.py:126
  79.8 9.8 %shard_map.140 = bf16[400,512]{1,0:T(8,128)(2,1)S(1)} custom-call(s32[2,4,80]{2,1,0:T(4,128)S(1)} %copy-done.16, bf16[400,768]{1,0:T(8,128)(2,1)S(1)} %shard_map.139.refs_0_, bf16[2,1024,128]{2,1,0:T(8,128)(2,1)S(1)} %copy-done.1, bf16[2,1024,128]{2,1,0:T(8,128)(2,1)} %collective-permute-done.3.refs_2_, ...), custom_call_target="tpu_custom_call" | custom-call | flops 1610612736 | bytes 8388608 | tf_op jit(solution)/shard_map/pallas_call | solution.py:270
  89.6 6.4 %collective-permute-done.22.refs_0_ = bf16[400,768]{1,0:T(8,128)(2,1)S(1)} collective-permute-done((bf16[400,768]{1,0:T(8,128)(2,1)S(1)}, bf16[400,768]{1,0:T(8,128)(2,1)S(1)}, u32[]{:S(2)}, u32[]{:S(2)}) %collective-permute-start.22) | collective-permute-done | bytes 614432 | tf_op jit(solution)/shard_map/ppermute | solution.py:407
  96.0 9.8 %shard_map.141 = bf16[400,512]{1,0:T(8,128)(2,1)S(1)} custom-call(s32[2,4,80]{2,1,0:T(4,128)S(1)} %copy-done.16, bf16[400,768]{1,0:T(8,128)(2,1)S(1)} %collective-permute-done.22.refs_0_, bf16[2,1024,128]{2,1,0:T(8,128)(2,1)S(1)} %copy-done.1, bf16[2,1024,128]{2,1,0:T(8,128)(2,1)} %collective-permute-done.3.refs_2_, ...), custom_call_target="tpu_custom_call" | custom-call | flops 1610612736 | bytes 8388608 | tf_op jit(solution)/shard_map/pallas_call | solution.py:270
  105.8 2.4 %collective-permute-start.23 = (bf16[400,512]{1,0:T(8,128)(2,1)S(1)}, bf16[400,512]{1,0:T(8,128)(2,1)S(1)}, u32[]{:S(2)}, u32[]{:S(2)}) collective-permute-start(bf16[400,512]{1,0:T(8,128)(2,1)S(1)} %shard_map.141), channel_id=1, source_target_pairs={{0,16},{8,24},{16,0},{24,8},{32,48},{40,56},{48,32},{56,40},{64,80... | collective-permute-start | bytes 1228808 | tf_op jit(solution)/shard_map/ppermute | solution.py:411
  108.2 10.7 %collective-permute-done.23 = bf16[400,512]{1,0:T(8,128)(2,1)S(1)} collective-permute-done((bf16[400,512]{1,0:T(8,128)(2,1)S(1)}, bf16[400,512]{1,0:T(8,128)(2,1)S(1)}, u32[]{:S(2)}, u32[]{:S(2)}) %collective-permute-start.23) | collective-permute-done | bytes 409632 | tf_op jit(solution)/shard_map/ppermute | solution.py:411
  122.4 1.7 collective-permute-start.29
  129.1 7.0 %collective-permute-done.29 = bf16[400,512]{1,0:T(8,128)(2,1)S(1)} collective-permute-done((bf16[400,512]{1,0:T(8,128)(2,1)S(1)}, bf16[400,512]{1,0:T(8,128)(2,1)S(1)}, u32[]{:S(2)}, u32[]{:S(2)}) %collective-permute-start.29) | collective-permute-done | bytes 409632 | tf_op jit(solution)/shard_map/ppermute | solution.py:323
  136.1 1.8 fusion.5
  138.0 1.8 fusion.3
  140.7 2.1 %collective-permute-start.31 = (bf16[400,1024]{1,0:T(8,128)(2,1)S(1)}, bf16[400,1024]{1,0:T(8,128)(2,1)S(1)}, u32[]{:S(2)}, u32[]{:S(2)}) collective-permute-start(bf16[400,1024]{1,0:T(8,128)(2,1)S(1)} %pad_maximum_fusion.3), channel_id=1, source_target_pairs={{0,6},{1,7},{2,0},{3,1},{4,2},{5,3},{6,4},{7,5},{8,14},{9,15},{10,... | collective-permute-start | bytes 2457608 | tf_op jit(solution)/shard_map/ppermute | solution.py:323
  142.7 2.1 %collective-permute-done.25 = bf16[400,512]{1,0:T(8,128)(2,1)S(1)} collective-permute-done((bf16[400,512]{1,0:T(8,128)(2,1)S(1)}, bf16[400,512]{1,0:T(8,128)(2,1)S(1)}, u32[]{:S(2)}, u32[]{:S(2)}) %collective-permute-start.25) | collective-permute-done | bytes 409632 | tf_op jit(solution)/shard_map/ppermute | solution.py:323
  144.9 1.8 fusion.9
  146.7 1.8 fusion.11
  150.9 3.2 %collective-permute-start.26 = (bf16[400,1024]{1,0:T(8,128)(2,1)}, bf16[400,1024]{1,0:T(8,128)(2,1)}, u32[]{:S(2)}, u32[]{:S(2)}) collective-permute-start(bf16[400,1024]{1,0:T(8,128)(2,1)} %pad_maximum_fusion), channel_id=1, source_target_pairs={{0,2},{1,3},{2,4},{3,5},{4,6},{5,7},{6,0},{7,1},{8,10},{9,11},{10,... | collective-permute-start | bytes 2457608 | tf_op jit(solution)/shard_map/ppermute | solution.py:320
  154.2 7.4 %collective-permute-done.30 = bf16[400,1024]{1,0:T(8,128)(2,1)S(1)} collective-permute-done((bf16[400,1024]{1,0:T(8,128)(2,1)S(1)}, bf16[400,1024]{1,0:T(8,128)(2,1)S(1)}, u32[]{:S(2)}, u32[]{:S(2)}) %collective-permute-start.30) | collective-permute-done | bytes 819232 | tf_op jit(solution)/shard_map/ppermute | solution.py:320
  163.1 2.8 %add_convert_fusion = bf16[400,1024]{1,0:T(8,128)(2,1)} fusion(bf16[400,1024]{1,0:T(8,128)(2,1)S(1)} %collective-permute-done.31, bf16[400,1024]{1,0:T(8,128)(2,1)S(1)} %collective-permute-done.30, bf16[400,512]{1,0:T(8,128)(2,1)S(1)} %broadcast_select_fusion, bf16[512,8192]{1,0:T(8,128)(2,1)} %param.22, s32[]{:T(128)S(6)} %select_n.194), kind=kOutput, calls=%fused_computation | convolution fusion | flops 421478400 | bytes 3915780 | tf_op jit(solution)/shard_map/dot_general | solution.py:35
  167.1 1.9 %fusion.7.term = f32[400,1024]{1,0:T(8,128)S(1)} fusion(bf16[400,512]{1,0:T(8,128)(2,1)S(1)} %broadcast_select_fusion, bf16[512,8192]{1,0:T(8,128)(2,1)} %param.22, s32[]{:T(128)S(6)} %select_n.191), kind=kOutput, calls=%fused_computation.15 | convolution fusion | flops 419430400 | bytes 3096580 | tf_op jit(solution)/shard_map/dot_general | solution.py:35
  169.1 9.4 %collective-permute-done.27.down = bf16[400,1024]{1,0:T(8,128)(2,1)} collective-permute-done((bf16[400,1024]{1,0:T(8,128)(2,1)}, bf16[400,1024]{1,0:T(8,128)(2,1)}, u32[]{:S(2)}, u32[]{:S(2)}) %collective-permute-start.27) | collective-permute-done | bytes 819232 | tf_op jit(solution)/shard_map/ppermute | solution.py:323
  178.5 3.4 %collective-permute-done.32.crossed = bf16[400,1024]{1,0:T(8,128)(2,1)} collective-permute-done((bf16[400,1024]{1,0:T(8,128)(2,1)}, bf16[400,1024]{1,0:T(8,128)(2,1)}, u32[]{:S(2)}, u32[]{:S(2)}) %collective-permute-start.32) | collective-permute-done | bytes 819232 | tf_op jit(solution)/shard_map/ppermute | solution.py:326
  181.8 5.3 %shard_map.142 = bf16[768,1024]{1,0:T(8,128)(2,1)} custom-call(bf16[768,400]{1,0:T(8,128)(2,1)S(1)} %fusion.spread, bf16[768,1024]{1,0:T(8,128)(2,1)S(1)} %bitcast.34, f32[400,1024]{1,0:T(8,128)S(1)} %fusion.7.term, bf16[400,1024]{1,0:T(8,128)(2,1)} %collective-permute-done.26.up, bf16[400,1024]{1,0:T(8,128)(2,1)} %collective-permute-done.27.down, ...), custom_call_target="tpu_custom_call" | custom-call | flops 1258291200 | bytes 6291456 | tf_op jit(solution)/shard_map/pallas_call | solution.py:156
  (143 shorter events, 47.7 us)
Async XLA Ops:
  4.0 20.2 %collective-permute-start = (bf16[400,1024]{1,0:T(8,128)(2,1)S(1)}, bf16[400,1024]{1,0:T(8,128)(2,1)}, u32[]{:S(2)}, u32[]{:S(2)}) collective-permute-start(bf16[400,1024]{1,0:T(8,128)(2,1)S(1)} %convolution_convert_fusion.refs_0_), channel_id=1, source_target_pairs={{0,2},{1,3},{2,4},{3,5},{4,6},{5,7},{6,0},{7,1},{8,10},{9,11},{10,... | collective-permute-start | bytes 2457608 | tf_op jit(solution)/shard_map/ppermute | solution.py:320
  4.6 20.9 %collective-permute-start.1 = (bf16[400,1024]{1,0:T(8,128)(2,1)S(1)}, bf16[400,1024]{1,0:T(8,128)(2,1)S(1)}, u32[]{:S(2)}, u32[]{:S(2)}) collective-permute-start(bf16[400,1024]{1,0:T(8,128)(2,1)S(1)} %convolution_convert_fusion.refs_0_), channel_id=1, source_target_pairs={{0,6},{1,7},{2,0},{3,1},{4,2},{5,3},{6,4},{7,5},{8,14},{9,15},{10,... | collective-permute-start | bytes 2457608 | tf_op jit(solution)/shard_map/ppermute | solution.py:323
  6.1 20.3 %collective-permute-start.2 = (bf16[400,1024]{1,0:T(8,128)(2,1)S(1)}, bf16[400,1024]{1,0:T(8,128)(2,1)}, u32[]{:S(2)}, u32[]{:S(2)}) collective-permute-start(bf16[400,1024]{1,0:T(8,128)(2,1)S(1)} %convolution_convert_fusion.refs_0_), channel_id=1, source_target_pairs={{0,1},{1,0},{2,3},{3,2},{4,5},{5,4},{6,7},{7,6},{8,9},{9,8},{10,11... | collective-permute-start | bytes 2457608 | tf_op jit(solution)/shard_map/ppermute | solution.py:326
  9.0 12.9 %collective-permute-start.3 = (bf16[2,1024,128]{2,1,0:T(8,128)(2,1)S(1)}, bf16[2,1024,128]{2,1,0:T(8,128)(2,1)}, u32[]{:S(2)}, u32[]{:S(2)}) collective-permute-start(bf16[2,1024,128]{2,1,0:T(8,128)(2,1)S(1)} %copy-done.1), channel_id=1, source_target_pairs={{0,32},{8,40},{16,48},{24,56},{32,64},{40,72},{48,80},{56,88},{64,... | collective-permute-start | bytes 1572872 | tf_op jit(solution)/shard_map/ppermute | solution.py:344
  10.5 12.5 %collective-permute-start.4 = (bf16[2,1024,128]{2,1,0:T(8,128)(2,1)S(1)}, bf16[2,1024,128]{2,1,0:T(8,128)(2,1)S(1)}, u32[]{:S(2)}, u32[]{:S(2)}) collective-permute-start(bf16[2,1024,128]{2,1,0:T(8,128)(2,1)S(1)} %copy-done.2), channel_id=1, source_target_pairs={{0,96},{8,104},{16,112},{24,120},{32,0},{40,8},{48,16},{56,24},{64... | collective-permute-start | bytes 1572872 | tf_op jit(solution)/shard_map/ppermute | solution.py:345
  26.4 19.1 %collective-permute-start.5 = (bf16[400,1024]{1,0:T(8,128)(2,1)}, bf16[400,1024]{1,0:T(8,128)(2,1)}, u32[]{:S(2)}, u32[]{:S(2)}) collective-permute-start(bf16[400,1024]{1,0:T(8,128)(2,1)} %collective-permute-done.2.refs_3_), channel_id=1, source_target_pairs={{0,2},{1,3},{2,4},{3,5},{4,6},{5,7},{6,0},{7,1},{8,10},{9,11},{10,... | collective-permute-start | bytes 2457608 | tf_op jit(solution)/shard_map/ppermute | solution.py:320
  27.5 19.9 %collective-permute-start.6 = (bf16[400,1024]{1,0:T(8,128)(2,1)}, bf16[400,1024]{1,0:T(8,128)(2,1)}, u32[]{:S(2)}, u32[]{:S(2)}) collective-permute-start(bf16[400,1024]{1,0:T(8,128)(2,1)} %collective-permute-done.2.refs_3_), channel_id=1, source_target_pairs={{0,6},{1,7},{2,0},{3,1},{4,2},{5,3},{6,4},{7,5},{8,14},{9,15},{10,... | collective-permute-start | bytes 2457608 | tf_op jit(solution)/shard_map/ppermute | solution.py:323
  28.9 12.3 %collective-permute-start.7 = (bf16[2,1024,128]{2,1,0:T(8,128)(2,1)}, bf16[2,1024,128]{2,1,0:T(8,128)(2,1)}, u32[]{:S(2)}, u32[]{:S(2)}) collective-permute-start(bf16[2,1024,128]{2,1,0:T(8,128)(2,1)} %collective-permute-done.3.refs_2_), channel_id=1, source_target_pairs={{0,32},{8,40},{16,48},{24,56},{32,64},{40,72},{48,80},{56,88},{64,... | collective-permute-start | bytes 1572872 | tf_op jit(solution)/shard_map/ppermute | solution.py:344
  30.5 11.9 %collective-permute-start.8 = (bf16[2,1024,128]{2,1,0:T(8,128)(2,1)}, bf16[2,1024,128]{2,1,0:T(8,128)(2,1)}, u32[]{:S(2)}, u32[]{:S(2)}) collective-permute-start(bf16[2,1024,128]{2,1,0:T(8,128)(2,1)} %copy-done.3), channel_id=1, source_target_pairs={{0,96},{8,104},{16,112},{24,120},{32,0},{40,8},{48,16},{56,24},{64... | collective-permute-start | bytes 1572872 | tf_op jit(solution)/shard_map/ppermute | solution.py:345
  47.5 19.8 %collective-permute-start.12 = (bf16[400,1024]{1,0:T(8,128)(2,1)}, bf16[400,1024]{1,0:T(8,128)(2,1)}, u32[]{:S(2)}, u32[]{:S(2)}) collective-permute-start(bf16[400,1024]{1,0:T(8,128)(2,1)} %collective-permute-done.refs_1_), channel_id=1, source_target_pairs={{0,2},{1,3},{2,4},{3,5},{4,6},{5,7},{6,0},{7,1},{8,10},{9,11},{10,... | collective-permute-start | bytes 2457608 | tf_op jit(solution)/shard_map/ppermute | solution.py:320
  48.1 18.5 %collective-permute-start.10 = (bf16[2,1024,128]{2,1,0:T(8,128)(2,1)}, bf16[2,1024,128]{2,1,0:T(8,128)(2,1)}, u32[]{:S(2)}, u32[]{:S(2)}) collective-permute-start(bf16[2,1024,128]{2,1,0:T(8,128)(2,1)} %collective-permute-done.8.refs_11_), channel_id=1, source_target_pairs={{0,96},{8,104},{16,112},{24,120},{32,0},{40,8},{48,16},{56,24},{64... | collective-permute-start | bytes 1572872 | tf_op jit(solution)/shard_map/ppermute | solution.py:345
  48.7 17.9 %collective-permute-start.9 = (bf16[2,1024,128]{2,1,0:T(8,128)(2,1)}, bf16[2,1024,128]{2,1,0:T(8,128)(2,1)}, u32[]{:S(2)}, u32[]{:S(2)}) collective-permute-start(bf16[2,1024,128]{2,1,0:T(8,128)(2,1)} %collective-permute-done.7.refs_3_), channel_id=1, source_target_pairs={{0,32},{8,40},{16,48},{24,56},{32,64},{40,72},{48,80},{56,88},{64,... | collective-permute-start | bytes 1572872 | tf_op jit(solution)/shard_map/ppermute | solution.py:344
  50.3 5.9 %collective-permute-start.11 = (s32[2,32]{1,0:T(2,128)S(1)}, s32[2,32]{1,0:T(2,128)S(1)}, u32[]{:S(2)}, u32[]{:S(2)}) collective-permute-start(s32[2,32]{1,0:T(2,128)S(1)} %pad_add_fusion.mine), channel_id=1, source_target_pairs={{0,16},{8,24},{16,0},{24,8},{32,48},{40,56},{48,32},{56,40},{64,80... | collective-permute-start | bytes 776 | tf_op jit(solution)/shard_map/ppermute | solution.py:353
  53.9 18.0 %collective-permute-start.13 = (bf16[400,1024]{1,0:T(8,128)(2,1)}, bf16[400,1024]{1,0:T(8,128)(2,1)}, u32[]{:S(2)}, u32[]{:S(2)}) collective-permute-start(bf16[400,1024]{1,0:T(8,128)(2,1)} %collective-permute-done.6.refs_1_), channel_id=1, source_target_pairs={{0,6},{1,7},{2,0},{3,1},{4,2},{5,3},{6,4},{7,5},{8,14},{9,15},{10,... | collective-permute-start | bytes 2457608 | tf_op jit(solution)/shard_map/ppermute | solution.py:323
  66.7 5.8 %collective-permute-start.15 = (bf16[2,1024,128]{2,1,0:T(8,128)(2,1)}, bf16[2,1024,128]{2,1,0:T(8,128)(2,1)}, u32[]{:S(2)}, u32[]{:S(2)}) collective-permute-start(bf16[2,1024,128]{2,1,0:T(8,128)(2,1)} %collective-permute-done.3.refs_2_), channel_id=1, source_target_pairs={{0,8},{8,0},{16,24},{24,16},{32,40},{40,32},{48,56},{56,48},{64,72... | collective-permute-start | bytes 1572872 | tf_op jit(solution)/shard_map/ppermute | solution.py:379
  67.2 5.4 %collective-permute-start.16 = (bf16[2,1024,128]{2,1,0:T(8,128)(2,1)}, bf16[2,1024,128]{2,1,0:T(8,128)(2,1)}, u32[]{:S(2)}, u32[]{:S(2)}) collective-permute-start(bf16[2,1024,128]{2,1,0:T(8,128)(2,1)} %collective-permute-done.7.refs_3_), channel_id=1, source_target_pairs={{0,8},{8,0},{16,24},{24,16},{32,40},{40,32},{48,56},{56,48},{64,72... | collective-permute-start | bytes 1572872 | tf_op jit(solution)/shard_map/ppermute | solution.py:379
  67.3 11.3 %collective-permute-start.17 = (bf16[2,1024,128]{2,1,0:T(8,128)(2,1)}, bf16[2,1024,128]{2,1,0:T(8,128)(2,1)S(1)}, u32[]{:S(2)}, u32[]{:S(2)}) collective-permute-start(bf16[2,1024,128]{2,1,0:T(8,128)(2,1)} %collective-permute-done.9.refs_4_), channel_id=1, source_target_pairs={{0,8},{8,0},{16,24},{24,16},{32,40},{40,32},{48,56},{56,48},{64,72... | collective-permute-start | bytes 1572872 | tf_op jit(solution)/shard_map/ppermute | solution.py:379
  71.9 7.8 %collective-permute-start.18 = (bf16[2,1024,128]{2,1,0:T(8,128)(2,1)S(1)}, bf16[2,1024,128]{2,1,0:T(8,128)(2,1)S(1)}, u32[]{:S(2)}, u32[]{:S(2)}) collective-permute-start(bf16[2,1024,128]{2,1,0:T(8,128)(2,1)S(1)} %copy-done.2), channel_id=1, source_target_pairs={{0,8},{8,0},{16,24},{24,16},{32,40},{40,32},{48,56},{56,48},{64,72... | collective-permute-start | bytes 1572872 | tf_op jit(solution)/shard_map/ppermute | solution.py:379
  72.0 7.8 %collective-permute-start.19 = (bf16[2,1024,128]{2,1,0:T(8,128)(2,1)S(1)}, bf16[2,1024,128]{2,1,0:T(8,128)(2,1)S(1)}, u32[]{:S(2)}, u32[]{:S(2)}) collective-permute-start(bf16[2,1024,128]{2,1,0:T(8,128)(2,1)S(1)} %copy-done.4), channel_id=1, source_target_pairs={{0,8},{8,0},{16,24},{24,16},{32,40},{40,32},{48,56},{56,48},{64,72... | collective-permute-start | bytes 1572872 | tf_op jit(solution)/shard_map/ppermute | solution.py:379
  72.5 7.3 %collective-permute-start.20 = (bf16[2,1024,128]{2,1,0:T(8,128)(2,1)}, bf16[2,1024,128]{2,1,0:T(8,128)(2,1)S(1)}, u32[]{:S(2)}, u32[]{:S(2)}) collective-permute-start(bf16[2,1024,128]{2,1,0:T(8,128)(2,1)} %collective-permute-done.8.refs_11_), channel_id=1, source_target_pairs={{0,8},{8,0},{16,24},{24,16},{32,40},{40,32},{48,56},{56,48},{64,72... | collective-permute-start | bytes 1572872 | tf_op jit(solution)/shard_map/ppermute | solution.py:379
  72.6 7.2 %collective-permute-start.21 = (bf16[2,1024,128]{2,1,0:T(8,128)(2,1)}, bf16[2,1024,128]{2,1,0:T(8,128)(2,1)S(1)}, u32[]{:S(2)}, u32[]{:S(2)}) collective-permute-start(bf16[2,1024,128]{2,1,0:T(8,128)(2,1)} %collective-permute-done.10.refs_12_), channel_id=1, source_target_pairs={{0,8},{8,0},{16,24},{24,16},{32,40},{40,32},{48,56},{56,48},{64,72... | collective-permute-start | bytes 1572872 | tf_op jit(solution)/shard_map/ppermute | solution.py:379
  78.6 17.4 %collective-permute-start.22 = (bf16[400,768]{1,0:T(8,128)(2,1)S(1)}, bf16[400,768]{1,0:T(8,128)(2,1)S(1)}, u32[]{:S(2)}, u32[]{:S(2)}) collective-permute-start(bf16[400,768]{1,0:T(8,128)(2,1)S(1)} %shard_map.139.refs_0_), channel_id=1, source_target_pairs={{0,16},{8,24},{16,0},{24,8},{32,48},{40,56},{48,32},{56,40},{64,80... | collective-permute-start | bytes 1843208 | tf_op jit(solution)/shard_map/ppermute | solution.py:407
  105.8 13.1 %collective-permute-start.23 = (bf16[400,512]{1,0:T(8,128)(2,1)S(1)}, bf16[400,512]{1,0:T(8,128)(2,1)S(1)}, u32[]{:S(2)}, u32[]{:S(2)}) collective-permute-start(bf16[400,512]{1,0:T(8,128)(2,1)S(1)} %shard_map.141), channel_id=1, source_target_pairs={{0,16},{8,24},{16,0},{24,8},{32,48},{40,56},{48,32},{56,40},{64,80... | collective-permute-start | bytes 1228808 | tf_op jit(solution)/shard_map/ppermute | solution.py:411
  120.5 15.6 %collective-permute-start.28 = (bf16[400,512]{1,0:T(8,128)(2,1)S(1)}, bf16[400,512]{1,0:T(8,128)(2,1)S(1)}, u32[]{:S(2)}, u32[]{:S(2)}) collective-permute-start(bf16[400,512]{1,0:T(8,128)(2,1)S(1)} %convolution_convert_fusion.4), channel_id=1, source_target_pairs={{0,2},{1,3},{2,4},{3,5},{4,6},{5,7},{6,0},{7,1},{8,10},{9,11},{10,... | collective-permute-start | bytes 1228808 | tf_op jit(solution)/shard_map/ppermute | solution.py:320
  122.4 13.7 %collective-permute-start.29 = (bf16[400,512]{1,0:T(8,128)(2,1)S(1)}, bf16[400,512]{1,0:T(8,128)(2,1)S(1)}, u32[]{:S(2)}, u32[]{:S(2)}) collective-permute-start(bf16[400,512]{1,0:T(8,128)(2,1)S(1)} %convolution_convert_fusion.3), channel_id=1, source_target_pairs={{0,6},{1,7},{2,0},{3,1},{4,2},{5,3},{6,4},{7,5},{8,14},{9,15},{10,... | collective-permute-start | bytes 1228808 | tf_op jit(solution)/shard_map/ppermute | solution.py:323
  125.5 19.3 %collective-permute-start.24 = (bf16[400,512]{1,0:T(8,128)(2,1)S(1)}, bf16[400,512]{1,0:T(8,128)(2,1)S(1)}, u32[]{:S(2)}, u32[]{:S(2)}) collective-permute-start(bf16[400,512]{1,0:T(8,128)(2,1)S(1)} %convolution_convert_fusion.2), channel_id=1, source_target_pairs={{0,2},{1,3},{2,4},{3,5},{4,6},{5,7},{6,0},{7,1},{8,10},{9,11},{10,... | collective-permute-start | bytes 1228808 | tf_op jit(solution)/shard_map/ppermute | solution.py:320
  128.6 16.2 %collective-permute-start.25 = (bf16[400,512]{1,0:T(8,128)(2,1)S(1)}, bf16[400,512]{1,0:T(8,128)(2,1)S(1)}, u32[]{:S(2)}, u32[]{:S(2)}) collective-permute-start(bf16[400,512]{1,0:T(8,128)(2,1)S(1)} %convolution_convert_fusion.1), channel_id=1, source_target_pairs={{0,6},{1,7},{2,0},{3,1},{4,2},{5,3},{6,4},{7,5},{8,14},{9,15},{10,... | collective-permute-start | bytes 1228808 | tf_op jit(solution)/shard_map/ppermute | solution.py:323
  140.1 21.5 %collective-permute-start.30 = (bf16[400,1024]{1,0:T(8,128)(2,1)S(1)}, bf16[400,1024]{1,0:T(8,128)(2,1)S(1)}, u32[]{:S(2)}, u32[]{:S(2)}) collective-permute-start(bf16[400,1024]{1,0:T(8,128)(2,1)S(1)} %pad_maximum_fusion.2), channel_id=1, source_target_pairs={{0,2},{1,3},{2,4},{3,5},{4,6},{5,7},{6,0},{7,1},{8,10},{9,11},{10,... | collective-permute-start | bytes 2457608 | tf_op jit(solution)/shard_map/ppermute | solution.py:320
  140.7 22.5 %collective-permute-start.31 = (bf16[400,1024]{1,0:T(8,128)(2,1)S(1)}, bf16[400,1024]{1,0:T(8,128)(2,1)S(1)}, u32[]{:S(2)}, u32[]{:S(2)}) collective-permute-start(bf16[400,1024]{1,0:T(8,128)(2,1)S(1)} %pad_maximum_fusion.3), channel_id=1, source_target_pairs={{0,6},{1,7},{2,0},{3,1},{4,2},{5,3},{6,4},{7,5},{8,14},{9,15},{10,... | collective-permute-start | bytes 2457608 | tf_op jit(solution)/shard_map/ppermute | solution.py:323
  149.8 28.7 %collective-permute-start.27 = (bf16[400,1024]{1,0:T(8,128)(2,1)}, bf16[400,1024]{1,0:T(8,128)(2,1)}, u32[]{:S(2)}, u32[]{:S(2)}) collective-permute-start(bf16[400,1024]{1,0:T(8,128)(2,1)} %pad_maximum_fusion.1), channel_id=1, source_target_pairs={{0,6},{1,7},{2,0},{3,1},{4,2},{5,3},{6,4},{7,5},{8,14},{9,15},{10,... | collective-permute-start | bytes 2457608 | tf_op jit(solution)/shard_map/ppermute | solution.py:323
  150.9 27.5 %collective-permute-start.26 = (bf16[400,1024]{1,0:T(8,128)(2,1)}, bf16[400,1024]{1,0:T(8,128)(2,1)}, u32[]{:S(2)}, u32[]{:S(2)}) collective-permute-start(bf16[400,1024]{1,0:T(8,128)(2,1)} %pad_maximum_fusion), channel_id=1, source_target_pairs={{0,2},{1,3},{2,4},{3,5},{4,6},{5,7},{6,0},{7,1},{8,10},{9,11},{10,... | collective-permute-start | bytes 2457608 | tf_op jit(solution)/shard_map/ppermute | solution.py:320
  165.9 15.9 %collective-permute-start.32 = (bf16[400,1024]{1,0:T(8,128)(2,1)}, bf16[400,1024]{1,0:T(8,128)(2,1)}, u32[]{:S(2)}, u32[]{:S(2)}) collective-permute-start(bf16[400,1024]{1,0:T(8,128)(2,1)} %add_convert_fusion), channel_id=1, source_target_pairs={{0,1},{1,0},{2,3},{3,2},{4,5},{5,4},{6,7},{7,6},{8,9},{9,8},{10,11... | collective-permute-start | bytes 2457608 | tf_op jit(solution)/shard_map/ppermute | solution.py:326
  (27 other events, 248.6 us)

commit v4 on v3

--- a/solution.py
+++ b/solution.py
@@ -352,9 +352,6 @@
     o_low, o_high = pass_up(across), pass_down(across)
     other_table = lax.ppermute(late_table, "cand", ACROSS_Z_HI)
     pass_prefixes()
-    lists = candidate_lists(
-        jnp.stack([y_at, half_at, core_at]), table, other_table, problem_slot
-    )
     add_up = functools.partial(
         project_parts, gain=norm_gain[None, :], w_query=w_query, w_key=w_key, w_value=w_value
     )
@@ -366,8 +363,11 @@
         None,
         None,
     )
-    o_low, o_high, low2, key_parts[2], value_parts[2], sums = tie(
-        (o_low, o_high, low, key_parts[2], value_parts[2], sums), block
+    o_low, o_high, low2, key_parts[2], value_parts[2], sums, other_table = tie(
+        (o_low, o_high, low, key_parts[2], value_parts[2], sums, other_table), block
+    )
+    lists = candidate_lists(
+        jnp.stack([y_at, half_at, core_at]), table, other_table, problem_slot
     )
     fars = pass_up(low2), pass_down(o_high)
     pass_prefixes()

time: 189 us -> 187 us (0.989)
  the two profiles are of different devices: /device:TPU:14 before, /device:TPU:30 now
where the time goes in v4:
time: 187 us; the launch traced here: 185 us
  waiting for transfers between devices  65.7 us (35%)
  Pallas kernels  42.3 us (23%)
  starting transfers between devices  38.6 us (21%)
  matrix products  20.3 us (11%)
  local copies, waits for them, and re-layouts  10.9 us (6%)
  other arithmetic  6.61 us (4%)
    ppermute x7, waiting for transfers between devices, pass_down(): return lax.ppermute(part, 'tp', along_x(-1))  25.5 us
    dot_general x12, matrix products, dot(): return jnp.dot(a, b, preferred_element_type=f32)  20.3 us
    pallas_call x2, Pallas kernels, attention(): pl.pallas_call(functools.partial(attention_kernel, which, bounds, len(row...  19.6 us
    pallas_call x3, Pallas kernels, project_parts(): pl.pallas_call(functools.partial(project_kernel, len(parts), plan, sums i...  14.8 us
    ppermute x3, waiting for transfers between devices, pass_prefixes(): key_parts.append(lax.ppermute(key_parts[-1], 'cand', along_y(1)))  10.9 us
    ppermute x7, waiting for transfers between devices, pass_up(): return lax.ppermute(part, 'tp', along_x(1))  10.4 us
    unnamed x52, local copies, waits for them, and re-layouts  10.3 us
    ppermute x7, starting transfers between devices, pass_down(): return lax.ppermute(part, 'tp', along_x(-1))  9.87 us
  transfers between devices with their start and end apart: 33, of which 16 were waited for; matrix products, arithmetic and copies ran while one was open for 12% of the time, Pallas kernels for 15%

profile of v4, /device:TPU:30, one launch (start us, length us, event | category | flops | bytes accessed | tf_op | source)
XLA Modules:
  0.0 185.1 jit_solution(2189496102408033407)
XLA Ops:
  1.7 2.4 %convolution_convert_fusion.refs_0_ = bf16[400,1024]{1,0:T(8,128)(2,1)S(1)} fusion(bf16[768,1024]{1,0:T(8,128)(2,1)} %bitcast.33, s32[768]{0:T(1024)S(1)} %select_n.162), kind=kOutput, calls=%fused_computation.3 | convolution fusion | flops 629862400 | bytes 2395136 | tf_op jit(solution)/shard_map/dot_general | solution.py:35
  6.1 1.9 %collective-permute-start.2 = (bf16[400,1024]{1,0:T(8,128)(2,1)S(1)}, bf16[400,1024]{1,0:T(8,128)(2,1)}, u32[]{:S(2)}, u32[]{:S(2)}) collective-permute-start(bf16[400,1024]{1,0:T(8,128)(2,1)S(1)} %convolution_convert_fusion.refs_0_), channel_id=1, source_target_pairs={{0,1},{1,0},{2,3},{3,2},{4,5},{5,4},{6,7},{7,6},{8,9},{9,8},{10,11... | collective-permute-start | bytes 2457608 | tf_op jit(solution)/shard_map/ppermute | solution.py:326
  11.0 10.9 %collective-permute-done.3.refs_2_ = bf16[2,1024,128]{2,1,0:T(8,128)(2,1)} collective-permute-done((bf16[2,1024,128]{2,1,0:T(8,128)(2,1)S(1)}, bf16[2,1024,128]{2,1,0:T(8,128)(2,1)}, u32[]{:S(2)}, u32[]{:S(2)}) %collective-permute-start.3) | collective-permute-done | bytes 524320 | tf_op jit(solution)/shard_map/ppermute | solution.py:344
  29.0 1.9 %collective-permute-start.8 = (bf16[2,1024,128]{2,1,0:T(8,128)(2,1)}, bf16[2,1024,128]{2,1,0:T(8,128)(2,1)}, u32[]{:S(2)}, u32[]{:S(2)}) collective-permute-start(bf16[2,1024,128]{2,1,0:T(8,128)(2,1)} %copy-done.3), channel_id=1, source_target_pairs={{0,96},{8,104},{16,112},{24,120},{32,0},{40,8},{48,16},{56,24},{64... | collective-permute-start | bytes 1572872 | tf_op jit(solution)/shard_map/ppermute | solution.py:345
  31.4 3.9 %collective-permute-start.9 = (s32[2,32]{1,0:T(2,128)S(1)}, s32[2,32]{1,0:T(2,128)S(1)}, u32[]{:S(2)}, u32[]{:S(2)}) collective-permute-start(s32[2,32]{1,0:T(2,128)S(1)} %pad_add_fusion.mine), channel_id=1, source_target_pairs={{0,16},{8,24},{16,0},{24,8},{32,48},{40,56},{48,32},{56,40},{64,80... | collective-permute-start | bytes 776 | tf_op jit(solution)/shard_map/ppermute | solution.py:353
  37.6 6.3 %shard_map.136 = (f32[400,768]{1,0:T(8,128)S(1)}, f32[400,128]{1,0:T(8,128)S(1)}) custom-call(s32[4]{0:T(128)S(1)} %pad_add_fusion.1.starts, bf16[400,1024]{1,0:T(8,128)(2,1)S(1)} %copy-done.11, bf16[400,1024]{1,0:T(8,128)(2,1)} %collective-permute-done.refs_1_, bf16[400,1024]{1,0:T(8,128)(2,1)S(1)} %copy-done.13, ...), custom_call_target="tpu_custom_call" | custom-call | flops 2516582400 | bytes 6291456 | tf_op jit(solution)/shard_map/pallas_call | solution.py:126
  45.5 1.9 %collective-permute-done.6.refs_1_ = bf16[400,1024]{1,0:T(8,128)(2,1)} collective-permute-done((bf16[400,1024]{1,0:T(8,128)(2,1)}, bf16[400,1024]{1,0:T(8,128)(2,1)}, u32[]{:S(2)}, u32[]{:S(2)}) %collective-permute-start.6) | collective-permute-done | bytes 819232 | tf_op jit(solution)/shard_map/ppermute | solution.py:323
  52.6 2.6 %shard_map.138.meta = s32[2,4,80]{2,1,0:T(4,128)} custom-call(s32[3]{0:T(128)} %pad_add_fusion.3.at, s32[2,32]{1,0:T(2,128)} %copy-done.18, s32[2,32]{1,0:T(2,128)} %copy-done.21, s32[32]{0:T(128)} %problem_slot.1), custom_call_target="tpu_custom_call" | custom-call | tf_op jit(solution)/shard_map/pallas_call | solution.py:195
  56.6 4.1 %shard_map.137 = (f32[400,768]{1,0:T(8,128)S(1)}, f32[400,128]{1,0:T(8,128)S(1)}) custom-call(s32[2]{0:T(128)S(1)} %pad_add_fusion.2.starts, bf16[400,1024]{1,0:T(8,128)(2,1)} %collective-permute-done.5.refs_0_, bf16[400,1024]{1,0:T(8,128)(2,1)} %collective-permute-done.6.refs_1_, bf16[1,8192]{1,0:T(2,128)(2,1)S(1)} %broadcast_in_dim.59.refs_4_.refs_2_, ...), custom_call_target="tpu_custom_call" | custom-call | flops 1258291200 | bytes 3145728 | tf_op jit(solution)/shard_map/pallas_call | solution.py:126
  63.1 2.1 %collective-permute-done.12.refs_0_ = bf16[400,1024]{1,0:T(8,128)(2,1)} collective-permute-done((bf16[400,1024]{1,0:T(8,128)(2,1)}, bf16[400,1024]{1,0:T(8,128)(2,1)}, u32[]{:S(2)}, u32[]{:S(2)}) %collective-permute-start.12) | collective-permute-done | bytes 819232 | tf_op jit(solution)/shard_map/ppermute | solution.py:320
  66.3 2.4 %collective-permute-done.13.refs_1_ = bf16[400,1024]{1,0:T(8,128)(2,1)} collective-permute-done((bf16[400,1024]{1,0:T(8,128)(2,1)}, bf16[400,1024]{1,0:T(8,128)(2,1)}, u32[]{:S(2)}, u32[]{:S(2)}) %collective-permute-start.13) | collective-permute-done | bytes 819232 | tf_op jit(solution)/shard_map/ppermute | solution.py:323
  71.1 4.3 %shard_map.139.refs_0_ = bf16[400,768]{1,0:T(8,128)(2,1)S(1)} custom-call(s32[2]{0:T(128)S(1)} %pad_add_fusion.4.starts, bf16[400,1024]{1,0:T(8,128)(2,1)} %collective-permute-done.12.refs_0_, bf16[400,1024]{1,0:T(8,128)(2,1)} %collective-permute-done.13.refs_1_, bf16[1,8192]{1,0:T(2,128)(2,1)S(1)} %broadcast_in_dim.59.refs_4_.refs_2_, ...), custom_call_target="tpu_custom_call" | custom-call | flops 1258291200 | bytes 3145728 | tf_op jit(solution)/shard_map/pallas_call | solution.py:126
  75.4 3.5 %collective-permute-start.22 = (bf16[400,768]{1,0:T(8,128)(2,1)S(1)}, bf16[400,768]{1,0:T(8,128)(2,1)S(1)}, u32[]{:S(2)}, u32[]{:S(2)}) collective-permute-start(bf16[400,768]{1,0:T(8,128)(2,1)S(1)} %shard_map.139.refs_0_), channel_id=1, source_target_pairs={{0,16},{8,24},{16,0},{24,8},{32,48},{40,56},{48,32},{56,40},{64,80... | collective-permute-start | bytes 1843208 | tf_op jit(solution)/shard_map/ppermute | solution.py:407
  79.0 9.8 %shard_map.140 = bf16[400,512]{1,0:T(8,128)(2,1)S(1)} custom-call(s32[2,4,80]{2,1,0:T(4,128)S(1)} %copy-done.16, bf16[400,768]{1,0:T(8,128)(2,1)S(1)} %shard_map.139.refs_0_, bf16[2,1024,128]{2,1,0:T(8,128)(2,1)S(1)} %copy-done.1, bf16[2,1024,128]{2,1,0:T(8,128)(2,1)} %collective-permute-done.3.refs_2_, ...), custom_call_target="tpu_custom_call" | custom-call | flops 1610612736 | bytes 8388608 | tf_op jit(solution)/shard_map/pallas_call | solution.py:270
  88.8 4.3 %collective-permute-done.22.refs_0_ = bf16[400,768]{1,0:T(8,128)(2,1)S(1)} collective-permute-done((bf16[400,768]{1,0:T(8,128)(2,1)S(1)}, bf16[400,768]{1,0:T(8,128)(2,1)S(1)}, u32[]{:S(2)}, u32[]{:S(2)}) %collective-permute-start.22) | collective-permute-done | bytes 614432 | tf_op jit(solution)/shard_map/ppermute | solution.py:407
  93.0 9.8 %shard_map.141 = bf16[400,512]{1,0:T(8,128)(2,1)S(1)} custom-call(s32[2,4,80]{2,1,0:T(4,128)S(1)} %copy-done.16, bf16[400,768]{1,0:T(8,128)(2,1)S(1)} %collective-permute-done.22.refs_0_, bf16[2,1024,128]{2,1,0:T(8,128)(2,1)S(1)} %copy-done.1, bf16[2,1024,128]{2,1,0:T(8,128)(2,1)} %collective-permute-done.3.refs_2_, ...), custom_call_target="tpu_custom_call" | custom-call | flops 1610612736 | bytes 8388608 | tf_op jit(solution)/shard_map/pallas_call | solution.py:270
  102.9 4.2 %collective-permute-start.23 = (bf16[400,512]{1,0:T(8,128)(2,1)S(1)}, bf16[400,512]{1,0:T(8,128)(2,1)S(1)}, u32[]{:S(2)}, u32[]{:S(2)}) collective-permute-start(bf16[400,512]{1,0:T(8,128)(2,1)S(1)} %shard_map.141), channel_id=1, source_target_pairs={{0,16},{8,24},{16,0},{24,8},{32,48},{40,56},{48,32},{56,40},{64,80... | collective-permute-start | bytes 1228808 | tf_op jit(solution)/shard_map/ppermute | solution.py:411
  107.1 9.8 %collective-permute-done.23 = bf16[400,512]{1,0:T(8,128)(2,1)S(1)} collective-permute-done((bf16[400,512]{1,0:T(8,128)(2,1)S(1)}, bf16[400,512]{1,0:T(8,128)(2,1)S(1)}, u32[]{:S(2)}, u32[]{:S(2)}) %collective-permute-start.23) | collective-permute-done | bytes 409632 | tf_op jit(solution)/shard_map/ppermute | solution.py:411
  119.9 2.1 %collective-permute-start.29 = (bf16[400,512]{1,0:T(8,128)(2,1)S(1)}, bf16[400,512]{1,0:T(8,128)(2,1)S(1)}, u32[]{:S(2)}, u32[]{:S(2)}) collective-permute-start(bf16[400,512]{1,0:T(8,128)(2,1)S(1)} %convolution_convert_fusion.3), channel_id=1, source_target_pairs={{0,6},{1,7},{2,0},{3,1},{4,2},{5,3},{6,4},{7,5},{8,14},{9,15},{10,... | collective-permute-start | bytes 1228808 | tf_op jit(solution)/shard_map/ppermute | solution.py:323
  127.0 6.6 %collective-permute-done.29 = bf16[400,512]{1,0:T(8,128)(2,1)S(1)} collective-permute-done((bf16[400,512]{1,0:T(8,128)(2,1)S(1)}, bf16[400,512]{1,0:T(8,128)(2,1)S(1)}, u32[]{:S(2)}, u32[]{:S(2)}) %collective-permute-start.29) | collective-permute-done | bytes 409632 | tf_op jit(solution)/shard_map/ppermute | solution.py:323
  133.6 1.8 fusion.5
  135.5 1.8 fusion.3
  138.2 2.1 %collective-permute-start.31 = (bf16[400,1024]{1,0:T(8,128)(2,1)S(1)}, bf16[400,1024]{1,0:T(8,128)(2,1)S(1)}, u32[]{:S(2)}, u32[]{:S(2)}) collective-permute-start(bf16[400,1024]{1,0:T(8,128)(2,1)S(1)} %pad_maximum_fusion.3), channel_id=1, source_target_pairs={{0,6},{1,7},{2,0},{3,1},{4,2},{5,3},{6,4},{7,5},{8,14},{9,15},{10,... | collective-permute-start | bytes 2457608 | tf_op jit(solution)/shard_map/ppermute | solution.py:323
  140.2 2.1 %collective-permute-done.25 = bf16[400,512]{1,0:T(8,128)(2,1)S(1)} collective-permute-done((bf16[400,512]{1,0:T(8,128)(2,1)S(1)}, bf16[400,512]{1,0:T(8,128)(2,1)S(1)}, u32[]{:S(2)}, u32[]{:S(2)}) %collective-permute-start.25) | collective-permute-done | bytes 409632 | tf_op jit(solution)/shard_map/ppermute | solution.py:323
  144.2 1.8 fusion.11
  149.1 2.6 %collective-permute-start.26 = (bf16[400,1024]{1,0:T(8,128)(2,1)}, bf16[400,1024]{1,0:T(8,128)(2,1)}, u32[]{:S(2)}, u32[]{:S(2)}) collective-permute-start(bf16[400,1024]{1,0:T(8,128)(2,1)} %pad_maximum_fusion), channel_id=1, source_target_pairs={{0,2},{1,3},{2,4},{3,5},{4,6},{5,7},{6,0},{7,1},{8,10},{9,11},{10,... | collective-permute-start | bytes 2457608 | tf_op jit(solution)/shard_map/ppermute | solution.py:320
  151.7 7.4 %collective-permute-done.30 = bf16[400,1024]{1,0:T(8,128)(2,1)S(1)} collective-permute-done((bf16[400,1024]{1,0:T(8,128)(2,1)S(1)}, bf16[400,1024]{1,0:T(8,128)(2,1)S(1)}, u32[]{:S(2)}, u32[]{:S(2)}) %collective-permute-start.30) | collective-permute-done | bytes 819232 | tf_op jit(solution)/shard_map/ppermute | solution.py:320
  160.6 2.8 %add_convert_fusion = bf16[400,1024]{1,0:T(8,128)(2,1)} fusion(bf16[400,1024]{1,0:T(8,128)(2,1)S(1)} %collective-permute-done.31, bf16[400,1024]{1,0:T(8,128)(2,1)S(1)} %collective-permute-done.30, bf16[400,512]{1,0:T(8,128)(2,1)S(1)} %broadcast_select_fusion, bf16[512,8192]{1,0:T(8,128)(2,1)} %param.22, s32[]{:T(128)S(6)} %select_n.194), kind=kOutput, calls=%fused_computation | convolution fusion | flops 421478400 | bytes 3915780 | tf_op jit(solution)/shard_map/dot_general | solution.py:35
  164.6 1.9 %fusion.7.term = f32[400,1024]{1,0:T(8,128)S(1)} fusion(bf16[400,512]{1,0:T(8,128)(2,1)S(1)} %broadcast_select_fusion, bf16[512,8192]{1,0:T(8,128)(2,1)} %param.22, s32[]{:T(128)S(6)} %select_n.191), kind=kOutput, calls=%fused_computation.15 | convolution fusion | flops 419430400 | bytes 3096580 | tf_op jit(solution)/shard_map/dot_general | solution.py:35
  166.6 9.6 %collective-permute-done.27.down = bf16[400,1024]{1,0:T(8,128)(2,1)} collective-permute-done((bf16[400,1024]{1,0:T(8,128)(2,1)}, bf16[400,1024]{1,0:T(8,128)(2,1)}, u32[]{:S(2)}, u32[]{:S(2)}) %collective-permute-start.27) | collective-permute-done | bytes 819232 | tf_op jit(solution)/shard_map/ppermute | solution.py:323
  176.2 3.6 %collective-permute-done.32.crossed = bf16[400,1024]{1,0:T(8,128)(2,1)} collective-permute-done((bf16[400,1024]{1,0:T(8,128)(2,1)}, bf16[400,1024]{1,0:T(8,128)(2,1)}, u32[]{:S(2)}, u32[]{:S(2)}) %collective-permute-start.32) | collective-permute-done | bytes 819232 | tf_op jit(solution)/shard_map/ppermute | solution.py:326
  179.8 5.3 %shard_map.142 = bf16[768,1024]{1,0:T(8,128)(2,1)} custom-call(bf16[768,400]{1,0:T(8,128)(2,1)S(1)} %fusion.spread, bf16[768,1024]{1,0:T(8,128)(2,1)S(1)} %bitcast.34, f32[400,1024]{1,0:T(8,128)S(1)} %fusion.7.term, bf16[400,1024]{1,0:T(8,128)(2,1)} %collective-permute-done.26.up, bf16[400,1024]{1,0:T(8,128)(2,1)} %collective-permute-done.27.down, ...), custom_call_target="tpu_custom_call" | custom-call | flops 1258291200 | bytes 6291456 | tf_op jit(solution)/shard_map/pallas_call | solution.py:156
  (143 shorter events, 46.6 us)
Async XLA Ops:
  4.0 20.2 %collective-permute-start = (bf16[400,1024]{1,0:T(8,128)(2,1)S(1)}, bf16[400,1024]{1,0:T(8,128)(2,1)}, u32[]{:S(2)}, u32[]{:S(2)}) collective-permute-start(bf16[400,1024]{1,0:T(8,128)(2,1)S(1)} %convolution_convert_fusion.refs_0_), channel_id=1, source_target_pairs={{0,2},{1,3},{2,4},{3,5},{4,6},{5,7},{6,0},{7,1},{8,10},{9,11},{10,... | collective-permute-start | bytes 2457608 | tf_op jit(solution)/shard_map/ppermute | solution.py:320
  4.6 20.9 %collective-permute-start.1 = (bf16[400,1024]{1,0:T(8,128)(2,1)S(1)}, bf16[400,1024]{1,0:T(8,128)(2,1)S(1)}, u32[]{:S(2)}, u32[]{:S(2)}) collective-permute-start(bf16[400,1024]{1,0:T(8,128)(2,1)S(1)} %convolution_convert_fusion.refs_0_), channel_id=1, source_target_pairs={{0,6},{1,7},{2,0},{3,1},{4,2},{5,3},{6,4},{7,5},{8,14},{9,15},{10,... | collective-permute-start | bytes 2457608 | tf_op jit(solution)/shard_map/ppermute | solution.py:323
  6.1 20.3 %collective-permute-start.2 = (bf16[400,1024]{1,0:T(8,128)(2,1)S(1)}, bf16[400,1024]{1,0:T(8,128)(2,1)}, u32[]{:S(2)}, u32[]{:S(2)}) collective-permute-start(bf16[400,1024]{1,0:T(8,128)(2,1)S(1)} %convolution_convert_fusion.refs_0_), channel_id=1, source_target_pairs={{0,1},{1,0},{2,3},{3,2},{4,5},{5,4},{6,7},{7,6},{8,9},{9,8},{10,11... | collective-permute-start | bytes 2457608 | tf_op jit(solution)/shard_map/ppermute | solution.py:326
  9.0 12.9 %collective-permute-start.3 = (bf16[2,1024,128]{2,1,0:T(8,128)(2,1)S(1)}, bf16[2,1024,128]{2,1,0:T(8,128)(2,1)}, u32[]{:S(2)}, u32[]{:S(2)}) collective-permute-start(bf16[2,1024,128]{2,1,0:T(8,128)(2,1)S(1)} %copy-done.1), channel_id=1, source_target_pairs={{0,32},{8,40},{16,48},{24,56},{32,64},{40,72},{48,80},{56,88},{64,... | collective-permute-start | bytes 1572872 | tf_op jit(solution)/shard_map/ppermute | solution.py:344
  9.2 13.9 %collective-permute-start.4 = (bf16[2,1024,128]{2,1,0:T(8,128)(2,1)S(1)}, bf16[2,1024,128]{2,1,0:T(8,128)(2,1)S(1)}, u32[]{:S(2)}, u32[]{:S(2)}) collective-permute-start(bf16[2,1024,128]{2,1,0:T(8,128)(2,1)S(1)} %copy-done.2), channel_id=1, source_target_pairs={{0,96},{8,104},{16,112},{24,120},{32,0},{40,8},{48,16},{56,24},{64... | collective-permute-start | bytes 1572872 | tf_op jit(solution)/shard_map/ppermute | solution.py:345
  26.4 19.1 %collective-permute-start.5 = (bf16[400,1024]{1,0:T(8,128)(2,1)}, bf16[400,1024]{1,0:T(8,128)(2,1)}, u32[]{:S(2)}, u32[]{:S(2)}) collective-permute-start(bf16[400,1024]{1,0:T(8,128)(2,1)} %collective-permute-done.2.refs_3_), channel_id=1, source_target_pairs={{0,2},{1,3},{2,4},{3,5},{4,6},{5,7},{6,0},{7,1},{8,10},{9,11},{10,... | collective-permute-start | bytes 2457608 | tf_op jit(solution)/shard_map/ppermute | solution.py:320
  27.5 19.9 %collective-permute-start.6 = (bf16[400,1024]{1,0:T(8,128)(2,1)}, bf16[400,1024]{1,0:T(8,128)(2,1)}, u32[]{:S(2)}, u32[]{:S(2)}) collective-permute-start(bf16[400,1024]{1,0:T(8,128)(2,1)} %collective-permute-done.2.refs_3_), channel_id=1, source_target_pairs={{0,6},{1,7},{2,0},{3,1},{4,2},{5,3},{6,4},{7,5},{8,14},{9,15},{10,... | collective-permute-start | bytes 2457608 | tf_op jit(solution)/shard_map/ppermute | solution.py:323
  28.9 16.1 %collective-permute-start.7 = (bf16[2,1024,128]{2,1,0:T(8,128)(2,1)}, bf16[2,1024,128]{2,1,0:T(8,128)(2,1)}, u32[]{:S(2)}, u32[]{:S(2)}) collective-permute-start(bf16[2,1024,128]{2,1,0:T(8,128)(2,1)} %collective-permute-done.3.refs_2_), channel_id=1, source_target_pairs={{0,32},{8,40},{16,48},{24,56},{32,64},{40,72},{48,80},{56,88},{64,... | collective-permute-start | bytes 1572872 | tf_op jit(solution)/shard_map/ppermute | solution.py:344
  29.0 15.9 %collective-permute-start.8 = (bf16[2,1024,128]{2,1,0:T(8,128)(2,1)}, bf16[2,1024,128]{2,1,0:T(8,128)(2,1)}, u32[]{:S(2)}, u32[]{:S(2)}) collective-permute-start(bf16[2,1024,128]{2,1,0:T(8,128)(2,1)} %copy-done.3), channel_id=1, source_target_pairs={{0,96},{8,104},{16,112},{24,120},{32,0},{40,8},{48,16},{56,24},{64... | collective-permute-start | bytes 1572872 | tf_op jit(solution)/shard_map/ppermute | solution.py:345
  31.4 13.6 %collective-permute-start.9 = (s32[2,32]{1,0:T(2,128)S(1)}, s32[2,32]{1,0:T(2,128)S(1)}, u32[]{:S(2)}, u32[]{:S(2)}) collective-permute-start(s32[2,32]{1,0:T(2,128)S(1)} %pad_add_fusion.mine), channel_id=1, source_target_pairs={{0,16},{8,24},{16,0},{24,8},{32,48},{40,56},{48,32},{56,40},{64,80... | collective-permute-start | bytes 776 | tf_op jit(solution)/shard_map/ppermute | solution.py:353
  47.5 17.8 %collective-permute-start.12 = (bf16[400,1024]{1,0:T(8,128)(2,1)}, bf16[400,1024]{1,0:T(8,128)(2,1)}, u32[]{:S(2)}, u32[]{:S(2)}) collective-permute-start(bf16[400,1024]{1,0:T(8,128)(2,1)} %collective-permute-done.refs_1_), channel_id=1, source_target_pairs={{0,2},{1,3},{2,4},{3,5},{4,6},{5,7},{6,0},{7,1},{8,10},{9,11},{10,... | collective-permute-start | bytes 2457608 | tf_op jit(solution)/shard_map/ppermute | solution.py:320
  48.1 14.3 %collective-permute-start.10 = (bf16[2,1024,128]{2,1,0:T(8,128)(2,1)}, bf16[2,1024,128]{2,1,0:T(8,128)(2,1)}, u32[]{:S(2)}, u32[]{:S(2)}) collective-permute-start(bf16[2,1024,128]{2,1,0:T(8,128)(2,1)} %collective-permute-done.7.refs_3_), channel_id=1, source_target_pairs={{0,32},{8,40},{16,48},{24,56},{32,64},{40,72},{48,80},{56,88},{64,... | collective-permute-start | bytes 1572872 | tf_op jit(solution)/shard_map/ppermute | solution.py:344
  49.1 13.3 %collective-permute-start.11 = (bf16[2,1024,128]{2,1,0:T(8,128)(2,1)}, bf16[2,1024,128]{2,1,0:T(8,128)(2,1)}, u32[]{:S(2)}, u32[]{:S(2)}) collective-permute-start(bf16[2,1024,128]{2,1,0:T(8,128)(2,1)} %collective-permute-done.8.refs_11_), channel_id=1, source_target_pairs={{0,96},{8,104},{16,112},{24,120},{32,0},{40,8},{48,16},{56,24},{64... | collective-permute-start | bytes 1572872 | tf_op jit(solution)/shard_map/ppermute | solution.py:345
  50.3 18.4 %collective-permute-start.13 = (bf16[400,1024]{1,0:T(8,128)(2,1)}, bf16[400,1024]{1,0:T(8,128)(2,1)}, u32[]{:S(2)}, u32[]{:S(2)}) collective-permute-start(bf16[400,1024]{1,0:T(8,128)(2,1)} %collective-permute-done.6.refs_1_), channel_id=1, source_target_pairs={{0,6},{1,7},{2,0},{3,1},{4,2},{5,3},{6,4},{7,5},{8,14},{9,15},{10,... | collective-permute-start | bytes 2457608 | tf_op jit(solution)/shard_map/ppermute | solution.py:323
  62.5 6.7 %collective-permute-start.15 = (bf16[2,1024,128]{2,1,0:T(8,128)(2,1)}, bf16[2,1024,128]{2,1,0:T(8,128)(2,1)}, u32[]{:S(2)}, u32[]{:S(2)}) collective-permute-start(bf16[2,1024,128]{2,1,0:T(8,128)(2,1)} %collective-permute-done.3.refs_2_), channel_id=1, source_target_pairs={{0,8},{8,0},{16,24},{24,16},{32,40},{40,32},{48,56},{56,48},{64,72... | collective-permute-start | bytes 1572872 | tf_op jit(solution)/shard_map/ppermute | solution.py:379
  63.0 6.3 %collective-permute-start.16 = (bf16[2,1024,128]{2,1,0:T(8,128)(2,1)}, bf16[2,1024,128]{2,1,0:T(8,128)(2,1)}, u32[]{:S(2)}, u32[]{:S(2)}) collective-permute-start(bf16[2,1024,128]{2,1,0:T(8,128)(2,1)} %collective-permute-done.7.refs_3_), channel_id=1, source_target_pairs={{0,8},{8,0},{16,24},{24,16},{32,40},{40,32},{48,56},{56,48},{64,72... | collective-permute-start | bytes 1572872 | tf_op jit(solution)/shard_map/ppermute | solution.py:379
  65.2 10.1 %collective-permute-start.17 = (bf16[2,1024,128]{2,1,0:T(8,128)(2,1)}, bf16[2,1024,128]{2,1,0:T(8,128)(2,1)S(1)}, u32[]{:S(2)}, u32[]{:S(2)}) collective-permute-start(bf16[2,1024,128]{2,1,0:T(8,128)(2,1)} %collective-permute-done.10.refs_4_), channel_id=1, source_target_pairs={{0,8},{8,0},{16,24},{24,16},{32,40},{40,32},{48,56},{56,48},{64,72... | collective-permute-start | bytes 1572872 | tf_op jit(solution)/shard_map/ppermute | solution.py:379
  68.7 10.2 %collective-permute-start.18 = (bf16[2,1024,128]{2,1,0:T(8,128)(2,1)S(1)}, bf16[2,1024,128]{2,1,0:T(8,128)(2,1)S(1)}, u32[]{:S(2)}, u32[]{:S(2)}) collective-permute-start(bf16[2,1024,128]{2,1,0:T(8,128)(2,1)S(1)} %copy-done.2), channel_id=1, source_target_pairs={{0,8},{8,0},{16,24},{24,16},{32,40},{40,32},{48,56},{56,48},{64,72... | collective-permute-start | bytes 1572872 | tf_op jit(solution)/shard_map/ppermute | solution.py:379
  68.7 10.2 %collective-permute-start.19 = (bf16[2,1024,128]{2,1,0:T(8,128)(2,1)S(1)}, bf16[2,1024,128]{2,1,0:T(8,128)(2,1)S(1)}, u32[]{:S(2)}, u32[]{:S(2)}) collective-permute-start(bf16[2,1024,128]{2,1,0:T(8,128)(2,1)S(1)} %copy-done.4), channel_id=1, source_target_pairs={{0,8},{8,0},{16,24},{24,16},{32,40},{40,32},{48,56},{56,48},{64,72... | collective-permute-start | bytes 1572872 | tf_op jit(solution)/shard_map/ppermute | solution.py:379
  69.3 9.7 %collective-permute-start.20 = (bf16[2,1024,128]{2,1,0:T(8,128)(2,1)}, bf16[2,1024,128]{2,1,0:T(8,128)(2,1)S(1)}, u32[]{:S(2)}, u32[]{:S(2)}) collective-permute-start(bf16[2,1024,128]{2,1,0:T(8,128)(2,1)} %collective-permute-done.8.refs_11_), channel_id=1, source_target_pairs={{0,8},{8,0},{16,24},{24,16},{32,40},{40,32},{48,56},{56,48},{64,72... | collective-permute-start | bytes 1572872 | tf_op jit(solution)/shard_map/ppermute | solution.py:379
  69.3 9.6 %collective-permute-start.21 = (bf16[2,1024,128]{2,1,0:T(8,128)(2,1)}, bf16[2,1024,128]{2,1,0:T(8,128)(2,1)S(1)}, u32[]{:S(2)}, u32[]{:S(2)}) collective-permute-start(bf16[2,1024,128]{2,1,0:T(8,128)(2,1)} %collective-permute-done.11.refs_12_), channel_id=1, source_target_pairs={{0,8},{8,0},{16,24},{24,16},{32,40},{40,32},{48,56},{56,48},{64,72... | collective-permute-start | bytes 1572872 | tf_op jit(solution)/shard_map/ppermute | solution.py:379
  75.4 17.7 %collective-permute-start.22 = (bf16[400,768]{1,0:T(8,128)(2,1)S(1)}, bf16[400,768]{1,0:T(8,128)(2,1)S(1)}, u32[]{:S(2)}, u32[]{:S(2)}) collective-permute-start(bf16[400,768]{1,0:T(8,128)(2,1)S(1)} %shard_map.139.refs_0_), channel_id=1, source_target_pairs={{0,16},{8,24},{16,0},{24,8},{32,48},{40,56},{48,32},{56,40},{64,80... | collective-permute-start | bytes 1843208 | tf_op jit(solution)/shard_map/ppermute | solution.py:407
  102.9 14.0 %collective-permute-start.23 = (bf16[400,512]{1,0:T(8,128)(2,1)S(1)}, bf16[400,512]{1,0:T(8,128)(2,1)S(1)}, u32[]{:S(2)}, u32[]{:S(2)}) collective-permute-start(bf16[400,512]{1,0:T(8,128)(2,1)S(1)} %shard_map.141), channel_id=1, source_target_pairs={{0,16},{8,24},{16,0},{24,8},{32,48},{40,56},{48,32},{56,40},{64,80... | collective-permute-start | bytes 1228808 | tf_op jit(solution)/shard_map/ppermute | solution.py:411
  118.4 15.2 %collective-permute-start.28 = (bf16[400,512]{1,0:T(8,128)(2,1)S(1)}, bf16[400,512]{1,0:T(8,128)(2,1)S(1)}, u32[]{:S(2)}, u32[]{:S(2)}) collective-permute-start(bf16[400,512]{1,0:T(8,128)(2,1)S(1)} %convolution_convert_fusion.4), channel_id=1, source_target_pairs={{0,2},{1,3},{2,4},{3,5},{4,6},{5,7},{6,0},{7,1},{8,10},{9,11},{10,... | collective-permute-start | bytes 1228808 | tf_op jit(solution)/shard_map/ppermute | solution.py:320
  119.9 13.7 %collective-permute-start.29 = (bf16[400,512]{1,0:T(8,128)(2,1)S(1)}, bf16[400,512]{1,0:T(8,128)(2,1)S(1)}, u32[]{:S(2)}, u32[]{:S(2)}) collective-permute-start(bf16[400,512]{1,0:T(8,128)(2,1)S(1)} %convolution_convert_fusion.3), channel_id=1, source_target_pairs={{0,6},{1,7},{2,0},{3,1},{4,2},{5,3},{6,4},{7,5},{8,14},{9,15},{10,... | collective-permute-start | bytes 1228808 | tf_op jit(solution)/shard_map/ppermute | solution.py:323
  123.4 18.9 %collective-permute-start.24 = (bf16[400,512]{1,0:T(8,128)(2,1)S(1)}, bf16[400,512]{1,0:T(8,128)(2,1)S(1)}, u32[]{:S(2)}, u32[]{:S(2)}) collective-permute-start(bf16[400,512]{1,0:T(8,128)(2,1)S(1)} %convolution_convert_fusion.2), channel_id=1, source_target_pairs={{0,2},{1,3},{2,4},{3,5},{4,6},{5,7},{6,0},{7,1},{8,10},{9,11},{10,... | collective-permute-start | bytes 1228808 | tf_op jit(solution)/shard_map/ppermute | solution.py:320
  126.1 16.2 %collective-permute-start.25 = (bf16[400,512]{1,0:T(8,128)(2,1)S(1)}, bf16[400,512]{1,0:T(8,128)(2,1)S(1)}, u32[]{:S(2)}, u32[]{:S(2)}) collective-permute-start(bf16[400,512]{1,0:T(8,128)(2,1)S(1)} %convolution_convert_fusion.1), channel_id=1, source_target_pairs={{0,6},{1,7},{2,0},{3,1},{4,2},{5,3},{6,4},{7,5},{8,14},{9,15},{10,... | collective-permute-start | bytes 1228808 | tf_op jit(solution)/shard_map/ppermute | solution.py:323
  137.6 21.5 %collective-permute-start.30 = (bf16[400,1024]{1,0:T(8,128)(2,1)S(1)}, bf16[400,1024]{1,0:T(8,128)(2,1)S(1)}, u32[]{:S(2)}, u32[]{:S(2)}) collective-permute-start(bf16[400,1024]{1,0:T(8,128)(2,1)S(1)} %pad_maximum_fusion.2), channel_id=1, source_target_pairs={{0,2},{1,3},{2,4},{3,5},{4,6},{5,7},{6,0},{7,1},{8,10},{9,11},{10,... | collective-permute-start | bytes 2457608 | tf_op jit(solution)/shard_map/ppermute | solution.py:320
  138.2 22.5 %collective-permute-start.31 = (bf16[400,1024]{1,0:T(8,128)(2,1)S(1)}, bf16[400,1024]{1,0:T(8,128)(2,1)S(1)}, u32[]{:S(2)}, u32[]{:S(2)}) collective-permute-start(bf16[400,1024]{1,0:T(8,128)(2,1)S(1)} %pad_maximum_fusion.3), channel_id=1, source_target_pairs={{0,6},{1,7},{2,0},{3,1},{4,2},{5,3},{6,4},{7,5},{8,14},{9,15},{10,... | collective-permute-start | bytes 2457608 | tf_op jit(solution)/shard_map/ppermute | solution.py:323
  147.3 28.9 %collective-permute-start.27 = (bf16[400,1024]{1,0:T(8,128)(2,1)}, bf16[400,1024]{1,0:T(8,128)(2,1)}, u32[]{:S(2)}, u32[]{:S(2)}) collective-permute-start(bf16[400,1024]{1,0:T(8,128)(2,1)} %pad_maximum_fusion.1), channel_id=1, source_target_pairs={{0,6},{1,7},{2,0},{3,1},{4,2},{5,3},{6,4},{7,5},{8,14},{9,15},{10,... | collective-permute-start | bytes 2457608 | tf_op jit(solution)/shard_map/ppermute | solution.py:323
  149.1 27.1 %collective-permute-start.26 = (bf16[400,1024]{1,0:T(8,128)(2,1)}, bf16[400,1024]{1,0:T(8,128)(2,1)}, u32[]{:S(2)}, u32[]{:S(2)}) collective-permute-start(bf16[400,1024]{1,0:T(8,128)(2,1)} %pad_maximum_fusion), channel_id=1, source_target_pairs={{0,2},{1,3},{2,4},{3,5},{4,6},{5,7},{6,0},{7,1},{8,10},{9,11},{10,... | collective-permute-start | bytes 2457608 | tf_op jit(solution)/shard_map/ppermute | solution.py:320
  163.4 16.4 %collective-permute-start.32 = (bf16[400,1024]{1,0:T(8,128)(2,1)}, bf16[400,1024]{1,0:T(8,128)(2,1)}, u32[]{:S(2)}, u32[]{:S(2)}) collective-permute-start(bf16[400,1024]{1,0:T(8,128)(2,1)} %add_convert_fusion), channel_id=1, source_target_pairs={{0,1},{1,0},{2,3},{3,2},{4,5},{5,4},{6,7},{7,6},{8,9},{9,8},{10,11... | collective-permute-start | bytes 2457608 | tf_op jit(solution)/shard_map/ppermute | solution.py:326
  (27 other events, 245.9 us)

commit v5 on v4

--- a/solution.py
+++ b/solution.py
@@ -430,7 +430,7 @@
         up = jnp.concatenate([up[:, :cut] + left.astype(f32), up[:, cut:]], 1).astype(bf16)
         down = jnp.concatenate([down[:, :cut], down[:, cut:] + right.astype(f32)], 1).astype(bf16)
         last = tie(attended, up, down)
-        near_sums.append((term(0, side, last), pass_up(up), pass_down(down)))
+        near_sums.append((tie(term(0, side, last), up), pass_up(up), pass_down(down)))
     (own, up, down), rest = near_sums[0], near_sums[1]
     crossed = pass_over((own + up.astype(f32) + down.astype(f32)).astype(bf16))
     return finish(spread, flat, *rest, crossed).reshape(tokens.shape)

time: 187 us -> 185 us (0.989)
  starting transfers between devices: 38.6 us -> 35 us
  Pallas kernels: 42.3 us -> 45 us
    ppermute x1, starting transfers between devices: 4.23 us -> 0.61 us  [on_device(): back = lax.ppermute(for_other, 'cand', ACROSS_Z_HI)]
    ppermute x1, waiting for transfers between devices: 9.76 us -> 12.8 us  [on_device(): back = lax.ppermute(for_other, 'cand', ACROSS_Z_HI)]
    pallas_call x2, Pallas kernels: 19.6 us -> 22.3 us  [attention(): pl.pallas_call(functools.partial(attention_kernel, which, bounds, len(row...]
  transfers between devices with their start and end apart: 33 -> 33, of which waited for: 16 -> 16; matrix products, arithmetic and copies ran while one was open for 12% -> 12% of each run, Pallas kernels for 15% -> 16%
where the time goes in v5:
time: 185 us; the launch traced here: 184 us
  waiting for transfers between devices  65 us (35%)
  Pallas kernels  45 us (24%)
  starting transfers between devices  35 us (19%)
  matrix products  19.3 us (10%)
  local copies, waits for them, and re-layouts  10.9 us (6%)
  other arithmetic  7.89 us (4%)
    ppermute x7, waiting for transfers between devices, pass_down(): return lax.ppermute(part, 'tp', along_x(-1))  27.1 us
    pallas_call x2, Pallas kernels, attention(): pl.pallas_call(functools.partial(attention_kernel, which, bounds, len(row...  22.3 us
    dot_general x12, matrix products, dot(): return jnp.dot(a, b, preferred_element_type=f32)  19.3 us
    pallas_call x3, Pallas kernels, project_parts(): pl.pallas_call(functools.partial(project_kernel, len(parts), plan, sums i...  14.8 us
    ppermute x1, waiting for transfers between devices, on_device(): back = lax.ppermute(for_other, 'cand', ACROSS_Z_HI)  12.8 us
    ppermute x3, waiting for transfers between devices, pass_prefixes(): key_parts.append(lax.ppermute(key_parts[-1], 'cand', along_y(1)))  10.9 us
    unnamed x52, local copies, waits for them, and re-layouts  10.3 us
    ppermute x7, starting transfers between devices, pass_down(): return lax.ppermute(part, 'tp', along_x(-1))  9.81 us
  transfers between devices with their start and end apart: 33, of which 16 were waited for; matrix products, arithmetic and copies ran while one was open for 12% of the time, Pallas kernels for 16%

profile of v5, /device:TPU:30, one launch (start us, length us, event | category | flops | bytes accessed | tf_op | source)
XLA Modules:
  0.0 183.9 jit_solution(13038823978742251382)
XLA Ops:
  1.7 2.4 %convolution_convert_fusion.refs_0_ = bf16[400,1024]{1,0:T(8,128)(2,1)S(1)} fusion(bf16[768,1024]{1,0:T(8,128)(2,1)} %bitcast.33, s32[768]{0:T(1024)S(1)} %select_n.162), kind=kOutput, calls=%fused_computation.3 | convolution fusion | flops 629862400 | bytes 2395136 | tf_op jit(solution)/shard_map/dot_general | solution.py:35
  6.1 1.9 %collective-permute-start.2 = (bf16[400,1024]{1,0:T(8,128)(2,1)S(1)}, bf16[400,1024]{1,0:T(8,128)(2,1)}, u32[]{:S(2)}, u32[]{:S(2)}) collective-permute-start(bf16[400,1024]{1,0:T(8,128)(2,1)S(1)} %convolution_convert_fusion.refs_0_), channel_id=1, source_target_pairs={{0,1},{1,0},{2,3},{3,2},{4,5},{5,4},{6,7},{7,6},{8,9},{9,8},{10,11... | collective-permute-start | bytes 2457608 | tf_op jit(solution)/shard_map/ppermute | solution.py:326
  11.0 10.9 %collective-permute-done.3.refs_2_ = bf16[2,1024,128]{2,1,0:T(8,128)(2,1)} collective-permute-done((bf16[2,1024,128]{2,1,0:T(8,128)(2,1)S(1)}, bf16[2,1024,128]{2,1,0:T(8,128)(2,1)}, u32[]{:S(2)}, u32[]{:S(2)}) %collective-permute-start.3) | collective-permute-done | bytes 524320 | tf_op jit(solution)/shard_map/ppermute | solution.py:344
  29.0 1.9 %collective-permute-start.8 = (bf16[2,1024,128]{2,1,0:T(8,128)(2,1)}, bf16[2,1024,128]{2,1,0:T(8,128)(2,1)}, u32[]{:S(2)}, u32[]{:S(2)}) collective-permute-start(bf16[2,1024,128]{2,1,0:T(8,128)(2,1)} %copy-done.3), channel_id=1, source_target_pairs={{0,96},{8,104},{16,112},{24,120},{32,0},{40,8},{48,16},{56,24},{64... | collective-permute-start | bytes 1572872 | tf_op jit(solution)/shard_map/ppermute | solution.py:345
  31.4 3.9 %collective-permute-start.9 = (s32[2,32]{1,0:T(2,128)S(1)}, s32[2,32]{1,0:T(2,128)S(1)}, u32[]{:S(2)}, u32[]{:S(2)}) collective-permute-start(s32[2,32]{1,0:T(2,128)S(1)} %pad_add_fusion.mine), channel_id=1, source_target_pairs={{0,16},{8,24},{16,0},{24,8},{32,48},{40,56},{48,32},{56,40},{64,80... | collective-permute-start | bytes 776 | tf_op jit(solution)/shard_map/ppermute | solution.py:353
  37.6 6.3 %shard_map.136 = (f32[400,768]{1,0:T(8,128)S(1)}, f32[400,128]{1,0:T(8,128)S(1)}) custom-call(s32[4]{0:T(128)S(1)} %pad_add_fusion.1.starts, bf16[400,1024]{1,0:T(8,128)(2,1)S(1)} %copy-done.11, bf16[400,1024]{1,0:T(8,128)(2,1)} %collective-permute-done.refs_1_, bf16[400,1024]{1,0:T(8,128)(2,1)S(1)} %copy-done.13, ...), custom_call_target="tpu_custom_call" | custom-call | flops 2516582400 | bytes 6291456 | tf_op jit(solution)/shard_map/pallas_call | solution.py:126
  45.5 1.9 %collective-permute-done.6.refs_1_ = bf16[400,1024]{1,0:T(8,128)(2,1)} collective-permute-done((bf16[400,1024]{1,0:T(8,128)(2,1)}, bf16[400,1024]{1,0:T(8,128)(2,1)}, u32[]{:S(2)}, u32[]{:S(2)}) %collective-permute-start.6) | collective-permute-done | bytes 819232 | tf_op jit(solution)/shard_map/ppermute | solution.py:323
  52.6 2.6 %shard_map.138.meta = s32[2,4,80]{2,1,0:T(4,128)} custom-call(s32[3]{0:T(128)} %pad_add_fusion.3.at, s32[2,32]{1,0:T(2,128)} %copy-done.18, s32[2,32]{1,0:T(2,128)} %copy-done.21, s32[32]{0:T(128)} %problem_slot.1), custom_call_target="tpu_custom_call" | custom-call | tf_op jit(solution)/shard_map/pallas_call | solution.py:195
  56.6 4.1 %shard_map.137 = (f32[400,768]{1,0:T(8,128)S(1)}, f32[400,128]{1,0:T(8,128)S(1)}) custom-call(s32[2]{0:T(128)S(1)} %pad_add_fusion.2.starts, bf16[400,1024]{1,0:T(8,128)(2,1)} %collective-permute-done.5.refs_0_, bf16[400,1024]{1,0:T(8,128)(2,1)} %collective-permute-done.6.refs_1_, bf16[1,8192]{1,0:T(2,128)(2,1)S(1)} %broadcast_in_dim.59.refs_4_.refs_2_, ...), custom_call_target="tpu_custom_call" | custom-call | flops 1258291200 | bytes 3145728 | tf_op jit(solution)/shard_map/pallas_call | solution.py:126
  63.1 2.1 %collective-permute-done.12.refs_0_ = bf16[400,1024]{1,0:T(8,128)(2,1)} collective-permute-done((bf16[400,1024]{1,0:T(8,128)(2,1)}, bf16[400,1024]{1,0:T(8,128)(2,1)}, u32[]{:S(2)}, u32[]{:S(2)}) %collective-permute-start.12) | collective-permute-done | bytes 819232 | tf_op jit(solution)/shard_map/ppermute | solution.py:320
  66.3 2.4 %collective-permute-done.13.refs_1_ = bf16[400,1024]{1,0:T(8,128)(2,1)} collective-permute-done((bf16[400,1024]{1,0:T(8,128)(2,1)}, bf16[400,1024]{1,0:T(8,128)(2,1)}, u32[]{:S(2)}, u32[]{:S(2)}) %collective-permute-start.13) | collective-permute-done | bytes 819232 | tf_op jit(solution)/shard_map/ppermute | solution.py:323
  71.1 4.3 %shard_map.139.refs_0_ = bf16[400,768]{1,0:T(8,128)(2,1)S(1)} custom-call(s32[2]{0:T(128)S(1)} %pad_add_fusion.4.starts, bf16[400,1024]{1,0:T(8,128)(2,1)} %collective-permute-done.12.refs_0_, bf16[400,1024]{1,0:T(8,128)(2,1)} %collective-permute-done.13.refs_1_, bf16[1,8192]{1,0:T(2,128)(2,1)S(1)} %broadcast_in_dim.59.refs_4_.refs_2_, ...), custom_call_target="tpu_custom_call" | custom-call | flops 1258291200 | bytes 3145728 | tf_op jit(solution)/shard_map/pallas_call | solution.py:126
  75.4 3.5 %collective-permute-start.22 = (bf16[400,768]{1,0:T(8,128)(2,1)S(1)}, bf16[400,768]{1,0:T(8,128)(2,1)S(1)}, u32[]{:S(2)}, u32[]{:S(2)}) collective-permute-start(bf16[400,768]{1,0:T(8,128)(2,1)S(1)} %shard_map.139.refs_0_), channel_id=1, source_target_pairs={{0,16},{8,24},{16,0},{24,8},{32,48},{40,56},{48,32},{56,40},{64,80... | collective-permute-start | bytes 1843208 | tf_op jit(solution)/shard_map/ppermute | solution.py:407
  79.0 11.6 %shard_map.140 = bf16[400,512]{1,0:T(8,128)(2,1)S(1)} custom-call(s32[2,4,80]{2,1,0:T(4,128)S(1)} %copy-done.16, bf16[400,768]{1,0:T(8,128)(2,1)S(1)} %shard_map.139.refs_0_, bf16[2,1024,128]{2,1,0:T(8,128)(2,1)S(1)} %copy-done.1, bf16[2,1024,128]{2,1,0:T(8,128)(2,1)} %collective-permute-done.3.refs_2_, ...), custom_call_target="tpu_custom_call" | custom-call | flops 1610612736 | bytes 8388608 | tf_op jit(solution)/shard_map/pallas_call | solution.py:270
  90.6 2.5 %collective-permute-done.22.refs_0_ = bf16[400,768]{1,0:T(8,128)(2,1)S(1)} collective-permute-done((bf16[400,768]{1,0:T(8,128)(2,1)S(1)}, bf16[400,768]{1,0:T(8,128)(2,1)S(1)}, u32[]{:S(2)}, u32[]{:S(2)}) %collective-permute-start.22) | collective-permute-done | bytes 614432 | tf_op jit(solution)/shard_map/ppermute | solution.py:407
  93.0 10.7 %shard_map.141 = bf16[400,512]{1,0:T(8,128)(2,1)S(1)} custom-call(s32[2,4,80]{2,1,0:T(4,128)S(1)} %copy-done.16, bf16[400,768]{1,0:T(8,128)(2,1)S(1)} %collective-permute-done.22.refs_0_, bf16[2,1024,128]{2,1,0:T(8,128)(2,1)S(1)} %copy-done.1, bf16[2,1024,128]{2,1,0:T(8,128)(2,1)} %collective-permute-done.3.refs_2_, ...), custom_call_target="tpu_custom_call" | custom-call | flops 1610612736 | bytes 8388608 | tf_op jit(solution)/shard_map/pallas_call | solution.py:270
  104.4 12.8 %collective-permute-done.23 = bf16[400,512]{1,0:T(8,128)(2,1)S(1)} collective-permute-done((bf16[400,512]{1,0:T(8,128)(2,1)S(1)}, bf16[400,512]{1,0:T(8,128)(2,1)S(1)}, u32[]{:S(2)}, u32[]{:S(2)}) %collective-permute-start.23) | collective-permute-done | bytes 409632 | tf_op jit(solution)/shard_map/ppermute | solution.py:411
  120.2 2.1 %collective-permute-start.29 = (bf16[400,512]{1,0:T(8,128)(2,1)S(1)}, bf16[400,512]{1,0:T(8,128)(2,1)S(1)}, u32[]{:S(2)}, u32[]{:S(2)}) collective-permute-start(bf16[400,512]{1,0:T(8,128)(2,1)S(1)} %convolution_convert_fusion.3), channel_id=1, source_target_pairs={{0,6},{1,7},{2,0},{3,1},{4,2},{5,3},{6,4},{7,5},{8,14},{9,15},{10,... | collective-permute-start | bytes 1228808 | tf_op jit(solution)/shard_map/ppermute | solution.py:323
  127.3 6.6 %collective-permute-done.29 = bf16[400,512]{1,0:T(8,128)(2,1)S(1)} collective-permute-done((bf16[400,512]{1,0:T(8,128)(2,1)S(1)}, bf16[400,512]{1,0:T(8,128)(2,1)S(1)}, u32[]{:S(2)}, u32[]{:S(2)}) %collective-permute-start.29) | collective-permute-done | bytes 409632 | tf_op jit(solution)/shard_map/ppermute | solution.py:323
  133.9 1.8 fusion.6
  135.8 1.8 fusion.4
  138.5 2.0 %collective-permute-start.31 = (bf16[400,1024]{1,0:T(8,128)(2,1)S(1)}, bf16[400,1024]{1,0:T(8,128)(2,1)S(1)}, u32[]{:S(2)}, u32[]{:S(2)}) collective-permute-start(bf16[400,1024]{1,0:T(8,128)(2,1)S(1)} %pad_maximum_fusion.3), channel_id=1, source_target_pairs={{0,6},{1,7},{2,0},{3,1},{4,2},{5,3},{6,4},{7,5},{8,14},{9,15},{10,... | collective-permute-start | bytes 2457608 | tf_op jit(solution)/shard_map/ppermute | solution.py:323
  140.5 2.1 %collective-permute-done.25 = bf16[400,512]{1,0:T(8,128)(2,1)S(1)} collective-permute-done((bf16[400,512]{1,0:T(8,128)(2,1)S(1)}, bf16[400,512]{1,0:T(8,128)(2,1)S(1)}, u32[]{:S(2)}, u32[]{:S(2)}) %collective-permute-start.25) | collective-permute-done | bytes 409632 | tf_op jit(solution)/shard_map/ppermute | solution.py:323
  142.7 1.8 fusion.10
  144.5 1.8 fusion.12
  146.3 1.8 fusion.2
  151.2 2.6 %collective-permute-start.26 = (bf16[400,1024]{1,0:T(8,128)(2,1)}, bf16[400,1024]{1,0:T(8,128)(2,1)}, u32[]{:S(2)}, u32[]{:S(2)}) collective-permute-start(bf16[400,1024]{1,0:T(8,128)(2,1)} %pad_maximum_fusion), channel_id=1, source_target_pairs={{0,2},{1,3},{2,4},{3,5},{4,6},{5,7},{6,0},{7,1},{8,10},{9,11},{10,... | collective-permute-start | bytes 2457608 | tf_op jit(solution)/shard_map/ppermute | solution.py:320
  153.8 5.6 %collective-permute-done.30 = bf16[400,1024]{1,0:T(8,128)(2,1)S(1)} collective-permute-done((bf16[400,1024]{1,0:T(8,128)(2,1)S(1)}, bf16[400,1024]{1,0:T(8,128)(2,1)S(1)}, u32[]{:S(2)}, u32[]{:S(2)}) %collective-permute-start.30) | collective-permute-done | bytes 819232 | tf_op jit(solution)/shard_map/ppermute | solution.py:320
  163.4 1.9 %fusion.8.term = f32[400,1024]{1,0:T(8,128)S(1)} fusion(bf16[400,512]{1,0:T(8,128)(2,1)S(1)} %broadcast_select_fusion, bf16[512,8192]{1,0:T(8,128)(2,1)} %param.22, s32[]{:T(128)S(6)} %select_n.191), kind=kOutput, calls=%fused_computation.16 | convolution fusion | flops 419430400 | bytes 3096580 | tf_op jit(solution)/shard_map/dot_general | solution.py:35
  165.4 11.1 %collective-permute-done.27.down = bf16[400,1024]{1,0:T(8,128)(2,1)} collective-permute-done((bf16[400,1024]{1,0:T(8,128)(2,1)}, bf16[400,1024]{1,0:T(8,128)(2,1)}, u32[]{:S(2)}, u32[]{:S(2)}) %collective-permute-start.27) | collective-permute-done | bytes 819232 | tf_op jit(solution)/shard_map/ppermute | solution.py:323
  176.5 2.1 %collective-permute-done.32.crossed = bf16[400,1024]{1,0:T(8,128)(2,1)} collective-permute-done((bf16[400,1024]{1,0:T(8,128)(2,1)}, bf16[400,1024]{1,0:T(8,128)(2,1)}, u32[]{:S(2)}, u32[]{:S(2)}) %collective-permute-start.32) | collective-permute-done | bytes 819232 | tf_op jit(solution)/shard_map/ppermute | solution.py:326
  178.6 5.3 %shard_map.142 = bf16[768,1024]{1,0:T(8,128)(2,1)} custom-call(bf16[768,400]{1,0:T(8,128)(2,1)S(1)} %fusion.spread, bf16[768,1024]{1,0:T(8,128)(2,1)S(1)} %bitcast.34, f32[400,1024]{1,0:T(8,128)S(1)} %fusion.8.term, bf16[400,1024]{1,0:T(8,128)(2,1)} %collective-permute-done.26.up, bf16[400,1024]{1,0:T(8,128)(2,1)} %collective-permute-done.27.down, ...), custom_call_target="tpu_custom_call" | custom-call | flops 1258291200 | bytes 6291456 | tf_op jit(solution)/shard_map/pallas_call | solution.py:156
  (144 shorter events, 46.7 us)
Async XLA Ops:
  4.0 20.2 %collective-permute-start = (bf16[400,1024]{1,0:T(8,128)(2,1)S(1)}, bf16[400,1024]{1,0:T(8,128)(2,1)}, u32[]{:S(2)}, u32[]{:S(2)}) collective-permute-start(bf16[400,1024]{1,0:T(8,128)(2,1)S(1)} %convolution_convert_fusion.refs_0_), channel_id=1, source_target_pairs={{0,2},{1,3},{2,4},{3,5},{4,6},{5,7},{6,0},{7,1},{8,10},{9,11},{10,... | collective-permute-start | bytes 2457608 | tf_op jit(solution)/shard_map/ppermute | solution.py:320
  4.6 20.9 %collective-permute-start.1 = (bf16[400,1024]{1,0:T(8,128)(2,1)S(1)}, bf16[400,1024]{1,0:T(8,128)(2,1)S(1)}, u32[]{:S(2)}, u32[]{:S(2)}) collective-permute-start(bf16[400,1024]{1,0:T(8,128)(2,1)S(1)} %convolution_convert_fusion.refs_0_), channel_id=1, source_target_pairs={{0,6},{1,7},{2,0},{3,1},{4,2},{5,3},{6,4},{7,5},{8,14},{9,15},{10,... | collective-permute-start | bytes 2457608 | tf_op jit(solution)/shard_map/ppermute | solution.py:323
  6.1 20.3 %collective-permute-start.2 = (bf16[400,1024]{1,0:T(8,128)(2,1)S(1)}, bf16[400,1024]{1,0:T(8,128)(2,1)}, u32[]{:S(2)}, u32[]{:S(2)}) collective-permute-start(bf16[400,1024]{1,0:T(8,128)(2,1)S(1)} %convolution_convert_fusion.refs_0_), channel_id=1, source_target_pairs={{0,1},{1,0},{2,3},{3,2},{4,5},{5,4},{6,7},{7,6},{8,9},{9,8},{10,11... | collective-permute-start | bytes 2457608 | tf_op jit(solution)/shard_map/ppermute | solution.py:326
  9.0 12.9 %collective-permute-start.3 = (bf16[2,1024,128]{2,1,0:T(8,128)(2,1)S(1)}, bf16[2,1024,128]{2,1,0:T(8,128)(2,1)}, u32[]{:S(2)}, u32[]{:S(2)}) collective-permute-start(bf16[2,1024,128]{2,1,0:T(8,128)(2,1)S(1)} %copy-done.1), channel_id=1, source_target_pairs={{0,32},{8,40},{16,48},{24,56},{32,64},{40,72},{48,80},{56,88},{64,... | collective-permute-start | bytes 1572872 | tf_op jit(solution)/shard_map/ppermute | solution.py:344
  9.2 13.9 %collective-permute-start.4 = (bf16[2,1024,128]{2,1,0:T(8,128)(2,1)S(1)}, bf16[2,1024,128]{2,1,0:T(8,128)(2,1)S(1)}, u32[]{:S(2)}, u32[]{:S(2)}) collective-permute-start(bf16[2,1024,128]{2,1,0:T(8,128)(2,1)S(1)} %copy-done.2), channel_id=1, source_target_pairs={{0,96},{8,104},{16,112},{24,120},{32,0},{40,8},{48,16},{56,24},{64... | collective-permute-start | bytes 1572872 | tf_op jit(solution)/shard_map/ppermute | solution.py:345
  26.4 19.1 %collective-permute-start.5 = (bf16[400,1024]{1,0:T(8,128)(2,1)}, bf16[400,1024]{1,0:T(8,128)(2,1)}, u32[]{:S(2)}, u32[]{:S(2)}) collective-permute-start(bf16[400,1024]{1,0:T(8,128)(2,1)} %collective-permute-done.2.refs_3_), channel_id=1, source_target_pairs={{0,2},{1,3},{2,4},{3,5},{4,6},{5,7},{6,0},{7,1},{8,10},{9,11},{10,... | collective-permute-start | bytes 2457608 | tf_op jit(solution)/shard_map/ppermute | solution.py:320
  27.5 19.9 %collective-permute-start.6 = (bf16[400,1024]{1,0:T(8,128)(2,1)}, bf16[400,1024]{1,0:T(8,128)(2,1)}, u32[]{:S(2)}, u32[]{:S(2)}) collective-permute-start(bf16[400,1024]{1,0:T(8,128)(2,1)} %collective-permute-done.2.refs_3_), channel_id=1, source_target_pairs={{0,6},{1,7},{2,0},{3,1},{4,2},{5,3},{6,4},{7,5},{8,14},{9,15},{10,... | collective-permute-start | bytes 2457608 | tf_op jit(solution)/shard_map/ppermute | solution.py:323
  28.9 16.1 %collective-permute-start.7 = (bf16[2,1024,128]{2,1,0:T(8,128)(2,1)}, bf16[2,1024,128]{2,1,0:T(8,128)(2,1)}, u32[]{:S(2)}, u32[]{:S(2)}) collective-permute-start(bf16[2,1024,128]{2,1,0:T(8,128)(2,1)} %collective-permute-done.3.refs_2_), channel_id=1, source_target_pairs={{0,32},{8,40},{16,48},{24,56},{32,64},{40,72},{48,80},{56,88},{64,... | collective-permute-start | bytes 1572872 | tf_op jit(solution)/shard_map/ppermute | solution.py:344
  29.0 15.9 %collective-permute-start.8 = (bf16[2,1024,128]{2,1,0:T(8,128)(2,1)}, bf16[2,1024,128]{2,1,0:T(8,128)(2,1)}, u32[]{:S(2)}, u32[]{:S(2)}) collective-permute-start(bf16[2,1024,128]{2,1,0:T(8,128)(2,1)} %copy-done.3), channel_id=1, source_target_pairs={{0,96},{8,104},{16,112},{24,120},{32,0},{40,8},{48,16},{56,24},{64... | collective-permute-start | bytes 1572872 | tf_op jit(solution)/shard_map/ppermute | solution.py:345
  31.4 13.6 %collective-permute-start.9 = (s32[2,32]{1,0:T(2,128)S(1)}, s32[2,32]{1,0:T(2,128)S(1)}, u32[]{:S(2)}, u32[]{:S(2)}) collective-permute-start(s32[2,32]{1,0:T(2,128)S(1)} %pad_add_fusion.mine), channel_id=1, source_target_pairs={{0,16},{8,24},{16,0},{24,8},{32,48},{40,56},{48,32},{56,40},{64,80... | collective-permute-start | bytes 776 | tf_op jit(solution)/shard_map/ppermute | solution.py:353
  47.5 17.8 %collective-permute-start.12 = (bf16[400,1024]{1,0:T(8,128)(2,1)}, bf16[400,1024]{1,0:T(8,128)(2,1)}, u32[]{:S(2)}, u32[]{:S(2)}) collective-permute-start(bf16[400,1024]{1,0:T(8,128)(2,1)} %collective-permute-done.refs_1_), channel_id=1, source_target_pairs={{0,2},{1,3},{2,4},{3,5},{4,6},{5,7},{6,0},{7,1},{8,10},{9,11},{10,... | collective-permute-start | bytes 2457608 | tf_op jit(solution)/shard_map/ppermute | solution.py:320
  48.1 14.3 %collective-permute-start.10 = (bf16[2,1024,128]{2,1,0:T(8,128)(2,1)}, bf16[2,1024,128]{2,1,0:T(8,128)(2,1)}, u32[]{:S(2)}, u32[]{:S(2)}) collective-permute-start(bf16[2,1024,128]{2,1,0:T(8,128)(2,1)} %collective-permute-done.7.refs_3_), channel_id=1, source_target_pairs={{0,32},{8,40},{16,48},{24,56},{32,64},{40,72},{48,80},{56,88},{64,... | collective-permute-start | bytes 1572872 | tf_op jit(solution)/shard_map/ppermute | solution.py:344
  49.1 13.3 %collective-permute-start.11 = (bf16[2,1024,128]{2,1,0:T(8,128)(2,1)}, bf16[2,1024,128]{2,1,0:T(8,128)(2,1)}, u32[]{:S(2)}, u32[]{:S(2)}) collective-permute-start(bf16[2,1024,128]{2,1,0:T(8,128)(2,1)} %collective-permute-done.8.refs_11_), channel_id=1, source_target_pairs={{0,96},{8,104},{16,112},{24,120},{32,0},{40,8},{48,16},{56,24},{64... | collective-permute-start | bytes 1572872 | tf_op jit(solution)/shard_map/ppermute | solution.py:345
  50.3 18.4 %collective-permute-start.13 = (bf16[400,1024]{1,0:T(8,128)(2,1)}, bf16[400,1024]{1,0:T(8,128)(2,1)}, u32[]{:S(2)}, u32[]{:S(2)}) collective-permute-start(bf16[400,1024]{1,0:T(8,128)(2,1)} %collective-permute-done.6.refs_1_), channel_id=1, source_target_pairs={{0,6},{1,7},{2,0},{3,1},{4,2},{5,3},{6,4},{7,5},{8,14},{9,15},{10,... | collective-permute-start | bytes 2457608 | tf_op jit(solution)/shard_map/ppermute | solution.py:323
  62.5 6.7 %collective-permute-start.15 = (bf16[2,1024,128]{2,1,0:T(8,128)(2,1)}, bf16[2,1024,128]{2,1,0:T(8,128)(2,1)}, u32[]{:S(2)}, u32[]{:S(2)}) collective-permute-start(bf16[2,1024,128]{2,1,0:T(8,128)(2,1)} %collective-permute-done.3.refs_2_), channel_id=1, source_target_pairs={{0,8},{8,0},{16,24},{24,16},{32,40},{40,32},{48,56},{56,48},{64,72... | collective-permute-start | bytes 1572872 | tf_op jit(solution)/shard_map/ppermute | solution.py:379
  63.0 6.3 %collective-permute-start.16 = (bf16[2,1024,128]{2,1,0:T(8,128)(2,1)}, bf16[2,1024,128]{2,1,0:T(8,128)(2,1)}, u32[]{:S(2)}, u32[]{:S(2)}) collective-permute-start(bf16[2,1024,128]{2,1,0:T(8,128)(2,1)} %collective-permute-done.7.refs_3_), channel_id=1, source_target_pairs={{0,8},{8,0},{16,24},{24,16},{32,40},{40,32},{48,56},{56,48},{64,72... | collective-permute-start | bytes 1572872 | tf_op jit(solution)/shard_map/ppermute | solution.py:379
  65.2 10.1 %collective-permute-start.17 = (bf16[2,1024,128]{2,1,0:T(8,128)(2,1)}, bf16[2,1024,128]{2,1,0:T(8,128)(2,1)S(1)}, u32[]{:S(2)}, u32[]{:S(2)}) collective-permute-start(bf16[2,1024,128]{2,1,0:T(8,128)(2,1)} %collective-permute-done.10.refs_4_), channel_id=1, source_target_pairs={{0,8},{8,0},{16,24},{24,16},{32,40},{40,32},{48,56},{56,48},{64,72... | collective-permute-start | bytes 1572872 | tf_op jit(solution)/shard_map/ppermute | solution.py:379
  68.7 10.2 %collective-permute-start.18 = (bf16[2,1024,128]{2,1,0:T(8,128)(2,1)S(1)}, bf16[2,1024,128]{2,1,0:T(8,128)(2,1)S(1)}, u32[]{:S(2)}, u32[]{:S(2)}) collective-permute-start(bf16[2,1024,128]{2,1,0:T(8,128)(2,1)S(1)} %copy-done.2), channel_id=1, source_target_pairs={{0,8},{8,0},{16,24},{24,16},{32,40},{40,32},{48,56},{56,48},{64,72... | collective-permute-start | bytes 1572872 | tf_op jit(solution)/shard_map/ppermute | solution.py:379
  68.7 10.2 %collective-permute-start.19 = (bf16[2,1024,128]{2,1,0:T(8,128)(2,1)S(1)}, bf16[2,1024,128]{2,1,0:T(8,128)(2,1)S(1)}, u32[]{:S(2)}, u32[]{:S(2)}) collective-permute-start(bf16[2,1024,128]{2,1,0:T(8,128)(2,1)S(1)} %copy-done.4), channel_id=1, source_target_pairs={{0,8},{8,0},{16,24},{24,16},{32,40},{40,32},{48,56},{56,48},{64,72... | collective-permute-start | bytes 1572872 | tf_op jit(solution)/shard_map/ppermute | solution.py:379
  69.3 9.7 %collective-permute-start.20 = (bf16[2,1024,128]{2,1,0:T(8,128)(2,1)}, bf16[2,1024,128]{2,1,0:T(8,128)(2,1)S(1)}, u32[]{:S(2)}, u32[]{:S(2)}) collective-permute-start(bf16[2,1024,128]{2,1,0:T(8,128)(2,1)} %collective-permute-done.8.refs_11_), channel_id=1, source_target_pairs={{0,8},{8,0},{16,24},{24,16},{32,40},{40,32},{48,56},{56,48},{64,72... | collective-permute-start | bytes 1572872 | tf_op jit(solution)/shard_map/ppermute | solution.py:379
  69.3 9.6 %collective-permute-start.21 = (bf16[2,1024,128]{2,1,0:T(8,128)(2,1)}, bf16[2,1024,128]{2,1,0:T(8,128)(2,1)S(1)}, u32[]{:S(2)}, u32[]{:S(2)}) collective-permute-start(bf16[2,1024,128]{2,1,0:T(8,128)(2,1)} %collective-permute-done.11.refs_12_), channel_id=1, source_target_pairs={{0,8},{8,0},{16,24},{24,16},{32,40},{40,32},{48,56},{56,48},{64,72... | collective-permute-start | bytes 1572872 | tf_op jit(solution)/shard_map/ppermute | solution.py:379
  75.4 17.7 %collective-permute-start.22 = (bf16[400,768]{1,0:T(8,128)(2,1)S(1)}, bf16[400,768]{1,0:T(8,128)(2,1)S(1)}, u32[]{:S(2)}, u32[]{:S(2)}) collective-permute-start(bf16[400,768]{1,0:T(8,128)(2,1)S(1)} %shard_map.139.refs_0_), channel_id=1, source_target_pairs={{0,16},{8,24},{16,0},{24,8},{32,48},{40,56},{48,32},{56,40},{64,80... | collective-permute-start | bytes 1843208 | tf_op jit(solution)/shard_map/ppermute | solution.py:407
  103.8 13.4 %collective-permute-start.23 = (bf16[400,512]{1,0:T(8,128)(2,1)S(1)}, bf16[400,512]{1,0:T(8,128)(2,1)S(1)}, u32[]{:S(2)}, u32[]{:S(2)}) collective-permute-start(bf16[400,512]{1,0:T(8,128)(2,1)S(1)} %shard_map.141), channel_id=1, source_target_pairs={{0,16},{8,24},{16,0},{24,8},{32,48},{40,56},{48,32},{56,40},{64,80... | collective-permute-start | bytes 1228808 | tf_op jit(solution)/shard_map/ppermute | solution.py:411
  118.7 15.2 %collective-permute-start.28 = (bf16[400,512]{1,0:T(8,128)(2,1)S(1)}, bf16[400,512]{1,0:T(8,128)(2,1)S(1)}, u32[]{:S(2)}, u32[]{:S(2)}) collective-permute-start(bf16[400,512]{1,0:T(8,128)(2,1)S(1)} %convolution_convert_fusion.4), channel_id=1, source_target_pairs={{0,2},{1,3},{2,4},{3,5},{4,6},{5,7},{6,0},{7,1},{8,10},{9,11},{10,... | collective-permute-start | bytes 1228808 | tf_op jit(solution)/shard_map/ppermute | solution.py:320
  120.2 13.7 %collective-permute-start.29 = (bf16[400,512]{1,0:T(8,128)(2,1)S(1)}, bf16[400,512]{1,0:T(8,128)(2,1)S(1)}, u32[]{:S(2)}, u32[]{:S(2)}) collective-permute-start(bf16[400,512]{1,0:T(8,128)(2,1)S(1)} %convolution_convert_fusion.3), channel_id=1, source_target_pairs={{0,6},{1,7},{2,0},{3,1},{4,2},{5,3},{6,4},{7,5},{8,14},{9,15},{10,... | collective-permute-start | bytes 1228808 | tf_op jit(solution)/shard_map/ppermute | solution.py:323
  123.7 19.0 %collective-permute-start.24 = (bf16[400,512]{1,0:T(8,128)(2,1)S(1)}, bf16[400,512]{1,0:T(8,128)(2,1)S(1)}, u32[]{:S(2)}, u32[]{:S(2)}) collective-permute-start(bf16[400,512]{1,0:T(8,128)(2,1)S(1)} %convolution_convert_fusion.2), channel_id=1, source_target_pairs={{0,2},{1,3},{2,4},{3,5},{4,6},{5,7},{6,0},{7,1},{8,10},{9,11},{10,... | collective-permute-start | bytes 1228808 | tf_op jit(solution)/shard_map/ppermute | solution.py:320
  126.4 16.2 %collective-permute-start.25 = (bf16[400,512]{1,0:T(8,128)(2,1)S(1)}, bf16[400,512]{1,0:T(8,128)(2,1)S(1)}, u32[]{:S(2)}, u32[]{:S(2)}) collective-permute-start(bf16[400,512]{1,0:T(8,128)(2,1)S(1)} %convolution_convert_fusion.1), channel_id=1, source_target_pairs={{0,6},{1,7},{2,0},{3,1},{4,2},{5,3},{6,4},{7,5},{8,14},{9,15},{10,... | collective-permute-start | bytes 1228808 | tf_op jit(solution)/shard_map/ppermute | solution.py:323
  137.9 21.5 %collective-permute-start.30 = (bf16[400,1024]{1,0:T(8,128)(2,1)S(1)}, bf16[400,1024]{1,0:T(8,128)(2,1)S(1)}, u32[]{:S(2)}, u32[]{:S(2)}) collective-permute-start(bf16[400,1024]{1,0:T(8,128)(2,1)S(1)} %pad_maximum_fusion.2), channel_id=1, source_target_pairs={{0,2},{1,3},{2,4},{3,5},{4,6},{5,7},{6,0},{7,1},{8,10},{9,11},{10,... | collective-permute-start | bytes 2457608 | tf_op jit(solution)/shard_map/ppermute | solution.py:320
  138.5 22.5 %collective-permute-start.31 = (bf16[400,1024]{1,0:T(8,128)(2,1)S(1)}, bf16[400,1024]{1,0:T(8,128)(2,1)S(1)}, u32[]{:S(2)}, u32[]{:S(2)}) collective-permute-start(bf16[400,1024]{1,0:T(8,128)(2,1)S(1)} %pad_maximum_fusion.3), channel_id=1, source_target_pairs={{0,6},{1,7},{2,0},{3,1},{4,2},{5,3},{6,4},{7,5},{8,14},{9,15},{10,... | collective-permute-start | bytes 2457608 | tf_op jit(solution)/shard_map/ppermute | solution.py:323
  149.4 27.1 %collective-permute-start.27 = (bf16[400,1024]{1,0:T(8,128)(2,1)}, bf16[400,1024]{1,0:T(8,128)(2,1)}, u32[]{:S(2)}, u32[]{:S(2)}) collective-permute-start(bf16[400,1024]{1,0:T(8,128)(2,1)} %pad_maximum_fusion.1), channel_id=1, source_target_pairs={{0,6},{1,7},{2,0},{3,1},{4,2},{5,3},{6,4},{7,5},{8,14},{9,15},{10,... | collective-permute-start | bytes 2457608 | tf_op jit(solution)/shard_map/ppermute | solution.py:323
  151.2 25.3 %collective-permute-start.26 = (bf16[400,1024]{1,0:T(8,128)(2,1)}, bf16[400,1024]{1,0:T(8,128)(2,1)}, u32[]{:S(2)}, u32[]{:S(2)}) collective-permute-start(bf16[400,1024]{1,0:T(8,128)(2,1)} %pad_maximum_fusion), channel_id=1, source_target_pairs={{0,2},{1,3},{2,4},{3,5},{4,6},{5,7},{6,0},{7,1},{8,10},{9,11},{10,... | collective-permute-start | bytes 2457608 | tf_op jit(solution)/shard_map/ppermute | solution.py:320
  162.2 16.3 %collective-permute-start.32 = (bf16[400,1024]{1,0:T(8,128)(2,1)}, bf16[400,1024]{1,0:T(8,128)(2,1)}, u32[]{:S(2)}, u32[]{:S(2)}) collective-permute-start(bf16[400,1024]{1,0:T(8,128)(2,1)} %add_convert_fusion), channel_id=1, source_target_pairs={{0,1},{1,0},{2,3},{3,2},{4,5},{5,4},{6,7},{7,6},{8,9},{9,8},{10,11... | collective-permute-start | bytes 2457608 | tf_op jit(solution)/shard_map/ppermute | solution.py:326
  (27 other events, 245.9 us)
